TPU v7x, 32 devices: a whole 2x2x4 slice. The times are simulated.
32 devices in a mesh: tok: 4 (over y, x), vocab: 8 (over z, core).
Axes of the slice: x: 2, y: 2, z: 4, core: 2. Of those that a mesh axis runs over, the one named last changes fastest.
Arguments:
- teacher_logits: bfloat16 [512, 32768], P('tok', 'vocab'), may hold values from -18 to 240
- hidden: bfloat16 [512, 4608], P('tok'), may hold values from -6 to 6
- new_head: bfloat16 [4608, 32768], P(None, ('tok', 'vocab')), may hold values from -0.26516504 to 0.26516504
- labels: int32 [512], replicated, may hold values from 0 to 32767
- map_target: int32 [256, 4], P('vocab'), may hold values from 0 to 255, as said below
- map_weight: bfloat16 [256, 4, 128, 128], P('vocab'), may hold values from 0 to 0.017578125, as said below
Outputs:
- loss: float32 [512], P('tok')
- head_grad: bfloat16 [4608, 32768], P(None, ('tok', 'vocab'))
Inputs may be any that keep to these rules, and one draw needn't show every extreme that they name: `map_target`: values are ids of new blocks; new block b belongs to the device at index b // 8 of tok and vocab together, tok first. Of the 128 entries of one vocab index, at most 8 belong to one device, and some device gets exactly 8. `map_weight`: entries are non-negative.
All inputs are finite; a program needn't handle non-finite values.
Results may differ from a plain program's by a relative error of at most 0.001.
The roundings to bfloat16 on the way count: a program that leaves them out, or rounds other values in their place, can miss the bound.
Values may be sent and summed in bfloat16 or wider, within the bound.
No kernel may reach another device: no remote copies, remote signals or barrier semaphores. Data moves between devices by JAX's collectives and lax.ppermute only.
A program may use at most 128 MiB of HBM per device.

v0:
```python
import functools

import jax
import jax.numpy as jnp
from jax import lax
from jax.experimental import pallas as pl
from jax.experimental.pallas import tpu as pltpu
from jax.sharding import PartitionSpec as P

F32 = jnp.float32
BF16 = jnp.bfloat16
LANES = 128
BATCH = 4
COST = pl.CostEstimate(flops=1024, bytes_accessed=1024, transcendentals=0)
SLOT_BASE = 1024
SMEM_SPEC = pl.BlockSpec(memory_space=pltpu.SMEM)
VMEM_SPEC = pl.BlockSpec(memory_space=pltpu.VMEM)


def params(mebibytes):
    return pltpu.CompilerParams(vmem_limit_bytes=mebibytes * 1024 * 1024)


def tree(op, items):
    while len(items) > 1:
        items = [op(items[i], items[i + 1]) if i + 1 < len(items) else items[i] for i in range(0, len(items), 2)]
    return items[0]


def total_at(rows_of, top_row, total_row):
    top = tree(jnp.maximum, [r[top_row] for r in rows_of])
    total = tree(jnp.add, [r[total_row] * jnp.exp(r[top_row] - top) for r in rows_of])
    return top, total


def split_rows(refs):
    return [[ref[k : k + 1, :] for k in range(8)] for ref in refs]


def rows_from_columns(columns):
    n = columns[0].shape[0]
    lane = lax.broadcasted_iota(jnp.int32, (n, LANES), 1)
    tile = jnp.zeros((n, LANES), F32)
    for place, column in enumerate(columns):
        tile = jnp.where(lane == place, column, tile)
    return tile.T[0:8, :]


def columns_from_rows(rows):
    n = rows[0].shape[1]
    return jnp.concatenate(rows + [jnp.zeros((LANES - len(rows), n), F32)], axis=0).T


def teacher_kernel(*refs):
    shards, stat_ref = refs[:-1], refs[-1]
    rows, cols = shards[0].shape
    places = [(ref, j) for ref in shards for j in range(0, cols, LANES)]
    read = lambda place: place[0][:, place[1] : place[1] + LANES].astype(F32)
    top = jnp.full((rows, LANES), -jnp.inf, F32)
    for place in places:
        top = jnp.maximum(top, read(place))
    top = jnp.max(top, axis=1, keepdims=True)
    total = jnp.zeros((rows, LANES), F32)
    for place in places:
        total = total + jnp.exp(read(place) - top)
    stat_ref[...] = rows_from_columns([top, jnp.sum(total, axis=1, keepdims=True)])


def teacher_stats(*shards):
    size = sum(x.size for x in shards)
    return pl.pallas_call(
        teacher_kernel,
        in_specs=[VMEM_SPEC] * len(shards),
        out_specs=VMEM_SPEC,
        out_shape=jax.ShapeDtypeStruct((8, shards[0].shape[0]), F32),
        compiler_params=params(40),
        cost_estimate=COST,
        name="teacher_stats",
    )(*shards)


def divide(x, n):
    return lax.shift_right_logical(x, n.bit_length() - 1) if n & (n - 1) == 0 else x // n


def plan_kernel(spot_ref, own_ref, peer_ref, list_ref, count_ref, *, per, n_vocab, in_line):
    core, z = spot_ref[0], spot_ref[1]
    pieces, room = list_ref.shape
    entries, fan = own_ref.shape
    for p in range(pieces):
        count_ref[p] = 0

    def visit(i, carry):
        for side, ref in enumerate((own_ref, peer_ref)):
            for f in range(fan):
                block = ref[i, f]
                owner = divide(block, per)
                owner_tok = divide(owner, n_vocab)
                owner_vocab = owner - owner_tok * n_vocab
                owner_z = divide(owner_vocab, 2)
                slot = owner_tok * per + block - owner * per
                if in_line:
                    outer = (owner_z == 0) | (owner_z == 3)
                    near = jnp.where(owner_z == z, 3, 2)
                    place = jnp.where(divide(owner_z, 2) == divide(z, 2), near, jnp.where(outer, 0, 1))
                else:
                    place = owner_z

                @pl.when(owner_vocab - owner_z * 2 == core)
                def _():
                    n = count_ref[place]
                    list_ref[place, n] = ((side * entries + i) * fan + f) * SLOT_BASE + slot
                    count_ref[place] = n + 1

        return carry

    lax.fori_loop(0, entries, visit, 0)
    for p in range(pieces):
        n = count_ref[p]
        for k in range(BATCH - 1):
            list_ref[p, n + k] = SLOT_BASE - 1


def plan(spot, own_target, peer_target, pieces, per, n_vocab, in_line):
    room = 2 * own_target.size + BATCH
    return pl.pallas_call(
        functools.partial(plan_kernel, per=per, n_vocab=n_vocab, in_line=in_line),
        in_specs=[SMEM_SPEC] * 3,
        out_specs=[SMEM_SPEC] * 2,
        out_shape=[jax.ShapeDtypeStruct((pieces, room), jnp.int32), jax.ShapeDtypeStruct((pieces,), jnp.int32)],
        cost_estimate=COST,
        name="entry_lists",
    )(spot, own_target, peer_target)


def probs_kernel(x_own, x_peer, *refs):
    stats, probs = refs[:-1], refs[-1]
    blocks = x_own.shape[1] // LANES
    top, total = total_at(split_rows(stats), 0, 1)
    columns = columns_from_rows([top, 1.0 / total])
    top, scale = columns[:, 0:1], columns[:, 1:2]
    for side, x in enumerate((x_own, x_peer)):
        for j in range(blocks):
            raised = jnp.exp(x[:, j * LANES : (j + 1) * LANES].astype(F32) - top)
            probs[side * blocks + j] = (raised * scale).astype(BF16)


def sums_kernel(list_ref, count_ref, probs, w_own, w_peer, *refs, first, fan):
    outs, mass_ref, acc = refs[:-2], refs[-2], refs[-1]
    step = pl.program_id(0)
    slots, rows, _ = outs[0].shape
    side = w_own.shape[0] * fan
    mass = jnp.zeros((rows, LANES), F32)
    for k, out in enumerate(outs):
        piece = first + k + step
        acc[...] = jnp.zeros_like(acc)

        def add(i, carry):
            parts = []
            for u in range(BATCH):
                item = list_ref[piece, i * BATCH + u]
                slot = item & (SLOT_BASE - 1)
                entry = lax.shift_right_logical(item, SLOT_BASE.bit_length() - 1)
                weight = jnp.where(entry < side, 0, 1)
                parts.append((entry, slot, weight))
            for entry, slot, peer in parts:
                j = divide(entry, fan)
                f = entry - j * fan
                local_j = j - peer * (side // fan)
                weight = jnp.where(peer == 1, w_peer[local_j, f], w_own[local_j, f])
                part = jnp.dot(probs[j], weight, preferred_element_type=F32)
                acc[jnp.minimum(slot, slots)] += part.astype(BF16).astype(F32)
            return carry

        lax.fori_loop(0, divide(count_ref[piece] + BATCH - 1, BATCH), add, 0)

        def drain(i, mass):
            block = acc[i]
            out[i] = block.astype(BF16)
            return mass + block

        mass = lax.fori_loop(0, slots, drain, mass, unroll=4)
    part = rows_from_columns([jnp.sum(mass, axis=1, keepdims=True)])

    @pl.when(step == 0)
    def _():
        mass_ref[...] = part

    @pl.when(step > 0)
    def _():
        mass_ref[...] += part


def teacher_probs(x_own, x_peer, stats):
    rows, cols = x_own.shape
    return pl.pallas_call(
        probs_kernel,
        in_specs=[VMEM_SPEC] * (2 + len(stats)),
        out_specs=VMEM_SPEC,
        out_shape=jax.ShapeDtypeStruct((2 * cols // LANES, rows, LANES), BF16),
        compiler_params=params(16),
        cost_estimate=COST,
        name="teacher_probs",
    )(x_own, x_peer, *stats)


def chip_sums(lists, counts, probs, w_own, w_peer, first, n_out, steps, slots):
    rows = probs.shape[1]
    fan = w_own.shape[1]
    whole = lambda shape: pl.BlockSpec(shape, lambda s: (0,) * len(shape))
    out = jax.ShapeDtypeStruct((steps * slots, rows, LANES), BF16)
    return pl.pallas_call(
        functools.partial(sums_kernel, first=first, fan=fan),
        grid=(steps,),
        in_specs=[SMEM_SPEC] * 2 + [VMEM_SPEC] * 3,
        out_specs=[pl.BlockSpec((slots, rows, LANES), lambda s: (s, 0, 0))] * n_out + [whole((8, rows))],
        out_shape=[out] * n_out + [jax.ShapeDtypeStruct((8, rows), F32)],
        scratch_shapes=[pltpu.VMEM((slots + 1, rows, LANES), F32)],
        compiler_params=params(32),
        cost_estimate=COST,
        name="chip_sums",
    )(lists, counts, probs, w_own, w_peer)


def logits_kernel(spot_ref, after_ref, near_ref, far_ref, head_ref, *refs):
    out_ref, turned_ref, everyone = refs
    n_tok = out_ref.shape[0]
    half = near_ref.shape[0] // n_tok
    del after_ref

    @pl.when(pl.program_id(0) == 0)
    def _():
        core = spot_ref[0]
        for r in range(n_tok):
            source = slice(r * half, (r + 1) * half)
            for side, ref in ((core, near_ref), (1 - core, far_ref)):
                start = pl.multiple_of((2 * r + side) * half, half)
                everyone[pl.ds(start, half), :] = ref[source, :]

    result = jnp.dot(everyone[...], head_ref[...], preferred_element_type=F32)
    for r in range(n_tok):
        out_ref[r] = result[2 * r * half : 2 * (r + 1) * half, :]
    part = turned_ref.shape[0]
    start = pl.multiple_of(pl.program_id(0) * part, part)
    turned_ref[...] = everyone[:, pl.ds(start, part)].T


def student_logits(spot, after, near, far, head, n_tok):
    every, depth = 2 * near.shape[0], near.shape[1]
    rows = every // n_tok
    cols = head.shape[1]
    tile = 256
    whole = lambda shape: pl.BlockSpec(shape, lambda i: (0, 0))
    return pl.pallas_call(
        logits_kernel,
        grid=(cols // tile,),
        in_specs=[SMEM_SPEC, pl.BlockSpec(memory_space=pl.ANY), whole(near.shape), whole(far.shape)]
        + [pl.BlockSpec((depth, tile), lambda i: (0, i))],
        out_specs=[pl.BlockSpec((n_tok, rows, tile), lambda i: (0, 0, i))]
        + [pl.BlockSpec((depth * tile // cols, every), lambda i: (i, 0))],
        out_shape=[jax.ShapeDtypeStruct((n_tok, rows, cols), F32), jax.ShapeDtypeStruct((depth, every), BF16)],
        scratch_shapes=[pltpu.VMEM((every, depth), BF16)],
        compiler_params=params(40),
        cost_estimate=COST,
        name="student_logits",
    )(spot, after, near, far, head)


def student_kernel(base_ref, labels_ref, mass_ref, logits_ref, stat_ref):
    n_tok, rows, cols = logits_ref.shape
    lane = lax.broadcasted_iota(jnp.int32, (rows, LANES), 1)
    label = labels_ref[...]
    top = jnp.full((rows, LANES), -jnp.inf, F32)
    hit = jnp.zeros((rows, LANES), F32)
    for t in range(n_tok):
        for b in range(0, cols, LANES):
            block = logits_ref[t, :, b : b + LANES]
            top = jnp.maximum(top, block)
            hit = hit + jnp.where(lane == label - (base_ref[t] + b), block, 0.0)
    top = jnp.max(top, axis=1, keepdims=True)
    total = jnp.zeros((rows, LANES), F32)
    for t in range(n_tok):
        for b in range(0, cols, LANES):
            total = total + jnp.exp(logits_ref[t, :, b : b + LANES] - top)
    total = jnp.sum(total, axis=1, keepdims=True)
    hit = jnp.sum(hit, axis=1, keepdims=True)
    stat_ref[...] = mass_ref[...] + rows_from_columns([jnp.zeros_like(hit), top, total, hit])


def student_stats(base, label_column, mass, logits):
    return pl.pallas_call(
        student_kernel,
        in_specs=[SMEM_SPEC] + [VMEM_SPEC] * 3,
        out_specs=VMEM_SPEC,
        out_shape=jax.ShapeDtypeStruct(mass.shape, F32),
        compiler_params=params(16),
        cost_estimate=COST,
        name="student_stats",
    )(base, label_column, mass, logits)


def grad_kernel(base_ref, labels_ref, *refs, n_stats, n_sums):
    stats, sums = refs[:n_stats], refs[n_stats : n_stats + n_sums]
    logits_ref, grad_ref, loss_ref, columns, inner = refs[n_stats + n_sums :]
    step = pl.program_id(0)
    _, rows, cols = logits_ref.shape

    @pl.when(step == 0)
    def _():
        parts = split_rows(stats)
        mass = tree(jnp.add, [r[0] for r in parts])
        top, total = total_at(parts, 1, 2)
        log_total = top + jnp.log(total)
        label_logit = tree(jnp.add, [r[3] for r in parts])
        columns[...] = columns_from_rows([mass + 1.0, log_total])
        inner[...] = jnp.zeros_like(inner)
        loss_ref[...] = jnp.zeros_like(loss_ref)
        loss_ref[0:1, :] = mass * log_total + log_total - label_logit

    lane = lax.broadcasted_iota(jnp.int32, (rows, LANES), 1)
    lift, log_total = columns[:, 0:1], columns[:, 1:2]
    label = labels_ref[...] - base_ref[step]
    running = inner[...]
    for b in range(cols // LANES):
        place = slice(b * LANES, (b + 1) * LANES)
        target = functools.reduce(jnp.add, [ref[z, b].astype(F32) for ref in sums for z in range(ref.shape[0])])
        score = logits_ref[0, :, place]
        running = running + target * score
        hit = jnp.where(lane == label - b * LANES, 1.0, 0.0)
        grad_ref[0, :, place] = (lift * jnp.exp(score - log_total) - target - hit).astype(BF16)
    inner[...] = running

    @pl.when(step == pl.num_programs(0) - 1)
    def _():
        loss_ref[1:2, :] = rows_from_columns([jnp.sum(inner[...], axis=1, keepdims=True)])[0:1, :]


def grad_logits(base, label_column, stats, sums, logits):
    n_tok, rows, cols = logits.shape
    per = cols // LANES
    whole = lambda shape: pl.BlockSpec(shape, lambda t: (0,) * len(shape))
    one = pl.BlockSpec((1, rows, cols), lambda t: (t, 0, 0))
    return pl.pallas_call(
        functools.partial(grad_kernel, n_stats=len(stats), n_sums=len(sums)),
        grid=(n_tok,),
        in_specs=[SMEM_SPEC, whole(label_column.shape)]
        + [whole(s.shape) for s in stats]
        + [pl.BlockSpec((s.shape[0], per, rows, LANES), lambda t: (0, t, 0, 0)) for s in sums]
        + [one],
        out_specs=[one, whole((8, rows))],
        out_shape=[jax.ShapeDtypeStruct((n_tok, rows, cols), BF16), jax.ShapeDtypeStruct((8, rows), F32)],
        scratch_shapes=[pltpu.VMEM((rows, LANES), F32), pltpu.VMEM((rows, LANES), F32)],
        compiler_params=params(24),
        cost_estimate=COST,
        name="grad_logits",
    )(base, label_column, *stats, *sums, logits)


def product_kernel(a_ref, b_ref, o_ref):
    o_ref[...] = jnp.dot(a_ref[...], b_ref[...], preferred_element_type=F32).astype(o_ref.dtype)


def head_product(a, b):
    m, k = a.shape
    n = b.shape[1]
    tile = m // 4
    return pl.pallas_call(
        product_kernel,
        grid=(m // tile,),
        in_specs=[pl.BlockSpec((tile, k), lambda i: (i, 0)), pl.BlockSpec((k, n), lambda i: (0, 0))],
        out_specs=pl.BlockSpec((tile, n), lambda i: (i, 0)),
        out_shape=jax.ShapeDtypeStruct((m, n), BF16),
        compiler_params=params(32),
        cost_estimate=COST,
        name="head_product",
    )(a, b)


def swap(x, axis, mask):
    return lax.ppermute(x, axis, [(i, i ^ mask) for i in range(lax.axis_size(axis))])


def gather_chips(x):
    n = lax.axis_size("vocab")
    if n > 8:
        lines = [[2 * z + c for z in range(n // 2)] for c in range(2)]
        everything = lax.all_gather(x, "vocab", axis=0, axis_index_groups=lines)
        return [everything[z] for z in range(n // 2)]
    return [x] + [swap(x, "vocab", r) for r in range(2, n, 2)]


def gather_cores(x):
    chips = gather_chips(x)
    return chips + [swap(chip, "vocab", 1) for chip in chips]


def exchange_tok(x):
    return lax.all_to_all(x, "tok", split_axis=0, concat_axis=0, tiled=True)


def plus(a, b):
    return (a.astype(F32) + b.astype(F32)).astype(BF16)


def send(x, hops):
    return lax.ppermute(x, "vocab", [(2 * a + c, 2 * b + c) for a, b in hops for c in range(2)])


def local(teacher_logits, hidden, new_head, labels, map_target, map_weight):
    rows = teacher_logits.shape[0]
    block = map_weight.shape[2]
    n_tok = lax.axis_size("tok")
    n_vocab = lax.axis_size("vocab")
    n_z = n_vocab // 2
    new_cols = new_head.shape[1]
    per = new_cols // block
    tok = lax.axis_index("tok")
    vocab = lax.axis_index("vocab")
    spot = jnp.stack([vocab % 2, vocab // 2]).astype(jnp.int32)
    slots = n_tok * per
    in_line = n_z == 4

    half = lax.dynamic_slice_in_dim(hidden, spot[0] * (rows // 2), rows // 2)
    near = exchange_tok(jnp.broadcast_to(half, (n_tok,) + half.shape)).reshape(n_tok * (rows // 2), -1)
    peer_logits = swap(teacher_logits, "vocab", 1)
    peer_target = swap(map_target, "vocab", 1)
    peer_weight = swap(map_weight, "vocab", 1)
    totals = gather_cores(teacher_stats(teacher_logits))
    lists, counts = plan(spot, map_target, peer_target, n_z, per, n_vocab, in_line)
    probs = teacher_probs(teacher_logits, peer_logits, totals)

    sums_args = (lists, counts, probs, map_weight, peer_weight)
    if in_line:
        inward, across, outward = [(0, 1), (3, 2)], [(1, 2), (2, 1)], [(1, 0), (2, 3)]
        far_outer, mass_a = chip_sums(*sums_args, 0, 1, 1, slots)
        first = send(far_outer, inward)
        probs, mass_a = lax.optimization_barrier((probs, mass_a))
        far_inner, beside, own, mass_b = chip_sums(lists, counts, probs, map_weight, peer_weight, 1, 3, 1, slots)
        mass = mass_a + mass_b
        second = send(far_inner, inward)
        third = send(beside, inward)
    else:
        sums, mass = chip_sums(*sums_args, 0, 1, n_z, slots)
        lines = [[2 * z + c for z in range(n_z)] for c in range(2)]
        sums = lax.all_to_all(
            sums.reshape(n_z, slots, rows, block),
            "vocab",
            split_axis=0,
            concat_axis=0,
            axis_index_groups=lines,
            tiled=True,
        )
        sums = [sums]

    near, mass = lax.optimization_barrier((near, mass))
    far = swap(near, "vocab", 1)
    scores, turned = student_logits(spot, mass, near, far, new_head, n_tok)
    scores = exchange_tok(scores)
    if in_line:
        first, turned = lax.optimization_barrier((first, turned))
        merged = plus(far_outer, first)
        crossed_outer = send(merged, across)
        second, merged = lax.optimization_barrier((second, merged))
        merged_inner = plus(far_inner, second)
        crossed_inner = send(merged_inner, across)
        merged_near = plus(beside, crossed_outer)
        arrived = send(merged_near, outward)
        scores, merged_inner, merged_near = lax.optimization_barrier((scores, merged_inner, merged_near))
        sums = [x[None] for x in (own, third, crossed_inner, arrived)]
    label_column = lax.dynamic_slice_in_dim(labels, tok * rows, rows).reshape(rows, 1)
    base = (jnp.arange(n_tok, dtype=jnp.int32) * n_vocab + vocab) * new_cols
    stats = gather_cores(student_stats(base, label_column, mass, scores))

    grads, loss_rows = grad_logits(base, label_column, stats, sums, scores)
    grads = exchange_tok(grads).reshape(n_tok * rows, new_cols)
    inner = tree(jnp.add, gather_cores(loss_rows[1]))
    loss = loss_rows[0] - inner
    return (loss, head_product(turned, grads))


def solution(mesh):
    return jax.shard_map(
        local,
        mesh=mesh,
        in_specs=(
            P("tok", "vocab"),
            P("tok", None),
            P(None, ("tok", "vocab")),
            P(),
            P("vocab", None),
            P("vocab", None, None, None),
        ),
        out_specs=(P("tok"), P(None, ("tok", "vocab"))),
        check_vma=False,
    )
```

profile of v0, /device:TPU:0, one launch (start us, length us, event | category | flops | bytes accessed | tf_op | source)
XLA Modules:
  0.0 168.7 jit_solution(10441544392405355503)
XLA Ops:
  1.9 1.6 broadcast_in_dim.15
  3.5 5.3 %all-to-all-start = ((bf16[4,64,4608]{2,1,0:T(8,128)(2,1)}), bf16[4,64,4608]{2,1,0:T(8,128)(2,1)S(1)}, u32[]{:S(2)}, u32[]{:S(2)}) async-start(bf16[4,64,4608]{2,1,0:T(8,128)(2,1)} %broadcast_in_dim.15), calls=%async_computation | async-start | bytes 4718592 | tf_op jit(solution)/shard_map/all_to_all | solution.py:398
  10.7 1.6 collective-permute-start.1
  13.2 2.6 %collective-permute-start.2 = (f32[8,128]{1,0:T(8,128)S(1)}, f32[8,128]{1,0:T(8,128)S(1)}, u32[]{:S(2)}, u32[]{:S(2)}) collective-permute-start(f32[8,128]{1,0:T(8,128)S(1)} %teacher_stats.1.refs_0_), channel_id=1, source_target_pairs={{0,4},{1,5},{2,6},{3,7},{4,0},{5,1},{6,2},{7,3},{8,12},{9,13},{10,... | collective-permute-start | bytes 12296 | tf_op jit(solution)/shard_map/ppermute | solution.py:380
  17.7 3.5 %collective-permute-done.3.refs_3_ = f32[8,128]{1,0:T(8,128)S(1)} collective-permute-done((f32[8,128]{1,0:T(8,128)S(1)}, f32[8,128]{1,0:T(8,128)S(1)}, u32[]{:S(2)}, u32[]{:S(2)}) %collective-permute-start.3) | collective-permute-done | bytes 4128 | tf_op jit(solution)/shard_map/ppermute | solution.py:380
  22.3 5.2 %entry_lists.1 = (s32[4,260]{1,0:T(4,128)}, s32[4]{0:T(128)}) custom-call(s32[2]{0:T(128)} %pad_add_fusion.spot_ref, s32[32,4]{1,0:T(8,128)} %copy.9.own_ref, s32[32,4]{1,0:T(8,128)} %copy-done.16), custom_call_target="tpu_custom_call" | custom-call | flops 1024 | bytes 1024 | tf_op jit(solution)/shard_map/entry_lists/pallas_call | solution.py:126
  29.0 2.3 %teacher_probs.1.probs = bf16[64,128,128]{2,1,0:T(8,128)(2,1)S(1)} custom-call(bf16[128,4096]{1,0:T(8,128)(2,1)S(1)} %copy-done.5, bf16[128,4096]{1,0:T(8,128)(2,1)} %collective-permute-done.x_peer, f32[8,128]{1,0:T(8,128)S(1)} %teacher_stats.1.refs_0_, f32[8,128]{1,0:T(8,128)S(1)} %collective-permute-done.1.refs_1_, ...), custom_call_target="tpu_custom_call" | custom-call | flops 1024 | bytes 1024 | tf_op jit(solution)/shard_map/teacher_probs/pallas_call | solution.py:196
  31.4 3.6 %chip_sums.2 = (bf16[32,128,128]{2,1,0:T(8,128)(2,1)S(1)}, f32[8,128]{1,0:T(8,128)S(1)}) custom-call(s32[4,260]{1,0:T(4,128)S(1)} %copy-done.13, s32[4]{0:T(128)S(1)} %copy-done.15, bf16[64,128,128]{2,1,0:T(8,128)(2,1)S(1)} %teacher_probs.1.probs, bf16[32,4,128,128]{3,2,1,0:T(8,128)(2,1)S(1)} %copy-done.1, ...), custom_call_target="tpu_custom_call" | custom-call | flops 1024 | bytes 1024 | tf_op jit(solution)/shard_map/chip_sums/pallas_call | solution.py:212
  36.0 9.1 %chip_sums.3 = (bf16[32,128,128]{2,1,0:T(8,128)(2,1)S(1)}, bf16[32,128,128]{2,1,0:T(8,128)(2,1)}, bf16[32,128,128]{2,1,0:T(8,128)(2,1)S(1)}, f32[8,128]{1,0:T(8,128)S(1)}) custom-call(s32[4,260]{1,0:T(4,128)S(1)} %copy-done.13, s32[4]{0:T(128)S(1)} %copy-done.15, bf16[64,128,128]{2,1,0:T(8,128)(2,1)S(1)} %teacher_probs.1.probs, ...), custom_call_target="tpu_custom_call" | custom-call | flops 1024 | bytes 1024 | tf_op jit(solution)/shard_map/chip_sums/pallas_call | solution.py:212
  49.8 2.5 %collective-permute-start.11 = (bf16[32,128,128]{2,1,0:T(8,128)(2,1)}, bf16[32,128,128]{2,1,0:T(8,128)(2,1)}, u32[]{:S(2)}, u32[]{:S(2)}) collective-permute-start(bf16[32,128,128]{2,1,0:T(8,128)(2,1)} %copy-done.9), channel_id=1, source_target_pairs={{0,2},{1,3},{6,4},{7,5},{8,10},{9,11},{14,12},{15,13},{16,18},{17,... | collective-permute-start | bytes 3145736 | tf_op jit(solution)/shard_map/ppermute | solution.py:406
  52.6 8.0 %student_logits.1 = (f32[4,128,1024]{2,1,0:T(8,128)S(1)}, bf16[4608,512]{1,0:T(8,128)(2,1)S(1)}) custom-call(s32[2]{0:T(128)S(1)} %copy-done.14, f32[8,128]{1,0:T(8,128)S(1)} %add.55.after_ref.mass_ref, bf16[256,4608]{1,0:T(8,128)(2,1)S(1)} %bitcast.17, bf16[256,4608]{1,0:T(8,128)(2,1)S(1)} %collective-permute-done.10.far_ref, bf16[4608,1024]{1,0:T(8,128)(2,1)} %head_ref.1), custom_call_target="tpu_custom_call" | custom-call | flops 1024 | bytes 1024 | tf_op jit(solution)/shard_map/student_logits/pallas_call | solution.py:254
  60.7 2.2 %copy-done.2 = bf16[4608,512]{1,0:T(8,128)(2,1)} copy-done((bf16[4608,512]{1,0:T(8,128)(2,1)}, bf16[4608,512]{1,0:T(8,128)(2,1)S(1)}, u32[]{:S(2)}) %copy-start.2) | copy-done | bytes 4718616
  62.8 10.7 %collective-permute-done.12 = bf16[32,128,128]{2,1,0:T(8,128)(2,1)S(1)} collective-permute-done((bf16[32,128,128]{2,1,0:T(8,128)(2,1)}, bf16[32,128,128]{2,1,0:T(8,128)(2,1)S(1)}, u32[]{:S(2)}, u32[]{:S(2)}) %collective-permute-start.12) | collective-permute-done | bytes 1048608 | tf_op jit(solution)/shard_map/ppermute | solution.py:406
  74.9 1.6 collective-permute-start.13
  76.5 5.8 %collective-permute-start.21 = (bf16[32,128,128]{2,1,0:T(8,128)(2,1)}, bf16[32,128,128]{2,1,0:T(8,128)(2,1)}, u32[]{:S(2)}, u32[]{:S(2)}) collective-permute-start(bf16[32,128,128]{2,1,0:T(8,128)(2,1)} %get-tuple-element.36), channel_id=1, source_target_pairs={{0,2},{1,3},{6,4},{7,5},{8,10},{9,11},{14,12},{15,13},{16,18},{17,... | collective-permute-start | bytes 3145736 | tf_op jit(solution)/shard_map/ppermute | solution.py:406
  82.3 13.7 %collective-permute-done.11 = bf16[32,128,128]{2,1,0:T(8,128)(2,1)} collective-permute-done((bf16[32,128,128]{2,1,0:T(8,128)(2,1)}, bf16[32,128,128]{2,1,0:T(8,128)(2,1)}, u32[]{:S(2)}, u32[]{:S(2)}) %collective-permute-start.11) | collective-permute-done | bytes 1048608 | tf_op jit(solution)/shard_map/ppermute | solution.py:406
  96.0 4.2 %all-to-all-start.1 = ((f32[4,128,1024]{2,1,0:T(8,128)}), f32[4,128,1024]{2,1,0:T(8,128)S(1)}, u32[]{:S(2)}, u32[]{:S(2)}) async-start(f32[4,128,1024]{2,1,0:T(8,128)} %copy-done.6), calls=%async_computation.1 | async-start | bytes 4194304 | tf_op jit(solution)/shard_map/all_to_all | solution.py:398
  100.2 3.0 %add_convert_fusion.1 = bf16[32,128,128]{2,1,0:T(8,128)(2,1)} fusion(bf16[32,128,128]{2,1,0:T(8,128)(2,1)} %collective-permute-done.11, bf16[32,128,128]{2,1,0:T(8,128)(2,1)} %copy-done.9), kind=kLoop, calls=%fused_computation.1 | loop fusion | flops 2097152 | bytes 3145728 | tf_op jit(solution)/shard_map/convert_element_type | solution.py:402
  103.2 1.6 collective-permute-start.22
  104.8 3.0 %add_convert_fusion = bf16[32,128,128]{2,1,0:T(8,128)(2,1)} fusion(bf16[32,128,128]{2,1,0:T(8,128)(2,1)} %collective-permute-done.13, bf16[32,128,128]{2,1,0:T(8,128)(2,1)} %get-tuple-element.36), kind=kLoop, calls=%fused_computation | loop fusion | flops 2097152 | bytes 3145728 | tf_op jit(solution)/shard_map/convert_element_type | solution.py:402
  110.0 14.1 %all-to-all-done.1.logits_ref.refs_12_ = f32[4,128,1024]{2,1,0:T(8,128)S(1)} async-done(((f32[4,128,1024]{2,1,0:T(8,128)}), f32[4,128,1024]{2,1,0:T(8,128)S(1)}, u32[]{:S(2)}, u32[]{:S(2)}) %all-to-all-start.1) | async-done | bytes 2097184 | tf_op jit(solution)/shard_map/all_to_all | solution.py:398
  125.5 2.5 %collective-permute-start.14 = (f32[8,128]{1,0:T(8,128)S(1)}, f32[8,128]{1,0:T(8,128)S(1)}, u32[]{:S(2)}, u32[]{:S(2)}) collective-permute-start(f32[8,128]{1,0:T(8,128)S(1)} %student_stats.1.refs_0_), channel_id=1, source_target_pairs={{0,2},{1,3},{2,0},{3,1},{4,6},{5,7},{6,4},{7,5},{8,10},{9,11},{10,... | collective-permute-start | bytes 12296 | tf_op jit(solution)/shard_map/ppermute | solution.py:380
  128.6 1.9 %collective-permute-start.16 = (f32[8,128]{1,0:T(8,128)S(1)}, f32[8,128]{1,0:T(8,128)S(1)}, u32[]{:S(2)}, u32[]{:S(2)}) collective-permute-start(f32[8,128]{1,0:T(8,128)S(1)} %student_stats.1.refs_0_), channel_id=1, source_target_pairs={{0,6},{1,7},{2,4},{3,5},{4,2},{5,3},{6,0},{7,1},{8,14},{9,15},{10,... | collective-permute-start | bytes 12296 | tf_op jit(solution)/shard_map/ppermute | solution.py:380
  130.5 4.6 %collective-permute-done.14.refs_1_ = f32[8,128]{1,0:T(8,128)S(1)} collective-permute-done((f32[8,128]{1,0:T(8,128)S(1)}, f32[8,128]{1,0:T(8,128)S(1)}, u32[]{:S(2)}, u32[]{:S(2)}) %collective-permute-start.14) | collective-permute-done | bytes 4128 | tf_op jit(solution)/shard_map/ppermute | solution.py:380
  136.7 3.7 %grad_logits.1 = (bf16[4,128,1024]{2,1,0:T(8,128)(2,1)S(1)}, f32[8,128]{1,0:T(8,128)S(1)}) custom-call(s32[4]{0:T(128)S(1)} %add_multiply_fusion.base_ref, s32[128,1]{1,0:T(8,128)S(1)} %copy.11.labels_ref, f32[8,128]{1,0:T(8,128)S(1)} %student_stats.1.refs_0_, f32[8,128]{1,0:T(8,128)S(1)} %collective-permute-done.14.refs_1_, ...), custom_call_target="tpu_custom_call" | custom-call | flops 1024 | bytes 1024 | tf_op jit(solution)/shard_map/grad_logits/pallas_call | solution.py:343
  141.5 3.9 %all-to-all-start.2 = ((bf16[4,128,1024]{2,1,0:T(8,128)(2,1)}), bf16[4,128,1024]{2,1,0:T(8,128)(2,1)S(1)}, u32[]{:S(2)}, u32[]{:S(2)}) async-start(bf16[4,128,1024]{2,1,0:T(8,128)(2,1)} %copy-done.12), calls=%async_computation.2 | async-start | bytes 2097152 | tf_op jit(solution)/shard_map/all_to_all | solution.py:398
  145.4 2.4 %collective-permute-start.25 = (f32[128]{0:T(128)S(1)}, f32[128]{0:T(128)S(1)}, u32[]{:S(2)}, u32[]{:S(2)}) collective-permute-start(f32[128]{0:T(128)S(1)} %slice_bitcast_fusion), channel_id=1, source_target_pairs={{0,4},{1,5},{2,6},{3,7},{4,0},{5,1},{6,2},{7,3},{8,12},{9,13},{10,... | collective-permute-start | bytes 1544 | tf_op jit(solution)/shard_map/ppermute | solution.py:380
  147.8 2.0 %collective-permute-start.26 = (f32[128]{0:T(128)S(1)}, f32[128]{0:T(128)S(1)}, u32[]{:S(2)}, u32[]{:S(2)}) collective-permute-start(f32[128]{0:T(128)S(1)} %slice_bitcast_fusion), channel_id=1, source_target_pairs={{0,6},{1,7},{2,4},{3,5},{4,2},{5,3},{6,0},{7,1},{8,14},{9,15},{10,... | collective-permute-start | bytes 1544 | tf_op jit(solution)/shard_map/ppermute | solution.py:380
  150.4 2.8 %collective-permute-done.26 = f32[128]{0:T(128)S(1)} collective-permute-done((f32[128]{0:T(128)S(1)}, f32[128]{0:T(128)S(1)}, u32[]{:S(2)}, u32[]{:S(2)}) %collective-permute-start.26) | collective-permute-done | bytes 544 | tf_op jit(solution)/shard_map/ppermute | solution.py:380
  154.8 4.6 %all-to-all-done.2 = bf16[4,128,1024]{2,1,0:T(8,128)(2,1)S(1)} async-done(((bf16[4,128,1024]{2,1,0:T(8,128)(2,1)}), bf16[4,128,1024]{2,1,0:T(8,128)(2,1)S(1)}, u32[]{:S(2)}, u32[]{:S(2)}) %all-to-all-start.2) | async-done | bytes 1048608 | tf_op jit(solution)/shard_map/all_to_all | solution.py:398
  159.4 2.3 %copy-done.3 = bf16[4608,512]{1,0:T(8,128)(2,1)S(1)} copy-done((bf16[4608,512]{1,0:T(8,128)(2,1)S(1)}, bf16[4608,512]{1,0:T(8,128)(2,1)}, u32[]{:S(2)}) %copy-start.3) | copy-done | bytes 4718616
  161.7 7.0 %head_product.1 = bf16[4608,1024]{1,0:T(8,128)(2,1)} custom-call(bf16[4608,512]{1,0:T(8,128)(2,1)S(1)} %copy-done.3, bf16[512,1024]{1,0:T(8,128)(2,1)S(1)} %bitcast.18), custom_call_target="tpu_custom_call" | custom-call | flops 1024 | bytes 1024 | tf_op jit(solution)/shard_map/head_product/pallas_call | solution.py:367
  (94 shorter events, 24.9 us)
Async XLA Ops:
  0.6 30.7 %collective-permute-start.9 = (bf16[32,4,128,128]{3,2,1,0:T(8,128)(2,1)}, bf16[32,4,128,128]{3,2,1,0:T(8,128)(2,1)}, u32[]{:S(2)}, u32[]{:S(2)}) collective-permute-start(bf16[32,4,128,128]{3,2,1,0:T(8,128)(2,1)} %w_own.3), channel_id=1, source_target_pairs={{0,1},{1,0},{2,3},{3,2},{4,5},{5,4},{6,7},{7,6},{8,9},{9,8},{10,11... | collective-permute-start | bytes 12582920 | tf_op jit(solution)/shard_map/ppermute | solution.py:380
  3.5 43.5 %all-to-all-start = ((bf16[4,64,4608]{2,1,0:T(8,128)(2,1)}), bf16[4,64,4608]{2,1,0:T(8,128)(2,1)S(1)}, u32[]{:S(2)}, u32[]{:S(2)}) async-start(bf16[4,64,4608]{2,1,0:T(8,128)(2,1)} %broadcast_in_dim.15), calls=%async_computation | async-start | bytes 4718592 | tf_op jit(solution)/shard_map/all_to_all | solution.py:398
  8.8 18.8 %collective-permute-start = (bf16[128,4096]{1,0:T(8,128)(2,1)}, bf16[128,4096]{1,0:T(8,128)(2,1)}, u32[]{:S(2)}, u32[]{:S(2)}) collective-permute-start(bf16[128,4096]{1,0:T(8,128)(2,1)} %x_own.1), channel_id=1, source_target_pairs={{0,1},{1,0},{2,3},{3,2},{4,5},{5,4},{6,7},{7,6},{8,9},{9,8},{10,11... | collective-permute-start | bytes 3145736 | tf_op jit(solution)/shard_map/ppermute | solution.py:380
  10.7 6.2 %collective-permute-start.1 = (f32[8,128]{1,0:T(8,128)S(1)}, f32[8,128]{1,0:T(8,128)S(1)}, u32[]{:S(2)}, u32[]{:S(2)}) collective-permute-start(f32[8,128]{1,0:T(8,128)S(1)} %teacher_stats.1.refs_0_), channel_id=1, source_target_pairs={{0,2},{1,3},{2,0},{3,1},{4,6},{5,7},{6,4},{7,5},{8,10},{9,11},{10,... | collective-permute-start | bytes 12296 | tf_op jit(solution)/shard_map/ppermute | solution.py:380
  13.0 2.8 %collective-permute-start.8 = (s32[32,4]{1,0:T(8,128)}, s32[32,4]{1,0:T(8,128)S(1)}, u32[]{:S(2)}, u32[]{:S(2)}) collective-permute-start(s32[32,4]{1,0:T(8,128)} %copy.9.own_ref), channel_id=1, source_target_pairs={{0,1},{1,0},{2,3},{3,2},{4,5},{5,4},{6,7},{7,6},{8,9},{9,8},{10,11... | collective-permute-start | bytes 1544 | tf_op jit(solution)/shard_map/ppermute | solution.py:380
  13.2 4.5 %collective-permute-start.2 = (f32[8,128]{1,0:T(8,128)S(1)}, f32[8,128]{1,0:T(8,128)S(1)}, u32[]{:S(2)}, u32[]{:S(2)}) collective-permute-start(f32[8,128]{1,0:T(8,128)S(1)} %teacher_stats.1.refs_0_), channel_id=1, source_target_pairs={{0,4},{1,5},{2,6},{3,7},{4,0},{5,1},{6,2},{7,3},{8,12},{9,13},{10,... | collective-permute-start | bytes 12296 | tf_op jit(solution)/shard_map/ppermute | solution.py:380
  15.8 5.4 %collective-permute-start.3 = (f32[8,128]{1,0:T(8,128)S(1)}, f32[8,128]{1,0:T(8,128)S(1)}, u32[]{:S(2)}, u32[]{:S(2)}) collective-permute-start(f32[8,128]{1,0:T(8,128)S(1)} %teacher_stats.1.refs_0_), channel_id=1, source_target_pairs={{0,6},{1,7},{2,4},{3,5},{4,2},{5,3},{6,0},{7,1},{8,14},{9,15},{10,... | collective-permute-start | bytes 12296 | tf_op jit(solution)/shard_map/ppermute | solution.py:380
  16.8 4.4 %collective-permute-start.4 = (f32[8,128]{1,0:T(8,128)S(1)}, f32[8,128]{1,0:T(8,128)}, u32[]{:S(2)}, u32[]{:S(2)}) collective-permute-start(f32[8,128]{1,0:T(8,128)S(1)} %teacher_stats.1.refs_0_), channel_id=1, source_target_pairs={{0,1},{1,0},{2,3},{3,2},{4,5},{5,4},{6,7},{7,6},{8,9},{9,8},{10,11... | collective-permute-start | bytes 12296 | tf_op jit(solution)/shard_map/ppermute | solution.py:380
  17.7 9.9 %collective-permute-start.5 = (f32[8,128]{1,0:T(8,128)S(1)}, f32[8,128]{1,0:T(8,128)}, u32[]{:S(2)}, u32[]{:S(2)}) collective-permute-start(f32[8,128]{1,0:T(8,128)S(1)} %collective-permute-done.1.refs_1_), channel_id=1, source_target_pairs={{0,1},{1,0},{2,3},{3,2},{4,5},{5,4},{6,7},{7,6},{8,9},{9,8},{10,11... | collective-permute-start | bytes 12296 | tf_op jit(solution)/shard_map/ppermute | solution.py:380
  21.2 6.4 %collective-permute-start.6 = (f32[8,128]{1,0:T(8,128)S(1)}, f32[8,128]{1,0:T(8,128)}, u32[]{:S(2)}, u32[]{:S(2)}) collective-permute-start(f32[8,128]{1,0:T(8,128)S(1)} %collective-permute-done.2.refs_2_), channel_id=1, source_target_pairs={{0,1},{1,0},{2,3},{3,2},{4,5},{5,4},{6,7},{7,6},{8,9},{9,8},{10,11... | collective-permute-start | bytes 12296 | tf_op jit(solution)/shard_map/ppermute | solution.py:380
  21.2 6.4 %collective-permute-start.7 = (f32[8,128]{1,0:T(8,128)S(1)}, f32[8,128]{1,0:T(8,128)}, u32[]{:S(2)}, u32[]{:S(2)}) collective-permute-start(f32[8,128]{1,0:T(8,128)S(1)} %collective-permute-done.3.refs_3_), channel_id=1, source_target_pairs={{0,1},{1,0},{2,3},{3,2},{4,5},{5,4},{6,7},{7,6},{8,9},{9,8},{10,11... | collective-permute-start | bytes 12296 | tf_op jit(solution)/shard_map/ppermute | solution.py:380
  47.1 5.5 %collective-permute-start.10 = (bf16[256,4608]{1,0:T(8,128)(2,1)S(1)}, bf16[256,4608]{1,0:T(8,128)(2,1)S(1)}, u32[]{:S(2)}, u32[]{:S(2)}) collective-permute-start(bf16[256,4608]{1,0:T(8,128)(2,1)S(1)} %bitcast.16), channel_id=1, source_target_pairs={{0,1},{1,0},{2,3},{3,2},{4,5},{5,4},{6,7},{7,6},{8,9},{9,8},{10,11... | collective-permute-start | bytes 7077896 | tf_op jit(solution)/shard_map/ppermute | solution.py:380
  48.5 25.1 %collective-permute-start.12 = (bf16[32,128,128]{2,1,0:T(8,128)(2,1)}, bf16[32,128,128]{2,1,0:T(8,128)(2,1)S(1)}, u32[]{:S(2)}, u32[]{:S(2)}) collective-permute-start(bf16[32,128,128]{2,1,0:T(8,128)(2,1)} %copy-done.10), channel_id=1, source_target_pairs={{0,2},{1,3},{6,4},{7,5},{8,10},{9,11},{14,12},{15,13},{16,18},{17,... | collective-permute-start | bytes 3145736 | tf_op jit(solution)/shard_map/ppermute | solution.py:406
  49.8 46.2 %collective-permute-start.11 = (bf16[32,128,128]{2,1,0:T(8,128)(2,1)}, bf16[32,128,128]{2,1,0:T(8,128)(2,1)}, u32[]{:S(2)}, u32[]{:S(2)}) collective-permute-start(bf16[32,128,128]{2,1,0:T(8,128)(2,1)} %copy-done.9), channel_id=1, source_target_pairs={{0,2},{1,3},{6,4},{7,5},{8,10},{9,11},{14,12},{15,13},{16,18},{17,... | collective-permute-start | bytes 3145736 | tf_op jit(solution)/shard_map/ppermute | solution.py:406
  74.9 29.9 %collective-permute-start.13 = (bf16[32,128,128]{2,1,0:T(8,128)(2,1)}, bf16[32,128,128]{2,1,0:T(8,128)(2,1)}, u32[]{:S(2)}, u32[]{:S(2)}) collective-permute-start(bf16[32,128,128]{2,1,0:T(8,128)(2,1)} %add_convert_fusion.2), channel_id=1, source_target_pairs={{2,4},{3,5},{4,2},{5,3},{10,12},{11,13},{12,10},{13,11},{18,20},{1... | collective-permute-start | bytes 3145736 | tf_op jit(solution)/shard_map/ppermute | solution.py:406
  76.5 52.1 %collective-permute-start.21 = (bf16[32,128,128]{2,1,0:T(8,128)(2,1)}, bf16[32,128,128]{2,1,0:T(8,128)(2,1)}, u32[]{:S(2)}, u32[]{:S(2)}) collective-permute-start(bf16[32,128,128]{2,1,0:T(8,128)(2,1)} %get-tuple-element.36), channel_id=1, source_target_pairs={{0,2},{1,3},{6,4},{7,5},{8,10},{9,11},{14,12},{15,13},{16,18},{17,... | collective-permute-start | bytes 3145736 | tf_op jit(solution)/shard_map/ppermute | solution.py:406
  96.0 28.1 %all-to-all-start.1 = ((f32[4,128,1024]{2,1,0:T(8,128)}), f32[4,128,1024]{2,1,0:T(8,128)S(1)}, u32[]{:S(2)}, u32[]{:S(2)}) async-start(f32[4,128,1024]{2,1,0:T(8,128)} %copy-done.6), calls=%async_computation.1 | async-start | bytes 4194304 | tf_op jit(solution)/shard_map/all_to_all | solution.py:398
  103.2 27.3 %collective-permute-start.22 = (bf16[32,128,128]{2,1,0:T(8,128)(2,1)}, bf16[32,128,128]{2,1,0:T(8,128)(2,1)}, u32[]{:S(2)}, u32[]{:S(2)}) collective-permute-start(bf16[32,128,128]{2,1,0:T(8,128)(2,1)} %add_convert_fusion.1), channel_id=1, source_target_pairs={{2,4},{3,5},{4,2},{5,3},{10,12},{11,13},{12,10},{13,11},{18,20},{1... | collective-permute-start | bytes 3145736 | tf_op jit(solution)/shard_map/ppermute | solution.py:406
  107.8 28.9 %collective-permute-start.23 = (bf16[32,128,128]{2,1,0:T(8,128)(2,1)}, bf16[32,128,128]{2,1,0:T(8,128)(2,1)}, u32[]{:S(2)}, u32[]{:S(2)}) collective-permute-start(bf16[32,128,128]{2,1,0:T(8,128)(2,1)} %add_convert_fusion), channel_id=1, source_target_pairs={{2,0},{3,1},{4,6},{5,7},{10,8},{11,9},{12,14},{13,15},{18,16},{19,... | collective-permute-start | bytes 3145736 | tf_op jit(solution)/shard_map/ppermute | solution.py:406
  125.5 9.6 %collective-permute-start.14 = (f32[8,128]{1,0:T(8,128)S(1)}, f32[8,128]{1,0:T(8,128)S(1)}, u32[]{:S(2)}, u32[]{:S(2)}) collective-permute-start(f32[8,128]{1,0:T(8,128)S(1)} %student_stats.1.refs_0_), channel_id=1, source_target_pairs={{0,2},{1,3},{2,0},{3,1},{4,6},{5,7},{6,4},{7,5},{8,10},{9,11},{10,... | collective-permute-start | bytes 12296 | tf_op jit(solution)/shard_map/ppermute | solution.py:380
  128.0 7.1 %collective-permute-start.15 = (f32[8,128]{1,0:T(8,128)S(1)}, f32[8,128]{1,0:T(8,128)S(1)}, u32[]{:S(2)}, u32[]{:S(2)}) collective-permute-start(f32[8,128]{1,0:T(8,128)S(1)} %student_stats.1.refs_0_), channel_id=1, source_target_pairs={{0,4},{1,5},{2,6},{3,7},{4,0},{5,1},{6,2},{7,3},{8,12},{9,13},{10,... | collective-permute-start | bytes 12296 | tf_op jit(solution)/shard_map/ppermute | solution.py:380
  128.6 7.0 %collective-permute-start.16 = (f32[8,128]{1,0:T(8,128)S(1)}, f32[8,128]{1,0:T(8,128)S(1)}, u32[]{:S(2)}, u32[]{:S(2)}) collective-permute-start(f32[8,128]{1,0:T(8,128)S(1)} %student_stats.1.refs_0_), channel_id=1, source_target_pairs={{0,6},{1,7},{2,4},{3,5},{4,2},{5,3},{6,0},{7,1},{8,14},{9,15},{10,... | collective-permute-start | bytes 12296 | tf_op jit(solution)/shard_map/ppermute | solution.py:380
  130.5 5.2 %collective-permute-start.17 = (f32[8,128]{1,0:T(8,128)S(1)}, f32[8,128]{1,0:T(8,128)S(1)}, u32[]{:S(2)}, u32[]{:S(2)}) collective-permute-start(f32[8,128]{1,0:T(8,128)S(1)} %student_stats.1.refs_0_), channel_id=1, source_target_pairs={{0,1},{1,0},{2,3},{3,2},{4,5},{5,4},{6,7},{7,6},{8,9},{9,8},{10,11... | collective-permute-start | bytes 12296 | tf_op jit(solution)/shard_map/ppermute | solution.py:380
  135.1 1.3 collective-permute-start.19
  135.6 1.2 collective-permute-start.20
  141.5 17.9 %all-to-all-start.2 = ((bf16[4,128,1024]{2,1,0:T(8,128)(2,1)}), bf16[4,128,1024]{2,1,0:T(8,128)(2,1)S(1)}, u32[]{:S(2)}, u32[]{:S(2)}) async-start(bf16[4,128,1024]{2,1,0:T(8,128)(2,1)} %copy-done.12), calls=%async_computation.2 | async-start | bytes 2097152 | tf_op jit(solution)/shard_map/all_to_all | solution.py:398
  145.4 4.4 %collective-permute-start.24 = (f32[128]{0:T(128)S(1)}, f32[128]{0:T(128)S(1)}, u32[]{:S(2)}, u32[]{:S(2)}) collective-permute-start(f32[128]{0:T(128)S(1)} %slice_bitcast_fusion), channel_id=1, source_target_pairs={{0,2},{1,3},{2,0},{3,1},{4,6},{5,7},{6,4},{7,5},{8,10},{9,11},{10,... | collective-permute-start | bytes 1544 | tf_op jit(solution)/shard_map/ppermute | solution.py:380
  145.4 4.9 %collective-permute-start.25 = (f32[128]{0:T(128)S(1)}, f32[128]{0:T(128)S(1)}, u32[]{:S(2)}, u32[]{:S(2)}) collective-permute-start(f32[128]{0:T(128)S(1)} %slice_bitcast_fusion), channel_id=1, source_target_pairs={{0,4},{1,5},{2,6},{3,7},{4,0},{5,1},{6,2},{7,3},{8,12},{9,13},{10,... | collective-permute-start | bytes 1544 | tf_op jit(solution)/shard_map/ppermute | solution.py:380
  147.8 5.3 %collective-permute-start.26 = (f32[128]{0:T(128)S(1)}, f32[128]{0:T(128)S(1)}, u32[]{:S(2)}, u32[]{:S(2)}) collective-permute-start(f32[128]{0:T(128)S(1)} %slice_bitcast_fusion), channel_id=1, source_target_pairs={{0,6},{1,7},{2,4},{3,5},{4,2},{5,3},{6,0},{7,1},{8,14},{9,15},{10,... | collective-permute-start | bytes 1544 | tf_op jit(solution)/shard_map/ppermute | solution.py:380
  149.8 3.4 %collective-permute-start.27 = (f32[128]{0:T(128)S(1)}, f32[128]{0:T(128)S(1)}, u32[]{:S(2)}, u32[]{:S(2)}) collective-permute-start(f32[128]{0:T(128)S(1)} %slice_bitcast_fusion), channel_id=1, source_target_pairs={{0,1},{1,0},{2,3},{3,2},{4,5},{5,4},{6,7},{7,6},{8,9},{9,8},{10,11... | collective-permute-start | bytes 1544 | tf_op jit(solution)/shard_map/ppermute | solution.py:380
  149.8 3.4 %collective-permute-start.28 = (f32[128]{0:T(128)S(1)}, f32[128]{0:T(128)S(1)}, u32[]{:S(2)}, u32[]{:S(2)}) collective-permute-start(f32[128]{0:T(128)S(1)} %collective-permute-done.24), channel_id=1, source_target_pairs={{0,1},{1,0},{2,3},{3,2},{4,5},{5,4},{6,7},{7,6},{8,9},{9,8},{10,11... | collective-permute-start | bytes 1544 | tf_op jit(solution)/shard_map/ppermute | solution.py:380
  150.3 2.9 %collective-permute-start.29 = (f32[128]{0:T(128)S(1)}, f32[128]{0:T(128)S(1)}, u32[]{:S(2)}, u32[]{:S(2)}) collective-permute-start(f32[128]{0:T(128)S(1)} %collective-permute-done.25), channel_id=1, source_target_pairs={{0,1},{1,0},{2,3},{3,2},{4,5},{5,4},{6,7},{7,6},{8,9},{9,8},{10,11... | collective-permute-start | bytes 1544 | tf_op jit(solution)/shard_map/ppermute | solution.py:380
  (20 other events, 119.1 us)
where the time goes:
time: 170 us; the launch traced here: 169 us
  waiting for transfers between devices  57.4 us (34%)
  starting transfers between devices  45.9 us (27%)
  Pallas kernels  41 us (24%)
  local copies, waits for them, and re-layouts  15.1 us (9%)
  other arithmetic  8.47 us (5%)
    ppermute x6, waiting for transfers between devices, send(): lax.ppermute(x, 'vocab', [(2 * a + c, 2 * b + c) for a, b in hops for c i...  24.4 us
    all_to_all x3, waiting for transfers between devices, exchange_tok(): return lax.all_to_all(x, 'tok', split_axis=0, concat_axis=0, tiled=True)  18.7 us
    ppermute x25, starting transfers between devices, swap(): lax.ppermute(x, axis, [(i, i ^ mask) for i in range(lax.axis_size(axis))])  18.4 us
    ppermute x25, waiting for transfers between devices, swap(): lax.ppermute(x, axis, [(i, i ^ mask) for i in range(lax.axis_size(axis))])  14.2 us
    ppermute x6, starting transfers between devices, send(): lax.ppermute(x, 'vocab', [(2 * a + c, 2 * b + c) for a, b in hops for c i...  14.1 us
    all_to_all x3, starting transfers between devices, exchange_tok(): return lax.all_to_all(x, 'tok', split_axis=0, concat_axis=0, tiled=True)  13.4 us
    pallas_call x2, Pallas kernels, chip_sums(): pl.pallas_call(functools.partial(sums_kernel, first=first, fan=fan), grid...  12.7 us
    unnamed x37, local copies, waits for them, and re-layouts  12.6 us
  transfers between devices with their start and end apart: 34, of which 13 were waited for; matrix products, arithmetic and copies ran while one was open for 7% of the time, Pallas kernels for 18%

commit v1 on v0

--- a/solution.py
+++ b/solution.py
@@ -33,8 +33,8 @@
     return top, total
 
 
-def split_rows(refs):
-    return [[ref[k : k + 1, :] for k in range(8)] for ref in refs]
+def split_rows(ref):
+    return [[ref[v, k : k + 1, :] for k in range(8)] for v in range(ref.shape[0])]
 
 
 def rows_from_columns(columns):
@@ -51,11 +51,10 @@
     return jnp.concatenate(rows + [jnp.zeros((LANES - len(rows), n), F32)], axis=0).T
 
 
-def teacher_kernel(*refs):
-    shards, stat_ref = refs[:-1], refs[-1]
-    rows, cols = shards[0].shape
-    places = [(ref, j) for ref in shards for j in range(0, cols, LANES)]
-    read = lambda place: place[0][:, place[1] : place[1] + LANES].astype(F32)
+def teacher_kernel(x_ref, stat_ref):
+    rows, cols = x_ref.shape
+    places = range(0, cols, LANES)
+    read = lambda place: x_ref[:, place : place + LANES].astype(F32)
     top = jnp.full((rows, LANES), -jnp.inf, F32)
     for place in places:
         top = jnp.maximum(top, read(place))
@@ -63,20 +62,19 @@
     total = jnp.zeros((rows, LANES), F32)
     for place in places:
         total = total + jnp.exp(read(place) - top)
-    stat_ref[...] = rows_from_columns([top, jnp.sum(total, axis=1, keepdims=True)])
-
-
-def teacher_stats(*shards):
-    size = sum(x.size for x in shards)
+    stat_ref[...] = jnp.broadcast_to(rows_from_columns([top, jnp.sum(total, axis=1, keepdims=True)]), stat_ref.shape)
+
+
+def teacher_stats(x, copies):
     return pl.pallas_call(
         teacher_kernel,
-        in_specs=[VMEM_SPEC] * len(shards),
+        in_specs=[VMEM_SPEC],
         out_specs=VMEM_SPEC,
-        out_shape=jax.ShapeDtypeStruct((8, shards[0].shape[0]), F32),
-        compiler_params=params(40),
+        out_shape=jax.ShapeDtypeStruct((copies, 8, x.shape[0]), F32),
+        compiler_params=params(16),
         cost_estimate=COST,
         name="teacher_stats",
-    )(*shards)
+    )(x)
 
 
 def divide(x, n):
@@ -133,8 +131,7 @@
     )(spot, own_target, peer_target)
 
 
-def probs_kernel(x_own, x_peer, *refs):
-    stats, probs = refs[:-1], refs[-1]
+def probs_kernel(x_own, x_peer, stats, probs):
     blocks = x_own.shape[1] // LANES
     top, total = total_at(split_rows(stats), 0, 1)
     columns = columns_from_rows([top, 1.0 / total])
@@ -195,13 +192,13 @@
     rows, cols = x_own.shape
     return pl.pallas_call(
         probs_kernel,
-        in_specs=[VMEM_SPEC] * (2 + len(stats)),
+        in_specs=[VMEM_SPEC] * 3,
         out_specs=VMEM_SPEC,
         out_shape=jax.ShapeDtypeStruct((2 * cols // LANES, rows, LANES), BF16),
         compiler_params=params(16),
         cost_estimate=COST,
         name="teacher_probs",
-    )(x_own, x_peer, *stats)
+    )(x_own, x_peer, stats)
 
 
 def chip_sums(lists, counts, probs, w_own, w_peer, first, n_out, steps, slots):
@@ -284,24 +281,25 @@
             total = total + jnp.exp(logits_ref[t, :, b : b + LANES] - top)
     total = jnp.sum(total, axis=1, keepdims=True)
     hit = jnp.sum(hit, axis=1, keepdims=True)
-    stat_ref[...] = mass_ref[...] + rows_from_columns([jnp.zeros_like(hit), top, total, hit])
-
-
-def student_stats(base, label_column, mass, logits):
+    tile = mass_ref[...] + rows_from_columns([jnp.zeros_like(hit), top, total, hit])
+    stat_ref[...] = jnp.broadcast_to(tile, stat_ref.shape)
+
+
+def student_stats(base, label_column, mass, logits, copies):
     return pl.pallas_call(
         student_kernel,
         in_specs=[SMEM_SPEC] + [VMEM_SPEC] * 3,
         out_specs=VMEM_SPEC,
-        out_shape=jax.ShapeDtypeStruct(mass.shape, F32),
+        out_shape=jax.ShapeDtypeStruct((copies,) + mass.shape, F32),
         compiler_params=params(16),
         cost_estimate=COST,
         name="student_stats",
     )(base, label_column, mass, logits)
 
 
-def grad_kernel(base_ref, labels_ref, *refs, n_stats, n_sums):
-    stats, sums = refs[:n_stats], refs[n_stats : n_stats + n_sums]
-    logits_ref, grad_ref, loss_ref, columns, inner = refs[n_stats + n_sums :]
+def grad_kernel(base_ref, labels_ref, stats, *refs, n_sums, first):
+    sums = refs[:n_sums]
+    logits_ref, grad_ref, loss_ref, columns, inner = refs[n_sums:]
     step = pl.program_id(0)
     _, rows, cols = logits_ref.shape
 
@@ -319,7 +317,7 @@
 
     lane = lax.broadcasted_iota(jnp.int32, (rows, LANES), 1)
     lift, log_total = columns[:, 0:1], columns[:, 1:2]
-    label = labels_ref[...] - base_ref[step]
+    label = labels_ref[...] - (base_ref[step] + first)
     running = inner[...]
     for b in range(cols // LANES):
         place = slice(b * LANES, (b + 1) * LANES)
@@ -335,44 +333,65 @@
         loss_ref[1:2, :] = rows_from_columns([jnp.sum(inner[...], axis=1, keepdims=True)])[0:1, :]
 
 
-def grad_logits(base, label_column, stats, sums, logits):
+def grad_logits(base, label_column, stats, sums, logits, part, parts):
     n_tok, rows, cols = logits.shape
+    cols //= parts
     per = cols // LANES
     whole = lambda shape: pl.BlockSpec(shape, lambda t: (0,) * len(shape))
-    one = pl.BlockSpec((1, rows, cols), lambda t: (t, 0, 0))
-    return pl.pallas_call(
-        functools.partial(grad_kernel, n_stats=len(stats), n_sums=len(sums)),
+    return pl.pallas_call(
+        functools.partial(grad_kernel, n_sums=len(sums), first=part * cols),
         grid=(n_tok,),
-        in_specs=[SMEM_SPEC, whole(label_column.shape)]
-        + [whole(s.shape) for s in stats]
-        + [pl.BlockSpec((s.shape[0], per, rows, LANES), lambda t: (0, t, 0, 0)) for s in sums]
-        + [one],
-        out_specs=[one, whole((8, rows))],
+        in_specs=[SMEM_SPEC, whole(label_column.shape), whole(stats.shape)]
+        + [pl.BlockSpec((s.shape[0], per, rows, LANES), lambda t: (0, parts * t + part, 0, 0)) for s in sums]
+        + [pl.BlockSpec((1, rows, cols), lambda t: (t, 0, part))],
+        out_specs=[pl.BlockSpec((1, rows, cols), lambda t: (t, 0, 0)), whole((8, rows))],
         out_shape=[jax.ShapeDtypeStruct((n_tok, rows, cols), BF16), jax.ShapeDtypeStruct((8, rows), F32)],
         scratch_shapes=[pltpu.VMEM((rows, LANES), F32), pltpu.VMEM((rows, LANES), F32)],
         compiler_params=params(24),
         cost_estimate=COST,
         name="grad_logits",
-    )(base, label_column, *stats, *sums, logits)
-
-
-def product_kernel(a_ref, b_ref, o_ref):
+    )(base, label_column, stats, *sums, logits)
+
+
+def product_kernel(a_ref, b_ref, *refs):
+    o_ref = refs[-1]
     o_ref[...] = jnp.dot(a_ref[...], b_ref[...], preferred_element_type=F32).astype(o_ref.dtype)
 
 
-def head_product(a, b):
+def head_product(a, b, part, parts, earlier):
     m, k = a.shape
     n = b.shape[1]
     tile = m // 4
     return pl.pallas_call(
         product_kernel,
         grid=(m // tile,),
-        in_specs=[pl.BlockSpec((tile, k), lambda i: (i, 0)), pl.BlockSpec((k, n), lambda i: (0, 0))],
-        out_specs=pl.BlockSpec((tile, n), lambda i: (i, 0)),
-        out_shape=jax.ShapeDtypeStruct((m, n), BF16),
+        in_specs=[pl.BlockSpec((tile, k), lambda i: (i, 0)), pl.BlockSpec((k, n), lambda i: (0, 0))]
+        + [pl.BlockSpec(memory_space=pl.ANY)] * len(earlier),
+        out_specs=pl.BlockSpec((tile, n), lambda i: (i, part)),
+        out_shape=jax.ShapeDtypeStruct((m, n * parts), BF16),
+        input_output_aliases={2: 0} if earlier else {},
         compiler_params=params(32),
         cost_estimate=COST,
         name="head_product",
+    )(a, b, *earlier)
+
+
+def plus_kernel(a_ref, b_ref, o_ref):
+    o_ref[...] = (a_ref[...].astype(F32) + b_ref[...].astype(F32)).astype(BF16)
+
+
+def plus(a, b):
+    blocks = 4
+    spec = pl.BlockSpec((a.shape[0] // blocks,) + a.shape[1:], lambda i: (i, 0, 0))
+    return pl.pallas_call(
+        plus_kernel,
+        grid=(blocks,),
+        in_specs=[spec, spec],
+        out_specs=spec,
+        out_shape=jax.ShapeDtypeStruct(a.shape, BF16),
+        compiler_params=params(16),
+        cost_estimate=COST,
+        name="merge",
     )(a, b)
 
 
@@ -380,26 +399,12 @@
     return lax.ppermute(x, axis, [(i, i ^ mask) for i in range(lax.axis_size(axis))])
 
 
-def gather_chips(x):
-    n = lax.axis_size("vocab")
-    if n > 8:
-        lines = [[2 * z + c for z in range(n // 2)] for c in range(2)]
-        everything = lax.all_gather(x, "vocab", axis=0, axis_index_groups=lines)
-        return [everything[z] for z in range(n // 2)]
-    return [x] + [swap(x, "vocab", r) for r in range(2, n, 2)]
-
-
-def gather_cores(x):
-    chips = gather_chips(x)
-    return chips + [swap(chip, "vocab", 1) for chip in chips]
+def gather_vocab(copies):
+    return lax.all_to_all(copies, "vocab", split_axis=0, concat_axis=0, tiled=True)
 
 
 def exchange_tok(x):
     return lax.all_to_all(x, "tok", split_axis=0, concat_axis=0, tiled=True)
-
-
-def plus(a, b):
-    return (a.astype(F32) + b.astype(F32)).astype(BF16)
 
 
 def send(x, hops):
@@ -420,27 +425,27 @@
     slots = n_tok * per
     in_line = n_z == 4
 
-    half = lax.dynamic_slice_in_dim(hidden, spot[0] * (rows // 2), rows // 2)
-    near = exchange_tok(jnp.broadcast_to(half, (n_tok,) + half.shape)).reshape(n_tok * (rows // 2), -1)
     peer_logits = swap(teacher_logits, "vocab", 1)
     peer_target = swap(map_target, "vocab", 1)
     peer_weight = swap(map_weight, "vocab", 1)
-    totals = gather_cores(teacher_stats(teacher_logits))
+    teacher = teacher_stats(teacher_logits, n_vocab)
+    totals = gather_vocab(teacher)
+    half = lax.dynamic_slice_in_dim(hidden, spot[0] * (rows // 2), rows // 2)
+    half, teacher = lax.optimization_barrier((half, teacher))
+    near = exchange_tok(jnp.broadcast_to(half, (n_tok,) + half.shape)).reshape(n_tok * (rows // 2), -1)
     lists, counts = plan(spot, map_target, peer_target, n_z, per, n_vocab, in_line)
     probs = teacher_probs(teacher_logits, peer_logits, totals)
 
-    sums_args = (lists, counts, probs, map_weight, peer_weight)
     if in_line:
         inward, across, outward = [(0, 1), (3, 2)], [(1, 2), (2, 1)], [(1, 0), (2, 3)]
-        far_outer, mass_a = chip_sums(*sums_args, 0, 1, 1, slots)
+        far_outer, far_inner, mass_a = chip_sums(lists, counts, probs, map_weight, peer_weight, 0, 2, 1, slots)
         first = send(far_outer, inward)
+        second = send(far_inner, inward)
         probs, mass_a = lax.optimization_barrier((probs, mass_a))
-        far_inner, beside, own, mass_b = chip_sums(lists, counts, probs, map_weight, peer_weight, 1, 3, 1, slots)
+        beside, own, mass_b = chip_sums(lists, counts, probs, map_weight, peer_weight, 2, 2, 1, slots)
         mass = mass_a + mass_b
-        second = send(far_inner, inward)
-        third = send(beside, inward)
     else:
-        sums, mass = chip_sums(*sums_args, 0, 1, n_z, slots)
+        sums, mass = chip_sums(lists, counts, probs, map_weight, peer_weight, 0, 1, n_z, slots)
         lines = [[2 * z + c for z in range(n_z)] for c in range(2)]
         sums = lax.all_to_all(
             sums.reshape(n_z, slots, rows, block),
@@ -456,26 +461,43 @@
     far = swap(near, "vocab", 1)
     scores, turned = student_logits(spot, mass, near, far, new_head, n_tok)
     scores = exchange_tok(scores)
+    label_column = lax.dynamic_slice_in_dim(labels, tok * rows, rows).reshape(rows, 1)
+    base = (jnp.arange(n_tok, dtype=jnp.int32) * n_vocab + vocab) * new_cols
     if in_line:
         first, turned = lax.optimization_barrier((first, turned))
         merged = plus(far_outer, first)
         crossed_outer = send(merged, across)
-        second, merged = lax.optimization_barrier((second, merged))
+        waited, merged = lax.optimization_barrier((beside, merged))
+        third = send(waited, inward)
+        scores, merged = lax.optimization_barrier((scores, merged))
+        student = student_stats(base, label_column, mass, scores, n_vocab)
+        second, student = lax.optimization_barrier((second, student))
         merged_inner = plus(far_inner, second)
         crossed_inner = send(merged_inner, across)
+        crossed_outer, merged_inner = lax.optimization_barrier((crossed_outer, merged_inner))
         merged_near = plus(beside, crossed_outer)
         arrived = send(merged_near, outward)
-        scores, merged_inner, merged_near = lax.optimization_barrier((scores, merged_inner, merged_near))
+        student, merged_near = lax.optimization_barrier((student, merged_near))
         sums = [x[None] for x in (own, third, crossed_inner, arrived)]
-    label_column = lax.dynamic_slice_in_dim(labels, tok * rows, rows).reshape(rows, 1)
-    base = (jnp.arange(n_tok, dtype=jnp.int32) * n_vocab + vocab) * new_cols
-    stats = gather_cores(student_stats(base, label_column, mass, scores))
-
-    grads, loss_rows = grad_logits(base, label_column, stats, sums, scores)
-    grads = exchange_tok(grads).reshape(n_tok * rows, new_cols)
-    inner = tree(jnp.add, gather_cores(loss_rows[1]))
-    loss = loss_rows[0] - inner
-    return (loss, head_product(turned, grads))
+    else:
+        student = student_stats(base, label_column, mass, scores, n_vocab)
+    stats = gather_vocab(student)
+
+    parts = 2
+    swapped, inner = [], 0.0
+    for part in range(parts):
+        if part:
+            scores, grads = lax.optimization_barrier((scores, grads))
+        grads, loss_rows = grad_logits(base, label_column, stats, sums, scores, part, parts)
+        swapped.append(exchange_tok(grads).reshape(n_tok * rows, -1))
+        inner = inner + loss_rows[1]
+    inner = gather_vocab(jnp.broadcast_to(inner, (n_vocab, 1, rows)))
+    loss = loss_rows[0] - jnp.sum(inner, axis=(0, 1))
+    head_grad = head_product(turned, swapped[0], 0, parts, [])
+    for part in range(1, parts):
+        late, head_grad = lax.optimization_barrier((swapped[part], head_grad))
+        head_grad = head_product(turned, late, part, parts, [head_grad])
+    return (loss, head_grad)
 
 
 def solution(mesh):

time: 170 us -> 185 us (1.088)
  blocking collectives: 0 us -> 21.4 us
  waiting for transfers between devices: 57.4 us -> 40.6 us
  Pallas kernels: 41 us -> 56.6 us
  other arithmetic: 8.47 us -> 1.16 us
  local copies, waits for them, and re-layouts: 15.1 us -> 21.6 us
  starting transfers between devices: 45.9 us -> 41.3 us
    all_to_all x0 -> x2, waiting for transfers between devices: none -> 21.8 us  [gather_vocab(): lax.all_to_all(copies, 'vocab', split_axis=0, concat_axis=0, tiled=True)]
    all_to_all x0 -> x2, blocking collectives: none -> 21.4 us  [the longest x1 12.5 us: exchange_tok(): return lax.all_to_all(x, 'tok', split_axis=0, concat_axis=0, tiled=True)]
    ppermute x6, waiting for transfers between devices: 24.4 us -> 4.66 us  [send(): lax.ppermute(x, 'vocab', [(2 * a + c, 2 * b + c) for a, b in hops for c i...]
    ppermute x25 -> x4, starting transfers between devices: 18.4 us -> 1.03 us  [swap(): lax.ppermute(x, axis, [(i, i ^ mask) for i in range(lax.axis_size(axis))])]
    all_to_all x0 -> x2, starting transfers between devices: none -> 14.1 us  [gather_vocab(): lax.all_to_all(copies, 'vocab', split_axis=0, concat_axis=0, tiled=True)]
    pallas_call x3 -> x7, Pallas kernels: 6.62 us -> 19.8 us  [the longest x3 10.4 us: plus(): pl.pallas_call(plus_kernel, grid=(blocks,), in_specs=[spec, spec], out_sp...]
    ppermute x25 -> x4, waiting for transfers between devices: 14.2 us -> 2.09 us  [swap(): lax.ppermute(x, axis, [(i, i ^ mask) for i in range(lax.axis_size(axis))])]
    convert_element_type x3 -> x0, other arithmetic: 7.29 us -> none  [plus(): return (a.astype(F32) + b.astype(F32)).astype(BF16)]
  transfers between devices with their start and end apart: 34 -> 15, of which waited for: 13 -> 7; matrix products, arithmetic and copies ran while one was open for 7% -> 2% of each run, Pallas kernels for 18% -> 25%
where the time goes in v1:
time: 185 us; the launch traced here: 184 us
  Pallas kernels  56.6 us (31%)
  starting transfers between devices  41.3 us (22%)
  waiting for transfers between devices  40.6 us (22%)
  local copies, waits for them, and re-layouts  21.6 us (12%)
  blocking collectives  21.4 us (12%)
    all_to_all x2, waiting for transfers between devices, gather_vocab(): lax.all_to_all(copies, 'vocab', split_axis=0, concat_axis=0, tiled=True)  21.8 us
    unnamed x47, local copies, waits for them, and re-layouts  19.1 us
    ppermute x6, starting transfers between devices, send(): lax.ppermute(x, 'vocab', [(2 * a + c, 2 * b + c) for a, b in hops for c i...  14.8 us
    all_to_all x2, starting transfers between devices, gather_vocab(): lax.all_to_all(copies, 'vocab', split_axis=0, concat_axis=0, tiled=True)  14.1 us
    pallas_call x2, Pallas kernels, chip_sums(): pl.pallas_call(functools.partial(sums_kernel, first=first, fan=fan), grid...  12.8 us
    all_to_all x1, blocking collectives, exchange_tok(): return lax.all_to_all(x, 'tok', split_axis=0, concat_axis=0, tiled=True)  12.5 us
    all_to_all x3, waiting for transfers between devices, exchange_tok(): return lax.all_to_all(x, 'tok', split_axis=0, concat_axis=0, tiled=True)  12 us
    all_to_all x3, starting transfers between devices, exchange_tok(): return lax.all_to_all(x, 'tok', split_axis=0, concat_axis=0, tiled=True)  11.4 us
  transfers between devices with their start and end apart: 15, of which 7 were waited for; matrix products, arithmetic and copies ran while one was open for 2% of the time, Pallas kernels for 25%

profile of v1, /device:TPU:0, one launch (start us, length us, event | category | flops | bytes accessed | tf_op | source)
XLA Modules:
  0.0 183.5 jit_solution(1920493229876518435)
XLA Ops:
  3.6 6.0 %all-to-all-start = ((f32[8,8,128]{2,1,0:T(8,128)}), f32[8,8,128]{2,1,0:T(8,128)S(1)}, u32[]{:S(2)}, u32[]{:S(2)}) async-start(f32[8,8,128]{2,1,0:T(8,128)} %teacher_stats.1), calls=%async_computation | async-start | bytes 65536 | tf_op jit(solution)/shard_map/all_to_all | solution.py:403
  9.7 5.7 %all-to-all-done.stats = f32[8,8,128]{2,1,0:T(8,128)S(1)} async-done(((f32[8,8,128]{2,1,0:T(8,128)}), f32[8,8,128]{2,1,0:T(8,128)S(1)}, u32[]{:S(2)}, u32[]{:S(2)}) %all-to-all-start) | async-done | bytes 32800 | tf_op jit(solution)/shard_map/all_to_all | solution.py:403
  17.0 3.7 %all-to-all-start.1 = ((bf16[4,64,4608]{2,1,0:T(8,128)(2,1)}), bf16[4,64,4608]{2,1,0:T(8,128)(2,1)S(1)}, u32[]{:S(2)}, u32[]{:S(2)}) async-start(bf16[4,64,4608]{2,1,0:T(8,128)(2,1)} %broadcast_in_dim.18), calls=%async_computation.1 | async-start | bytes 4718592 | tf_op jit(solution)/shard_map/all_to_all | solution.py:407
  23.5 5.2 %entry_lists.1 = (s32[4,260]{1,0:T(4,128)}, s32[4]{0:T(128)}) custom-call(s32[2]{0:T(128)} %pad_add_fusion.spot_ref, s32[32,4]{1,0:T(8,128)} %copy-done.22, s32[32,4]{1,0:T(8,128)} %collective-permute-done.peer_ref), custom_call_target="tpu_custom_call" | custom-call | flops 1024 | bytes 1024 | tf_op jit(solution)/shard_map/entry_lists/pallas_call | solution.py:124
  31.1 2.2 %teacher_probs.1.probs = bf16[64,128,128]{2,1,0:T(8,128)(2,1)S(1)} custom-call(bf16[128,4096]{1,0:T(8,128)(2,1)S(1)} %copy-done.8, bf16[128,4096]{1,0:T(8,128)(2,1)} %collective-permute-done.1.x_peer, f32[8,8,128]{2,1,0:T(8,128)S(1)} %copy-done.18), custom_call_target="tpu_custom_call" | custom-call | flops 1024 | bytes 1024 | tf_op jit(solution)/shard_map/teacher_probs/pallas_call | solution.py:193
  33.3 6.3 %chip_sums.2 = (bf16[32,128,128]{2,1,0:T(8,128)(2,1)S(1)}, bf16[32,128,128]{2,1,0:T(8,128)(2,1)S(1)}, f32[8,128]{1,0:T(8,128)S(1)}) custom-call(s32[4,260]{1,0:T(4,128)S(1)} %copy-done.19, s32[4]{0:T(128)S(1)} %copy-done.21, bf16[64,128,128]{2,1,0:T(8,128)(2,1)S(1)} %teacher_probs.1.probs, bf16[32,4,128,128]{3,2,1,0:T(8,128)(2,1)S(1)} %copy-done.4, ...), custom_call_target="tpu_custom_call" | custom-call | flops 1024 | bytes 1024 | tf_op jit(solution)/shard_map/chip_sums/pallas_call | solution.py:209
  41.7 6.5 %chip_sums.3 = (bf16[32,128,128]{2,1,0:T(8,128)(2,1)S(1)}, bf16[32,128,128]{2,1,0:T(8,128)(2,1)S(1)}, f32[8,128]{1,0:T(8,128)S(1)}) custom-call(s32[4,260]{1,0:T(4,128)S(1)} %copy-done.19, s32[4]{0:T(128)S(1)} %copy-done.21, bf16[64,128,128]{2,1,0:T(8,128)(2,1)S(1)} %teacher_probs.1.probs, bf16[32,4,128,128]{3,2,1,0:T(8,128)(2,1)S(1)} %copy-done.4, ...), custom_call_target="tpu_custom_call" | custom-call | flops 1024 | bytes 1024 | tf_op jit(solution)/shard_map/chip_sums/pallas_call | solution.py:209
  50.2 3.4 %collective-permute-start.5 = (bf16[32,128,128]{2,1,0:T(8,128)(2,1)}, bf16[32,128,128]{2,1,0:T(8,128)(2,1)}, u32[]{:S(2)}, u32[]{:S(2)}) collective-permute-start(bf16[32,128,128]{2,1,0:T(8,128)(2,1)} %copy-done.14), channel_id=1, source_target_pairs={{0,2},{1,3},{6,4},{7,5},{8,10},{9,11},{14,12},{15,13},{16,18},{17,... | collective-permute-start | bytes 3145736 | tf_op jit(solution)/shard_map/ppermute | solution.py:411
  54.8 8.0 %student_logits.1 = (f32[4,128,1024]{2,1,0:T(8,128)S(1)}, bf16[4608,512]{1,0:T(8,128)(2,1)S(1)}) custom-call(s32[2]{0:T(128)S(1)} %copy-done.20, f32[8,128]{1,0:T(8,128)S(1)} %add.31.after_ref.mass_ref, bf16[256,4608]{1,0:T(8,128)(2,1)S(1)} %bitcast.17, bf16[256,4608]{1,0:T(8,128)(2,1)S(1)} %collective-permute-done.4.far_ref, bf16[4608,1024]{1,0:T(8,128)(2,1)} %head_ref.1), custom_call_target="tpu_custom_call" | custom-call | flops 1024 | bytes 1024 | tf_op jit(solution)/shard_map/student_logits/pallas_call | solution.py:251
  62.8 2.1 %copy-done.1 = bf16[4608,512]{1,0:T(8,128)(2,1)} copy-done((bf16[4608,512]{1,0:T(8,128)(2,1)}, bf16[4608,512]{1,0:T(8,128)(2,1)S(1)}, u32[]{:S(2)}) %copy-start.1) | copy-done | bytes 4718616
  66.3 4.2 %all-to-all-start.2 = ((f32[4,128,1024]{2,1,0:T(8,128)}), f32[4,128,1024]{2,1,0:T(8,128)S(1)}, u32[]{:S(2)}, u32[]{:S(2)}) async-start(f32[4,128,1024]{2,1,0:T(8,128)} %copy-done.9), calls=%async_computation.2 | async-start | bytes 4194304 | tf_op jit(solution)/shard_map/all_to_all | solution.py:407
  70.5 3.3 %collective-permute-start.3 = (bf16[32,128,128]{2,1,0:T(8,128)(2,1)}, bf16[32,128,128]{2,1,0:T(8,128)(2,1)}, u32[]{:S(2)}, u32[]{:S(2)}) collective-permute-start(bf16[32,128,128]{2,1,0:T(8,128)(2,1)} %copy-done.12), channel_id=1, source_target_pairs={{0,2},{1,3},{6,4},{7,5},{8,10},{9,11},{14,12},{15,13},{16,18},{17,... | collective-permute-start | bytes 3145736 | tf_op jit(solution)/shard_map/ppermute | solution.py:411
  73.8 2.6 %collective-permute-done.5.b_ref = bf16[32,128,128]{2,1,0:T(8,128)(2,1)} collective-permute-done((bf16[32,128,128]{2,1,0:T(8,128)(2,1)}, bf16[32,128,128]{2,1,0:T(8,128)(2,1)}, u32[]{:S(2)}, u32[]{:S(2)}) %collective-permute-start.5) | collective-permute-done | bytes 1048608 | tf_op jit(solution)/shard_map/ppermute | solution.py:411
  77.6 3.5 %merge.3 = bf16[32,128,128]{2,1,0:T(8,128)(2,1)} custom-call(bf16[32,128,128]{2,1,0:T(8,128)(2,1)S(1)} %copy-done.15, bf16[32,128,128]{2,1,0:T(8,128)(2,1)} %collective-permute-done.5.b_ref), custom_call_target="tpu_custom_call" | custom-call | flops 1024 | bytes 1024 | tf_op jit(solution)/shard_map/merge/pallas_call | solution.py:386
  83.6 12.0 %all-to-all-done.2.logits_ref.refs_4_ = f32[4,128,1024]{2,1,0:T(8,128)S(1)} async-done(((f32[4,128,1024]{2,1,0:T(8,128)}), f32[4,128,1024]{2,1,0:T(8,128)S(1)}, u32[]{:S(2)}, u32[]{:S(2)}) %all-to-all-start.2) | async-done | bytes 2097184 | tf_op jit(solution)/shard_map/all_to_all | solution.py:407
  95.6 3.6 %collective-permute-start.7 = (bf16[32,128,128]{2,1,0:T(8,128)(2,1)}, bf16[32,128,128]{2,1,0:T(8,128)(2,1)}, u32[]{:S(2)}, u32[]{:S(2)}) collective-permute-start(bf16[32,128,128]{2,1,0:T(8,128)(2,1)} %copy-done.10), channel_id=1, source_target_pairs={{0,2},{1,3},{6,4},{7,5},{8,10},{9,11},{14,12},{15,13},{16,18},{17,... | collective-permute-start | bytes 3145736 | tf_op jit(solution)/shard_map/ppermute | solution.py:411
  99.2 2.0 %student_stats.1 = f32[8,8,128]{2,1,0:T(8,128)} custom-call(s32[4]{0:T(128)S(1)} %add_multiply_fusion.base_ref, s32[128,1]{1,0:T(8,128)S(1)} %copy.23.labels_ref, f32[8,128]{1,0:T(8,128)S(1)} %add.31.after_ref.mass_ref, f32[4,128,1024]{2,1,0:T(8,128)S(1)} %all-to-all-done.2.logits_ref.refs_4_), custom_call_target="tpu_custom_call" | custom-call | flops 1024 | bytes 1024 | tf_op jit(solution)/shard_map/student_stats/pallas_call | solution.py:289
  101.2 3.5 %merge.4 = bf16[32,128,128]{2,1,0:T(8,128)(2,1)} custom-call(bf16[32,128,128]{2,1,0:T(8,128)(2,1)S(1)} %copy-done.13, bf16[32,128,128]{2,1,0:T(8,128)(2,1)} %collective-permute-done.3.b_ref), custom_call_target="tpu_custom_call" | custom-call | flops 1024 | bytes 1024 | tf_op jit(solution)/shard_map/merge/pallas_call | solution.py:386
  104.6 1.7 collective-permute-start.8
  106.3 3.5 %merge.5 = bf16[32,128,128]{2,1,0:T(8,128)(2,1)} custom-call(bf16[32,128,128]{2,1,0:T(8,128)(2,1)S(1)} %copy-done.11, bf16[32,128,128]{2,1,0:T(8,128)(2,1)} %collective-permute-done.6.b_ref), custom_call_target="tpu_custom_call" | custom-call | flops 1024 | bytes 1024 | tf_op jit(solution)/shard_map/merge/pallas_call | solution.py:386
  111.1 8.1 %all-to-all-start.3 = ((f32[8,8,128]{2,1,0:T(8,128)}), f32[8,8,128]{2,1,0:T(8,128)S(1)}, u32[]{:S(2)}, u32[]{:S(2)}) async-start(f32[8,8,128]{2,1,0:T(8,128)} %student_stats.1), calls=%async_computation.3 | async-start | bytes 65536 | tf_op jit(solution)/shard_map/all_to_all | solution.py:403
  119.1 2.0 %collective-permute-done.7 = bf16[32,128,128]{2,1,0:T(8,128)(2,1)} collective-permute-done((bf16[32,128,128]{2,1,0:T(8,128)(2,1)}, bf16[32,128,128]{2,1,0:T(8,128)(2,1)}, u32[]{:S(2)}, u32[]{:S(2)}) %collective-permute-start.7) | collective-permute-done | bytes 1048608 | tf_op jit(solution)/shard_map/ppermute | solution.py:411
  121.2 16.1 %all-to-all-done.3.stats = f32[8,8,128]{2,1,0:T(8,128)S(1)} async-done(((f32[8,8,128]{2,1,0:T(8,128)}), f32[8,8,128]{2,1,0:T(8,128)S(1)}, u32[]{:S(2)}, u32[]{:S(2)}) %all-to-all-start.3) | async-done | bytes 32800 | tf_op jit(solution)/shard_map/all_to_all | solution.py:403
  138.5 3.0 %grad_logits.2 = (bf16[4,128,512]{2,1,0:T(8,128)(2,1)S(1)}, f32[8,128]{1,0:T(8,128)S(1)}) custom-call(s32[4]{0:T(128)S(1)} %add_multiply_fusion.base_ref, s32[128,1]{1,0:T(8,128)S(1)} %copy.23.labels_ref, f32[8,8,128]{2,1,0:T(8,128)S(1)} %all-to-all-done.3.stats, bf16[1,32,128,128]{3,2,1,0:T(8,128)(2,1)S(1)} %bitcast.18, ...), custom_call_target="tpu_custom_call" | custom-call | flops 1024 | bytes 1024 | tf_op jit(solution)/shard_map/grad_logits/pallas_call | solution.py:341
  141.6 3.0 %grad_logits.3 = (bf16[4,128,512]{2,1,0:T(8,128)(2,1)S(1)}, f32[8,128]{1,0:T(8,128)S(1)}) custom-call(s32[4]{0:T(128)S(1)} %add_multiply_fusion.base_ref, s32[128,1]{1,0:T(8,128)S(1)} %copy.23.labels_ref, f32[8,8,128]{2,1,0:T(8,128)S(1)} %all-to-all-done.3.stats, bf16[1,32,128,128]{3,2,1,0:T(8,128)(2,1)S(1)} %bitcast.19, ...), custom_call_target="tpu_custom_call" | custom-call | flops 1024 | bytes 1024 | tf_op jit(solution)/shard_map/grad_logits/pallas_call | solution.py:341
  144.7 9.0 %all_to_all.35 = f32[8,1,128]{2,1,0:T(1,128)S(1)} all-to-all(f32[8,1,128]{2,1,0:T(1,128)S(1)} %broadcast_in_dim.23), channel_id=1, replica_groups=mesh['tok'=4,'vocab'=8] {'vocab'}, dimensions={0} | all-to-all | bytes 8192 | tf_op jit(solution)/shard_map/all_to_all | solution.py:403
  153.6 12.5 %all_to_all.36 = bf16[4,128,512]{2,1,0:T(8,128)(2,1)S(1)} all-to-all(bf16[4,128,512]{2,1,0:T(8,128)(2,1)S(1)} %get-tuple-element.52), channel_id=1, replica_groups=mesh['tok'=4,'vocab'=8] {'tok'}, dimensions={0} | all-to-all | bytes 1048576 | tf_op jit(solution)/shard_map/all_to_all | solution.py:407
  166.1 3.5 %all-to-all-start.5 = ((bf16[4,128,512]{2,1,0:T(8,128)(2,1)}), bf16[4,128,512]{2,1,0:T(8,128)(2,1)S(1)}, u32[]{:S(2)}, u32[]{:S(2)}) async-start(bf16[4,128,512]{2,1,0:T(8,128)(2,1)} %copy-done.16), calls=%async_computation.5 | async-start | bytes 1048576 | tf_op jit(solution)/shard_map/all_to_all | solution.py:407
  170.1 2.3 %copy-done.2 = bf16[4608,512]{1,0:T(8,128)(2,1)S(1)} copy-done((bf16[4608,512]{1,0:T(8,128)(2,1)S(1)}, bf16[4608,512]{1,0:T(8,128)(2,1)}, u32[]{:S(2)}) %copy-start.2) | copy-done | bytes 4718616
  172.4 4.4 %head_product.2.refs_0_ = bf16[4608,1024]{1,0:T(8,128)(2,1)} custom-call(bf16[4608,512]{1,0:T(8,128)(2,1)S(1)} %copy-done.2, bf16[512,512]{1,0:T(8,128)(2,1)S(1)} %bitcast.21), custom_call_target="tpu_custom_call" | custom-call | flops 1024 | bytes 1024 | tf_op jit(solution)/shard_map/head_product/pallas_call | solution.py:365
  176.8 2.3 %copy-done.3 = bf16[4608,512]{1,0:T(8,128)(2,1)S(1)} copy-done((bf16[4608,512]{1,0:T(8,128)(2,1)S(1)}, bf16[4608,512]{1,0:T(8,128)(2,1)}, u32[]{:S(2)}) %copy-start.3) | copy-done | bytes 4718616
  179.2 4.4 %head_product.3 = bf16[4608,1024]{1,0:T(8,128)(2,1)} custom-call(bf16[4608,512]{1,0:T(8,128)(2,1)S(1)} %copy-done.3, bf16[512,512]{1,0:T(8,128)(2,1)S(1)} %bitcast.20, bf16[4608,1024]{1,0:T(8,128)(2,1)} %head_product.2.refs_0_), custom_call_target="tpu_custom_call", output_to_operand_aliasing={{}: (2, {})} | custom-call | flops 1024 | bytes 1024 | tf_op jit(solution)/shard_map/head_product/pallas_call | solution.py:365
  (72 shorter events, 23.2 us)
Async XLA Ops:
  0.6 9.0 %copy-start = (bf16[128,4608]{1,0:T(8,128)(2,1)S(1)}, bf16[128,4608]{1,0:T(8,128)(2,1)}, u32[]{:S(2)}) copy-start(bf16[128,4608]{1,0:T(8,128)(2,1)} %param.7) | copy-start | bytes 3538948
  0.6 32.6 %collective-permute-start.2 = (bf16[32,4,128,128]{3,2,1,0:T(8,128)(2,1)}, bf16[32,4,128,128]{3,2,1,0:T(8,128)(2,1)}, u32[]{:S(2)}, u32[]{:S(2)}) collective-permute-start(bf16[32,4,128,128]{3,2,1,0:T(8,128)(2,1)} %w_own.3), channel_id=1, source_target_pairs={{0,1},{1,0},{2,3},{3,2},{4,5},{5,4},{6,7},{7,6},{8,9},{9,8},{10,11... | collective-permute-start | bytes 12582920 | tf_op jit(solution)/shard_map/ppermute | solution.py:399
  1.2 1.2 copy-start.7
  3.6 11.7 %all-to-all-start = ((f32[8,8,128]{2,1,0:T(8,128)}), f32[8,8,128]{2,1,0:T(8,128)S(1)}, u32[]{:S(2)}, u32[]{:S(2)}) async-start(f32[8,8,128]{2,1,0:T(8,128)} %teacher_stats.1), calls=%async_computation | async-start | bytes 65536 | tf_op jit(solution)/shard_map/all_to_all | solution.py:403
  15.4 1.6 copy-start.17
  17.0 33.3 %all-to-all-start.1 = ((bf16[4,64,4608]{2,1,0:T(8,128)(2,1)}), bf16[4,64,4608]{2,1,0:T(8,128)(2,1)S(1)}, u32[]{:S(2)}, u32[]{:S(2)}) async-start(bf16[4,64,4608]{2,1,0:T(8,128)(2,1)} %broadcast_in_dim.18), calls=%async_computation.1 | async-start | bytes 4718592 | tf_op jit(solution)/shard_map/all_to_all | solution.py:407
  20.7 8.1 %collective-permute-start.1 = (bf16[128,4096]{1,0:T(8,128)(2,1)}, bf16[128,4096]{1,0:T(8,128)(2,1)}, u32[]{:S(2)}, u32[]{:S(2)}) collective-permute-start(bf16[128,4096]{1,0:T(8,128)(2,1)} %x_own.1), channel_id=1, source_target_pairs={{0,1},{1,0},{2,3},{3,2},{4,5},{5,4},{6,7},{7,6},{8,9},{9,8},{10,11... | collective-permute-start | bytes 3145736 | tf_op jit(solution)/shard_map/ppermute | solution.py:399
  21.5 2.0 %copy-start.22 = (s32[32,4]{1,0:T(8,128)}, s32[32,4]{1,0:T(8,128)S(1)}, u32[]{:S(2)}) copy-start(s32[32,4]{1,0:T(8,128)S(1)} %copy.20.own_ref) | copy-start | bytes 1540
  21.5 2.0 %collective-permute-start = (s32[32,4]{1,0:T(8,128)S(1)}, s32[32,4]{1,0:T(8,128)}, u32[]{:S(2)}, u32[]{:S(2)}) collective-permute-start(s32[32,4]{1,0:T(8,128)S(1)} %copy.20.own_ref), channel_id=1, source_target_pairs={{0,1},{1,0},{2,3},{3,2},{4,5},{5,4},{6,7},{7,6},{8,9},{9,8},{10,11... | collective-permute-start | bytes 1544 | tf_op jit(solution)/shard_map/ppermute | solution.py:399
  28.8 4.5 %copy-start.4 = (bf16[32,4,128,128]{3,2,1,0:T(8,128)(2,1)S(1)}, bf16[32,4,128,128]{3,2,1,0:T(8,128)(2,1)}, u32[]{:S(2)}) copy-start(bf16[32,4,128,128]{3,2,1,0:T(8,128)(2,1)} %w_own.3) | copy-start | bytes 12582916
  28.8 1.4 copy-start.8
  31.1 2.2 %copy-start.19 = (s32[4,260]{1,0:T(4,128)S(1)}, s32[4,260]{1,0:T(4,128)}, u32[]{:S(2)}) copy-start(s32[4,260]{1,0:T(4,128)} %get-tuple-element.31.list_ref) | copy-start | bytes 12484
  31.1 2.2 %copy-start.21 = (s32[4]{0:T(128)S(1)}, s32[4]{0:T(128)}, u32[]{:S(2)}) copy-start(s32[4]{0:T(128)} %get-tuple-element.32.count_ref) | copy-start | bytes 52
  41.7 13.1 %copy-start.20 = (s32[2]{0:T(128)S(1)}, s32[2]{0:T(128)}, u32[]{:S(2)}) copy-start(s32[2]{0:T(128)} %pad_add_fusion.spot_ref) | copy-start | bytes 28
  50.2 4.5 %collective-permute-start.4 = (bf16[256,4608]{1,0:T(8,128)(2,1)S(1)}, bf16[256,4608]{1,0:T(8,128)(2,1)S(1)}, u32[]{:S(2)}, u32[]{:S(2)}) collective-permute-start(bf16[256,4608]{1,0:T(8,128)(2,1)S(1)} %bitcast.16), channel_id=1, source_target_pairs={{0,1},{1,0},{2,3},{3,2},{4,5},{5,4},{6,7},{7,6},{8,9},{9,8},{10,11... | collective-permute-start | bytes 7077896 | tf_op jit(solution)/shard_map/ppermute | solution.py:399
  50.2 26.1 %collective-permute-start.5 = (bf16[32,128,128]{2,1,0:T(8,128)(2,1)}, bf16[32,128,128]{2,1,0:T(8,128)(2,1)}, u32[]{:S(2)}, u32[]{:S(2)}) collective-permute-start(bf16[32,128,128]{2,1,0:T(8,128)(2,1)} %copy-done.14), channel_id=1, source_target_pairs={{0,2},{1,3},{6,4},{7,5},{8,10},{9,11},{14,12},{15,13},{16,18},{17,... | collective-permute-start | bytes 3145736 | tf_op jit(solution)/shard_map/ppermute | solution.py:411
  62.8 2.2 %copy-start.1 = (bf16[4608,512]{1,0:T(8,128)(2,1)}, bf16[4608,512]{1,0:T(8,128)(2,1)S(1)}, u32[]{:S(2)}) copy-start(bf16[4608,512]{1,0:T(8,128)(2,1)S(1)} %get-tuple-element.56.a_ref) | copy-start | bytes 14155780
  64.9 1.3 copy-start.9
  66.3 29.4 %all-to-all-start.2 = ((f32[4,128,1024]{2,1,0:T(8,128)}), f32[4,128,1024]{2,1,0:T(8,128)S(1)}, u32[]{:S(2)}, u32[]{:S(2)}) async-start(f32[4,128,1024]{2,1,0:T(8,128)} %copy-done.9), calls=%async_computation.2 | async-start | bytes 4194304 | tf_op jit(solution)/shard_map/all_to_all | solution.py:407
  70.5 30.7 %collective-permute-start.3 = (bf16[32,128,128]{2,1,0:T(8,128)(2,1)}, bf16[32,128,128]{2,1,0:T(8,128)(2,1)}, u32[]{:S(2)}, u32[]{:S(2)}) collective-permute-start(bf16[32,128,128]{2,1,0:T(8,128)(2,1)} %copy-done.12), channel_id=1, source_target_pairs={{0,2},{1,3},{6,4},{7,5},{8,10},{9,11},{14,12},{15,13},{16,18},{17,... | collective-permute-start | bytes 3145736 | tf_op jit(solution)/shard_map/ppermute | solution.py:411
  81.1 25.2 %collective-permute-start.6 = (bf16[32,128,128]{2,1,0:T(8,128)(2,1)}, bf16[32,128,128]{2,1,0:T(8,128)(2,1)}, u32[]{:S(2)}, u32[]{:S(2)}) collective-permute-start(bf16[32,128,128]{2,1,0:T(8,128)(2,1)} %merge.3), channel_id=1, source_target_pairs={{2,4},{3,5},{4,2},{5,3},{10,12},{11,13},{12,10},{13,11},{18,20},{1... | collective-permute-start | bytes 3145736 | tf_op jit(solution)/shard_map/ppermute | solution.py:411
  95.6 5.6 %copy-start.13 = (bf16[32,128,128]{2,1,0:T(8,128)(2,1)S(1)}, bf16[32,128,128]{2,1,0:T(8,128)(2,1)}, u32[]{:S(2)}) copy-start(bf16[32,128,128]{2,1,0:T(8,128)(2,1)} %copy-done.12) | copy-start | bytes 3145732
  95.6 10.7 %copy-start.11 = (bf16[32,128,128]{2,1,0:T(8,128)(2,1)S(1)}, bf16[32,128,128]{2,1,0:T(8,128)(2,1)}, u32[]{:S(2)}) copy-start(bf16[32,128,128]{2,1,0:T(8,128)(2,1)} %copy-done.10) | copy-start | bytes 3145732
  95.6 25.5 %collective-permute-start.7 = (bf16[32,128,128]{2,1,0:T(8,128)(2,1)}, bf16[32,128,128]{2,1,0:T(8,128)(2,1)}, u32[]{:S(2)}, u32[]{:S(2)}) collective-permute-start(bf16[32,128,128]{2,1,0:T(8,128)(2,1)} %copy-done.10), channel_id=1, source_target_pairs={{0,2},{1,3},{6,4},{7,5},{8,10},{9,11},{14,12},{15,13},{16,18},{17,... | collective-permute-start | bytes 3145736 | tf_op jit(solution)/shard_map/ppermute | solution.py:411
  104.6 32.7 %collective-permute-start.8 = (bf16[32,128,128]{2,1,0:T(8,128)(2,1)}, bf16[32,128,128]{2,1,0:T(8,128)(2,1)}, u32[]{:S(2)}, u32[]{:S(2)}) collective-permute-start(bf16[32,128,128]{2,1,0:T(8,128)(2,1)} %merge.4), channel_id=1, source_target_pairs={{2,4},{3,5},{4,2},{5,3},{10,12},{11,13},{12,10},{13,11},{18,20},{1... | collective-permute-start | bytes 3145736 | tf_op jit(solution)/shard_map/ppermute | solution.py:411
  109.8 27.5 %collective-permute-start.9 = (bf16[32,128,128]{2,1,0:T(8,128)(2,1)}, bf16[32,128,128]{2,1,0:T(8,128)(2,1)}, u32[]{:S(2)}, u32[]{:S(2)}) collective-permute-start(bf16[32,128,128]{2,1,0:T(8,128)(2,1)} %merge.5), channel_id=1, source_target_pairs={{2,0},{3,1},{4,6},{5,7},{10,8},{11,9},{12,14},{13,15},{18,16},{19,... | collective-permute-start | bytes 3145736 | tf_op jit(solution)/shard_map/ppermute | solution.py:411
  111.1 26.2 %all-to-all-start.3 = ((f32[8,8,128]{2,1,0:T(8,128)}), f32[8,8,128]{2,1,0:T(8,128)S(1)}, u32[]{:S(2)}, u32[]{:S(2)}) async-start(f32[8,8,128]{2,1,0:T(8,128)} %student_stats.1), calls=%async_computation.3 | async-start | bytes 65536 | tf_op jit(solution)/shard_map/all_to_all | solution.py:403
  137.3 1.2 copy-start.6
  144.6 21.5 %copy-start.16 = (bf16[4,128,512]{2,1,0:T(8,128)(2,1)}, bf16[4,128,512]{2,1,0:T(8,128)(2,1)S(1)}, u32[]{:S(2)}) copy-start(bf16[4,128,512]{2,1,0:T(8,128)(2,1)S(1)} %get-tuple-element.57) | copy-start | bytes 1572868
  166.1 10.7 %all-to-all-start.5 = ((bf16[4,128,512]{2,1,0:T(8,128)(2,1)}), bf16[4,128,512]{2,1,0:T(8,128)(2,1)S(1)}, u32[]{:S(2)}, u32[]{:S(2)}) async-start(bf16[4,128,512]{2,1,0:T(8,128)(2,1)} %copy-done.16), calls=%async_computation.5 | async-start | bytes 1048576 | tf_op jit(solution)/shard_map/all_to_all | solution.py:407
  170.1 2.3 %copy-start.2 = (bf16[4608,512]{1,0:T(8,128)(2,1)S(1)}, bf16[4608,512]{1,0:T(8,128)(2,1)}, u32[]{:S(2)}) copy-start(bf16[4608,512]{1,0:T(8,128)(2,1)} %copy-done.1) | copy-start | bytes 14155780
  176.8 2.3 %copy-start.3 = (bf16[4608,512]{1,0:T(8,128)(2,1)S(1)}, bf16[4608,512]{1,0:T(8,128)(2,1)}, u32[]{:S(2)}) copy-start(bf16[4608,512]{1,0:T(8,128)(2,1)} %copy-done.1) | copy-start | bytes 14155780
  (6 other events, 6.3 us)

commit v2 on v0

--- a/solution.py
+++ b/solution.py
@@ -51,11 +51,10 @@
     return jnp.concatenate(rows + [jnp.zeros((LANES - len(rows), n), F32)], axis=0).T
 
 
-def teacher_kernel(*refs):
-    shards, stat_ref = refs[:-1], refs[-1]
-    rows, cols = shards[0].shape
-    places = [(ref, j) for ref in shards for j in range(0, cols, LANES)]
-    read = lambda place: place[0][:, place[1] : place[1] + LANES].astype(F32)
+def teacher_kernel(x_ref, stat_ref):
+    rows, cols = x_ref.shape
+    places = range(0, cols, LANES)
+    read = lambda place: x_ref[:, place : place + LANES].astype(F32)
     top = jnp.full((rows, LANES), -jnp.inf, F32)
     for place in places:
         top = jnp.maximum(top, read(place))
@@ -66,17 +65,16 @@
     stat_ref[...] = rows_from_columns([top, jnp.sum(total, axis=1, keepdims=True)])
 
 
-def teacher_stats(*shards):
-    size = sum(x.size for x in shards)
+def teacher_stats(x):
     return pl.pallas_call(
         teacher_kernel,
-        in_specs=[VMEM_SPEC] * len(shards),
+        in_specs=[VMEM_SPEC],
         out_specs=VMEM_SPEC,
-        out_shape=jax.ShapeDtypeStruct((8, shards[0].shape[0]), F32),
-        compiler_params=params(40),
+        out_shape=jax.ShapeDtypeStruct((8, x.shape[0]), F32),
+        compiler_params=params(16),
         cost_estimate=COST,
         name="teacher_stats",
-    )(*shards)
+    )(x)
 
 
 def divide(x, n):
@@ -85,12 +83,11 @@
 
 def plan_kernel(spot_ref, own_ref, peer_ref, list_ref, count_ref, *, per, n_vocab, in_line):
     core, z = spot_ref[0], spot_ref[1]
-    pieces, room = list_ref.shape
+    pieces = count_ref.shape[0]
     entries, fan = own_ref.shape
-    for p in range(pieces):
-        count_ref[p] = 0
-
-    def visit(i, carry):
+
+    def visit(i, counts):
+        counts = list(counts)
         for side, ref in enumerate((own_ref, peer_ref)):
             for f in range(fan):
                 block = ref[i, f]
@@ -105,20 +102,19 @@
                     place = jnp.where(divide(owner_z, 2) == divide(z, 2), near, jnp.where(outer, 0, 1))
                 else:
                     place = owner_z
-
-                @pl.when(owner_vocab - owner_z * 2 == core)
-                def _():
-                    n = count_ref[place]
-                    list_ref[place, n] = ((side * entries + i) * fan + f) * SLOT_BASE + slot
-                    count_ref[place] = n + 1
-
-        return carry
-
-    lax.fori_loop(0, entries, visit, 0)
+                place = jnp.where(owner_vocab - owner_z * 2 == core, place, pieces)
+                n = 0
+                for p in range(pieces):
+                    n = jnp.where(place == p, counts[p], n)
+                    counts[p] = counts[p] + jnp.where(place == p, 1, 0)
+                list_ref[place, n] = ((side * entries + i) * fan + f) * SLOT_BASE + slot
+        return tuple(counts)
+
+    counts = lax.fori_loop(0, entries, visit, (jnp.int32(0),) * pieces)
     for p in range(pieces):
-        n = count_ref[p]
+        count_ref[p] = counts[p]
         for k in range(BATCH - 1):
-            list_ref[p, n + k] = SLOT_BASE - 1
+            list_ref[p, counts[p] + k] = SLOT_BASE - 1
 
 
 def plan(spot, own_target, peer_target, pieces, per, n_vocab, in_line):
@@ -127,7 +123,7 @@
         functools.partial(plan_kernel, per=per, n_vocab=n_vocab, in_line=in_line),
         in_specs=[SMEM_SPEC] * 3,
         out_specs=[SMEM_SPEC] * 2,
-        out_shape=[jax.ShapeDtypeStruct((pieces, room), jnp.int32), jax.ShapeDtypeStruct((pieces,), jnp.int32)],
+        out_shape=[jax.ShapeDtypeStruct((pieces + 1, room), jnp.int32), jax.ShapeDtypeStruct((pieces,), jnp.int32)],
         cost_estimate=COST,
         name="entry_lists",
     )(spot, own_target, peer_target)
@@ -208,7 +204,7 @@
     rows = probs.shape[1]
     fan = w_own.shape[1]
     whole = lambda shape: pl.BlockSpec(shape, lambda s: (0,) * len(shape))
-    out = jax.ShapeDtypeStruct((steps * slots, rows, LANES), BF16)
+    out = pltpu.HBM((steps * slots, rows, LANES), BF16)
     return pl.pallas_call(
         functools.partial(sums_kernel, first=first, fan=fan),
         grid=(steps,),
@@ -258,7 +254,7 @@
         + [pl.BlockSpec((depth, tile), lambda i: (0, i))],
         out_specs=[pl.BlockSpec((n_tok, rows, tile), lambda i: (0, 0, i))]
         + [pl.BlockSpec((depth * tile // cols, every), lambda i: (i, 0))],
-        out_shape=[jax.ShapeDtypeStruct((n_tok, rows, cols), F32), jax.ShapeDtypeStruct((depth, every), BF16)],
+        out_shape=[pltpu.HBM((n_tok, rows, cols), F32), pltpu.HBM((depth, every), BF16)],
         scratch_shapes=[pltpu.VMEM((every, depth), BF16)],
         compiler_params=params(40),
         cost_estimate=COST,
@@ -299,9 +295,9 @@
     )(base, label_column, mass, logits)
 
 
-def grad_kernel(base_ref, labels_ref, *refs, n_stats, n_sums):
+def grad_kernel(tok_ref, base_ref, labels_ref, *refs, n_stats, n_sums):
     stats, sums = refs[:n_stats], refs[n_stats : n_stats + n_sums]
-    logits_ref, grad_ref, loss_ref, columns, inner = refs[n_stats + n_sums :]
+    logits_ref, *grads, loss_ref, columns, inner = refs[n_stats + n_sums :]
     step = pl.program_id(0)
     _, rows, cols = logits_ref.shape
 
@@ -319,61 +315,85 @@
 
     lane = lax.broadcasted_iota(jnp.int32, (rows, LANES), 1)
     lift, log_total = columns[:, 0:1], columns[:, 1:2]
-    label = labels_ref[...] - base_ref[step]
-    running = inner[...]
-    for b in range(cols // LANES):
-        place = slice(b * LANES, (b + 1) * LANES)
-        target = functools.reduce(jnp.add, [ref[z, b].astype(F32) for ref in sums for z in range(ref.shape[0])])
-        score = logits_ref[0, :, place]
-        running = running + target * score
-        hit = jnp.where(lane == label - b * LANES, 1.0, 0.0)
-        grad_ref[0, :, place] = (lift * jnp.exp(score - log_total) - target - hit).astype(BF16)
-    inner[...] = running
+    label = labels_ref[...] - base_ref[token_group(step, tok_ref, len(grads))]
+    for r in range(len(grads)):
+
+        @pl.when(step == r)
+        def _():
+            running = inner[...]
+            for b in range(cols // LANES):
+                place = slice(b * LANES, (b + 1) * LANES)
+                target = functools.reduce(
+                    jnp.add, [ref[z, b].astype(F32) for ref in sums for z in range(ref.shape[0])]
+                )
+                score = logits_ref[0, :, place]
+                running = running + target * score
+                hit = jnp.where(lane == label - b * LANES, 1.0, 0.0)
+                grads[r][:, place] = (lift * jnp.exp(score - log_total) - target - hit).astype(BF16)
+            inner[...] = running
 
     @pl.when(step == pl.num_programs(0) - 1)
     def _():
         loss_ref[1:2, :] = rows_from_columns([jnp.sum(inner[...], axis=1, keepdims=True)])[0:1, :]
 
 
-def grad_logits(base, label_column, stats, sums, logits):
+def token_group(step, tok_ref, n_tok):
+    return tok_ref[0] ^ (n_tok - 1 - step)
+
+
+def grad_logits(tok, base, label_column, stats, sums, logits):
     n_tok, rows, cols = logits.shape
     per = cols // LANES
-    whole = lambda shape: pl.BlockSpec(shape, lambda t: (0,) * len(shape))
-    one = pl.BlockSpec((1, rows, cols), lambda t: (t, 0, 0))
+    whole = lambda shape: pl.BlockSpec(shape, lambda t, tok_ref: (0,) * len(shape))
+    group = lambda t, tok_ref: token_group(t, tok_ref, n_tok)
     return pl.pallas_call(
         functools.partial(grad_kernel, n_stats=len(stats), n_sums=len(sums)),
-        grid=(n_tok,),
-        in_specs=[SMEM_SPEC, whole(label_column.shape)]
-        + [whole(s.shape) for s in stats]
-        + [pl.BlockSpec((s.shape[0], per, rows, LANES), lambda t: (0, t, 0, 0)) for s in sums]
-        + [one],
-        out_specs=[one, whole((8, rows))],
-        out_shape=[jax.ShapeDtypeStruct((n_tok, rows, cols), BF16), jax.ShapeDtypeStruct((8, rows), F32)],
-        scratch_shapes=[pltpu.VMEM((rows, LANES), F32), pltpu.VMEM((rows, LANES), F32)],
+        grid_spec=pltpu.PrefetchScalarGridSpec(
+            num_scalar_prefetch=1,
+            grid=(n_tok,),
+            in_specs=[SMEM_SPEC, whole(label_column.shape)]
+            + [whole(s.shape) for s in stats]
+            + [pl.BlockSpec((s.shape[0], per, rows, LANES), lambda t, r: (0, group(t, r), 0, 0)) for s in sums]
+            + [pl.BlockSpec((1, rows, cols), lambda t, r: (group(t, r), 0, 0))],
+            out_specs=[whole((rows, cols))] * n_tok + [whole((8, rows))],
+            scratch_shapes=[pltpu.VMEM((rows, LANES), F32), pltpu.VMEM((rows, LANES), F32)],
+        ),
+        out_shape=[pltpu.HBM((rows, cols), BF16)] * n_tok + [jax.ShapeDtypeStruct((8, rows), F32)],
         compiler_params=params(24),
         cost_estimate=COST,
         name="grad_logits",
-    )(base, label_column, *stats, *sums, logits)
-
-
-def product_kernel(a_ref, b_ref, o_ref):
+    )(tok, base, label_column, *stats, *sums, logits)
+
+
+def product_kernel(tok_ref, a_ref, *refs):
+    pieces, o_ref, b_ref = refs[:-2], refs[-2], refs[-1]
+    rows = pieces[0].shape[0]
+
+    @pl.when(pl.program_id(0) == 0)
+    def _():
+        for r, piece in enumerate(pieces):
+            start = pl.multiple_of(token_group(r, tok_ref, len(pieces)) * rows, rows)
+            b_ref[pl.ds(start, rows), :] = piece[...]
+
     o_ref[...] = jnp.dot(a_ref[...], b_ref[...], preferred_element_type=F32).astype(o_ref.dtype)
 
 
-def head_product(a, b):
+def head_product(tok, a, pieces):
     m, k = a.shape
-    n = b.shape[1]
+    rows, n = pieces[0].shape
     tile = m // 4
     return pl.pallas_call(
         product_kernel,
         grid=(m // tile,),
-        in_specs=[pl.BlockSpec((tile, k), lambda i: (i, 0)), pl.BlockSpec((k, n), lambda i: (0, 0))],
+        in_specs=[SMEM_SPEC, pl.BlockSpec((tile, k), lambda i: (i, 0))]
+        + [pl.BlockSpec((rows, n), lambda i: (0, 0))] * len(pieces),
         out_specs=pl.BlockSpec((tile, n), lambda i: (i, 0)),
         out_shape=jax.ShapeDtypeStruct((m, n), BF16),
+        scratch_shapes=[pltpu.VMEM((k, n), BF16)],
         compiler_params=params(32),
         cost_estimate=COST,
         name="head_product",
-    )(a, b)
+    )(tok, pltpu.with_memory_space_constraint(a, pltpu.HBM), *pieces)
 
 
 def swap(x, axis, mask):
@@ -394,12 +414,12 @@
     return chips + [swap(chip, "vocab", 1) for chip in chips]
 
 
+def plus(a, b):
+    return (a.astype(F32) + b.astype(F32)).astype(BF16)
+
+
 def exchange_tok(x):
     return lax.all_to_all(x, "tok", split_axis=0, concat_axis=0, tiled=True)
-
-
-def plus(a, b):
-    return (a.astype(F32) + b.astype(F32)).astype(BF16)
 
 
 def send(x, hops):
@@ -420,27 +440,31 @@
     slots = n_tok * per
     in_line = n_z == 4
 
-    half = lax.dynamic_slice_in_dim(hidden, spot[0] * (rows // 2), rows // 2)
-    near = exchange_tok(jnp.broadcast_to(half, (n_tok,) + half.shape)).reshape(n_tok * (rows // 2), -1)
     peer_logits = swap(teacher_logits, "vocab", 1)
     peer_target = swap(map_target, "vocab", 1)
     peer_weight = swap(map_weight, "vocab", 1)
-    totals = gather_cores(teacher_stats(teacher_logits))
+    teacher = teacher_stats(teacher_logits)
+    totals = gather_cores(teacher)
+    half = lax.dynamic_slice_in_dim(hidden, spot[0] * (rows // 2), rows // 2)
+    half, teacher = lax.optimization_barrier((half, teacher))
+    near = exchange_tok(jnp.broadcast_to(half, (n_tok,) + half.shape)).reshape(n_tok * (rows // 2), -1)
     lists, counts = plan(spot, map_target, peer_target, n_z, per, n_vocab, in_line)
     probs = teacher_probs(teacher_logits, peer_logits, totals)
 
-    sums_args = (lists, counts, probs, map_weight, peer_weight)
     if in_line:
         inward, across, outward = [(0, 1), (3, 2)], [(1, 2), (2, 1)], [(1, 0), (2, 3)]
-        far_outer, mass_a = chip_sums(*sums_args, 0, 1, 1, slots)
+        far_outer, far_inner, mass_a = chip_sums(lists, counts, probs, map_weight, peer_weight, 0, 2, 1, slots)
         first = send(far_outer, inward)
+        second = send(far_inner, inward)
         probs, mass_a = lax.optimization_barrier((probs, mass_a))
-        far_inner, beside, own, mass_b = chip_sums(lists, counts, probs, map_weight, peer_weight, 1, 3, 1, slots)
-        mass = mass_a + mass_b
-        second = send(far_inner, inward)
-        third = send(beside, inward)
+        beside, own, mass_b = chip_sums(lists, counts, probs, map_weight, peer_weight, 2, 2, 1, slots)
+        first, mass = lax.optimization_barrier((first, mass_a + mass_b))
+        merged = plus(far_outer, first)
+        crossed_outer = send(merged, across)
+        waited, near, after = lax.optimization_barrier((beside, near, merged))
+        third = send(waited, inward)
     else:
-        sums, mass = chip_sums(*sums_args, 0, 1, n_z, slots)
+        sums, mass = chip_sums(lists, counts, probs, map_weight, peer_weight, 0, 1, n_z, slots)
         lines = [[2 * z + c for z in range(n_z)] for c in range(2)]
         sums = lax.all_to_all(
             sums.reshape(n_z, slots, rows, block),
@@ -451,31 +475,33 @@
             tiled=True,
         )
         sums = [sums]
-
-    near, mass = lax.optimization_barrier((near, mass))
+        after = mass
+
     far = swap(near, "vocab", 1)
-    scores, turned = student_logits(spot, mass, near, far, new_head, n_tok)
+    scores, turned = student_logits(spot, after, near, far, new_head, n_tok)
     scores = exchange_tok(scores)
+    label_column = lax.dynamic_slice_in_dim(labels, tok * rows, rows).reshape(rows, 1)
+    base = (jnp.arange(n_tok, dtype=jnp.int32) * n_vocab + vocab) * new_cols
     if in_line:
-        first, turned = lax.optimization_barrier((first, turned))
-        merged = plus(far_outer, first)
-        crossed_outer = send(merged, across)
-        second, merged = lax.optimization_barrier((second, merged))
+        second, turned = lax.optimization_barrier((second, turned))
         merged_inner = plus(far_inner, second)
         crossed_inner = send(merged_inner, across)
+        crossed_outer, merged_inner = lax.optimization_barrier((crossed_outer, merged_inner))
         merged_near = plus(beside, crossed_outer)
         arrived = send(merged_near, outward)
-        scores, merged_inner, merged_near = lax.optimization_barrier((scores, merged_inner, merged_near))
+        scores, merged_near = lax.optimization_barrier((scores, merged_near))
         sums = [x[None] for x in (own, third, crossed_inner, arrived)]
-    label_column = lax.dynamic_slice_in_dim(labels, tok * rows, rows).reshape(rows, 1)
-    base = (jnp.arange(n_tok, dtype=jnp.int32) * n_vocab + vocab) * new_cols
     stats = gather_cores(student_stats(base, label_column, mass, scores))
 
-    grads, loss_rows = grad_logits(base, label_column, stats, sums, scores)
-    grads = exchange_tok(grads).reshape(n_tok * rows, new_cols)
-    inner = tree(jnp.add, gather_cores(loss_rows[1]))
-    loss = loss_rows[0] - inner
-    return (loss, head_product(turned, grads))
+    group = tok.astype(jnp.int32).reshape(1)
+    *grads, loss_rows = grad_logits(group, base, label_column, stats, sums, scores)
+    grads = [swap(x, "tok", n_tok - 1 - r) for r, x in enumerate(grads[:-1])] + [grads[-1]]
+    inner = loss_rows[1]
+    mask = 1
+    while mask < n_vocab:
+        inner = inner + swap(inner, "vocab", mask)
+        mask *= 2
+    return (loss_rows[0] - inner, head_product(group, turned, grads))
 
 
 def solution(mesh):

time: 170 us -> 167 us (0.982)
  Pallas kernels: 41 us -> 48.5 us
  local copies, waits for them, and re-layouts: 15.1 us -> 8.02 us
  waiting for transfers between devices: 57.4 us -> 54.8 us
    unnamed x37 -> x29, local copies, waits for them, and re-layouts: 12.6 us -> 5.5 us
    ppermute x25 -> x24, waiting for transfers between devices: 14.2 us -> 19.6 us  [swap(): lax.ppermute(x, axis, [(i, i ^ mask) for i in range(lax.axis_size(axis))])]
    all_to_all x3 -> x2, waiting for transfers between devices: 18.7 us -> 13.6 us  [exchange_tok(): return lax.all_to_all(x, 'tok', split_axis=0, concat_axis=0, tiled=True)]
    all_to_all x3 -> x2, starting transfers between devices: 13.4 us -> 9.46 us  [exchange_tok(): return lax.all_to_all(x, 'tok', split_axis=0, concat_axis=0, tiled=True)]
    ppermute x6, waiting for transfers between devices: 24.4 us -> 21.6 us  [send(): lax.ppermute(x, 'vocab', [(2 * a + c, 2 * b + c) for a, b in hops for c i...]
    ppermute x25 -> x24, starting transfers between devices: 18.4 us -> 20.8 us  [swap(): lax.ppermute(x, axis, [(i, i ^ mask) for i in range(lax.axis_size(axis))])]
    pallas_call x2, Pallas kernels: 7.59 us -> 9.76 us  [the longest x1 9.16 us: head_product(): pl.pallas_call(product_kernel, grid=(m // tile,), in_specs=[SMEM_SPEC, pl...]
  transfers between devices with their start and end apart: 34 -> 32, of which waited for: 13 -> 12; matrix products, arithmetic and copies ran while one was open for 7% -> 7% of each run, Pallas kernels for 18% -> 21%
where the time goes in v2:
time: 167 us; the launch traced here: 165 us
  waiting for transfers between devices  54.8 us (33%)
  Pallas kernels  48.5 us (29%)
  starting transfers between devices  45.1 us (27%)
  other arithmetic  8.18 us (5%)
  local copies, waits for them, and re-layouts  8.02 us (5%)
    ppermute x6, waiting for transfers between devices, send(): lax.ppermute(x, 'vocab', [(2 * a + c, 2 * b + c) for a, b in hops for c i...  21.6 us
    ppermute x24, starting transfers between devices, swap(): lax.ppermute(x, axis, [(i, i ^ mask) for i in range(lax.axis_size(axis))])  20.8 us
    ppermute x24, waiting for transfers between devices, swap(): lax.ppermute(x, axis, [(i, i ^ mask) for i in range(lax.axis_size(axis))])  19.6 us
    ppermute x6, starting transfers between devices, send(): lax.ppermute(x, 'vocab', [(2 * a + c, 2 * b + c) for a, b in hops for c i...  14.8 us
    pallas_call x2, Pallas kernels, chip_sums(): pl.pallas_call(functools.partial(sums_kernel, first=first, fan=fan), grid...  14 us
    all_to_all x2, waiting for transfers between devices, exchange_tok(): return lax.all_to_all(x, 'tok', split_axis=0, concat_axis=0, tiled=True)  13.6 us
    pallas_call x1, Pallas kernels, student_logits(): pl.pallas_call(logits_kernel, grid=(cols // tile,), in_specs=[SMEM_SPEC,...  9.62 us
    all_to_all x2, starting transfers between devices, exchange_tok(): return lax.all_to_all(x, 'tok', split_axis=0, concat_axis=0, tiled=True)  9.46 us
  transfers between devices with their start and end apart: 32, of which 12 were waited for; matrix products, arithmetic and copies ran while one was open for 7% of the time, Pallas kernels for 21%

profile of v2, /device:TPU:0, one launch (start us, length us, event | category | flops | bytes accessed | tf_op | source)
XLA Modules:
  0.0 165.5 jit_solution(6316078668923723409)
XLA Ops:
  3.1 1.6 broadcast_in_dim.15
  4.7 5.3 %all-to-all-start = ((bf16[4,64,4608]{2,1,0:T(8,128)(2,1)}), bf16[4,64,4608]{2,1,0:T(8,128)(2,1)S(1)}, u32[]{:S(2)}, u32[]{:S(2)}) async-start(bf16[4,64,4608]{2,1,0:T(8,128)(2,1)} %broadcast_in_dim.15), calls=%async_computation | async-start | bytes 4718592 | tf_op jit(solution)/shard_map/all_to_all | solution.py:422
  10.0 1.6 collective-permute-start.2
  12.3 2.6 %collective-permute-start.3 = (f32[8,128]{1,0:T(8,128)S(1)}, f32[8,128]{1,0:T(8,128)S(1)}, u32[]{:S(2)}, u32[]{:S(2)}) collective-permute-start(f32[8,128]{1,0:T(8,128)S(1)} %teacher_stats.1.refs_0_), channel_id=1, source_target_pairs={{0,4},{1,5},{2,6},{3,7},{4,0},{5,1},{6,2},{7,3},{8,12},{9,13},{10,... | collective-permute-start | bytes 12296 | tf_op jit(solution)/shard_map/ppermute | solution.py:400
  16.8 3.5 %collective-permute-done.4.refs_3_ = f32[8,128]{1,0:T(8,128)S(1)} collective-permute-done((f32[8,128]{1,0:T(8,128)S(1)}, f32[8,128]{1,0:T(8,128)S(1)}, u32[]{:S(2)}, u32[]{:S(2)}) %collective-permute-start.4) | collective-permute-done | bytes 4128 | tf_op jit(solution)/shard_map/ppermute | solution.py:400
  21.4 6.7 %entry_lists.1 = (s32[5,260]{1,0:T(8,128)}, s32[4]{0:T(128)}) custom-call(s32[2]{0:T(128)} %pad_add_fusion.spot_ref, s32[32,4]{1,0:T(8,128)} %copy.9.own_ref, s32[32,4]{1,0:T(8,128)} %copy-done.12), custom_call_target="tpu_custom_call" | custom-call | flops 1024 | bytes 1024 | tf_op jit(solution)/shard_map/entry_lists/pallas_call | solution.py:122
  29.5 2.3 %teacher_probs.1.probs = bf16[64,128,128]{2,1,0:T(8,128)(2,1)S(1)} custom-call(bf16[128,4096]{1,0:T(8,128)(2,1)S(1)} %copy-done.4, bf16[128,4096]{1,0:T(8,128)(2,1)} %collective-permute-done.1.x_peer, f32[8,128]{1,0:T(8,128)S(1)} %teacher_stats.1.refs_0_, f32[8,128]{1,0:T(8,128)S(1)} %collective-permute-done.2.refs_1_, ...), custom_call_target="tpu_custom_call" | custom-call | flops 1024 | bytes 1024 | tf_op jit(solution)/shard_map/teacher_probs/pallas_call | solution.py:192
  31.9 6.2 %chip_sums.2 = (bf16[32,128,128]{2,1,0:T(8,128)(2,1)}, bf16[32,128,128]{2,1,0:T(8,128)(2,1)}, f32[8,128]{1,0:T(8,128)S(1)}) custom-call(s32[5,260]{1,0:T(8,128)S(1)} %copy-done.7, s32[4]{0:T(128)S(1)} %copy-done.9, bf16[64,128,128]{2,1,0:T(8,128)(2,1)S(1)} %teacher_probs.1.probs, bf16[32,4,128,128]{3,2,1,0:T(8,128)(2,1)S(1)} %copy-done.1, ...), custom_call_target="tpu_custom_call" | custom-call | flops 1024 | bytes 1024 | tf_op jit(solution)/shard_map/chip_sums/pallas_call | solution.py:208
  39.4 7.8 %chip_sums.3 = (bf16[32,128,128]{2,1,0:T(8,128)(2,1)}, bf16[32,128,128]{2,1,0:T(8,128)(2,1)}, f32[8,128]{1,0:T(8,128)S(1)}) custom-call(s32[5,260]{1,0:T(8,128)S(1)} %copy-done.7, s32[4]{0:T(128)S(1)} %copy-done.9, bf16[64,128,128]{2,1,0:T(8,128)(2,1)S(1)} %teacher_probs.1.probs, bf16[32,4,128,128]{3,2,1,0:T(8,128)(2,1)S(1)} %copy-done.1, ...), custom_call_target="tpu_custom_call" | custom-call | flops 1024 | bytes 1024 | tf_op jit(solution)/shard_map/chip_sums/pallas_call | solution.py:208
  47.3 15.0 %collective-permute-done.10 = bf16[32,128,128]{2,1,0:T(8,128)(2,1)S(1)} collective-permute-done((bf16[32,128,128]{2,1,0:T(8,128)(2,1)}, bf16[32,128,128]{2,1,0:T(8,128)(2,1)S(1)}, u32[]{:S(2)}, u32[]{:S(2)}) %collective-permute-start.10) | collective-permute-done | bytes 1048608 | tf_op jit(solution)/shard_map/ppermute | solution.py:426
  64.7 5.0 %collective-permute-start.13 = (bf16[32,128,128]{2,1,0:T(8,128)(2,1)}, bf16[32,128,128]{2,1,0:T(8,128)(2,1)}, u32[]{:S(2)}, u32[]{:S(2)}) collective-permute-start(bf16[32,128,128]{2,1,0:T(8,128)(2,1)} %get-tuple-element.43), channel_id=1, source_target_pairs={{0,2},{1,3},{6,4},{7,5},{8,10},{9,11},{14,12},{15,13},{16,18},{17,... | collective-permute-start | bytes 3145736 | tf_op jit(solution)/shard_map/ppermute | solution.py:426
  69.7 1.7 %collective-permute-start.12 = (bf16[32,128,128]{2,1,0:T(8,128)(2,1)}, bf16[32,128,128]{2,1,0:T(8,128)(2,1)}, u32[]{:S(2)}, u32[]{:S(2)}) collective-permute-start(bf16[32,128,128]{2,1,0:T(8,128)(2,1)} %add_convert_fusion.2.after_ref), channel_id=1, source_target_pairs={{2,4},{3,5},{4,2},{5,3},{10,12},{11,13},{12,10},{13,11},{18,20},{1... | collective-permute-start | bytes 3145736 | tf_op jit(solution)/shard_map/ppermute | solution.py:426
  71.4 3.8 %collective-permute-start.21 = (bf16[32,128,128]{2,1,0:T(8,128)(2,1)}, bf16[32,128,128]{2,1,0:T(8,128)(2,1)}, u32[]{:S(2)}, u32[]{:S(2)}) collective-permute-start(bf16[32,128,128]{2,1,0:T(8,128)(2,1)} %get-tuple-element.49), channel_id=1, source_target_pairs={{0,2},{1,3},{6,4},{7,5},{8,10},{9,11},{14,12},{15,13},{16,18},{17,... | collective-permute-start | bytes 3145736 | tf_op jit(solution)/shard_map/ppermute | solution.py:426
  76.3 9.6 %student_logits.1 = (f32[4,128,1024]{2,1,0:T(8,128)}, bf16[4608,512]{1,0:T(8,128)(2,1)}) custom-call(s32[2]{0:T(128)S(1)} %copy-done.8, bf16[32,128,128]{2,1,0:T(8,128)(2,1)S(1)} %copy-done.2, bf16[256,4608]{1,0:T(8,128)(2,1)S(1)} %bitcast.17, bf16[256,4608]{1,0:T(8,128)(2,1)S(1)} %collective-permute-done.11.far_ref, bf16[4608,1024]{1,0:T(8,128)(2,1)} %head_ref.1), custom_call_target="tpu_custom_call" | custom-call | flops 1024 | bytes 1024 | tf_op jit(solution)/shard_map/student_logits/pallas_call | solution.py:250
  86.0 6.6 %collective-permute-done.13 = bf16[32,128,128]{2,1,0:T(8,128)(2,1)} collective-permute-done((bf16[32,128,128]{2,1,0:T(8,128)(2,1)}, bf16[32,128,128]{2,1,0:T(8,128)(2,1)}, u32[]{:S(2)}, u32[]{:S(2)}) %collective-permute-start.13) | collective-permute-done | bytes 1048608 | tf_op jit(solution)/shard_map/ppermute | solution.py:426
  92.5 4.2 %all-to-all-start.1 = ((f32[4,128,1024]{2,1,0:T(8,128)}), f32[4,128,1024]{2,1,0:T(8,128)S(1)}, u32[]{:S(2)}, u32[]{:S(2)}) async-start(f32[4,128,1024]{2,1,0:T(8,128)} %get-tuple-element.42), calls=%async_computation.1 | async-start | bytes 4194304 | tf_op jit(solution)/shard_map/all_to_all | solution.py:422
  96.7 3.1 %add_convert_fusion.1 = bf16[32,128,128]{2,1,0:T(8,128)(2,1)} fusion(bf16[32,128,128]{2,1,0:T(8,128)(2,1)} %collective-permute-done.13, bf16[32,128,128]{2,1,0:T(8,128)(2,1)} %get-tuple-element.43), kind=kLoop, calls=%fused_computation.1 | loop fusion | flops 2097152 | bytes 3145728 | tf_op jit(solution)/shard_map/convert_element_type | solution.py:418
  99.8 2.6 %add_convert_fusion = bf16[32,128,128]{2,1,0:T(8,128)(2,1)} fusion(bf16[32,128,128]{2,1,0:T(8,128)(2,1)} %collective-permute-done.12, bf16[32,128,128]{2,1,0:T(8,128)(2,1)S(1)} %copy-done.10), kind=kLoop, calls=%fused_computation | loop fusion | flops 2097152 | bytes 3145728 | tf_op jit(solution)/shard_map/convert_element_type | solution.py:418
  103.7 1.7 %collective-permute-start.22 = (bf16[32,128,128]{2,1,0:T(8,128)(2,1)}, bf16[32,128,128]{2,1,0:T(8,128)(2,1)}, u32[]{:S(2)}, u32[]{:S(2)}) collective-permute-start(bf16[32,128,128]{2,1,0:T(8,128)(2,1)} %add_convert_fusion.1), channel_id=1, source_target_pairs={{2,4},{3,5},{4,2},{5,3},{10,12},{11,13},{12,10},{13,11},{18,20},{1... | collective-permute-start | bytes 3145736 | tf_op jit(solution)/shard_map/ppermute | solution.py:426
  106.3 13.6 %all-to-all-done.1.logits_ref.refs_12_ = f32[4,128,1024]{2,1,0:T(8,128)S(1)} async-done(((f32[4,128,1024]{2,1,0:T(8,128)}), f32[4,128,1024]{2,1,0:T(8,128)S(1)}, u32[]{:S(2)}, u32[]{:S(2)}) %all-to-all-start.1) | async-done | bytes 2097184 | tf_op jit(solution)/shard_map/all_to_all | solution.py:422
  119.9 1.4 student_stats.1.refs_0_
  121.3 2.5 %collective-permute-start.14 = (f32[8,128]{1,0:T(8,128)S(1)}, f32[8,128]{1,0:T(8,128)S(1)}, u32[]{:S(2)}, u32[]{:S(2)}) collective-permute-start(f32[8,128]{1,0:T(8,128)S(1)} %student_stats.1.refs_0_), channel_id=1, source_target_pairs={{0,2},{1,3},{2,0},{3,1},{4,6},{5,7},{6,4},{7,5},{8,10},{9,11},{10,... | collective-permute-start | bytes 12296 | tf_op jit(solution)/shard_map/ppermute | solution.py:400
  123.8 2.8 %collective-permute-start.15 = (f32[8,128]{1,0:T(8,128)S(1)}, f32[8,128]{1,0:T(8,128)S(1)}, u32[]{:S(2)}, u32[]{:S(2)}) collective-permute-start(f32[8,128]{1,0:T(8,128)S(1)} %student_stats.1.refs_0_), channel_id=1, source_target_pairs={{0,4},{1,5},{2,6},{3,7},{4,0},{5,1},{6,2},{7,3},{8,12},{9,13},{10,... | collective-permute-start | bytes 12296 | tf_op jit(solution)/shard_map/ppermute | solution.py:400
  126.6 1.4 collective-permute-start.16
  128.5 5.0 %collective-permute-done.15.refs_2_ = f32[8,128]{1,0:T(8,128)S(1)} collective-permute-done((f32[8,128]{1,0:T(8,128)S(1)}, f32[8,128]{1,0:T(8,128)S(1)}, u32[]{:S(2)}, u32[]{:S(2)}) %collective-permute-start.15) | collective-permute-done | bytes 4128 | tf_op jit(solution)/shard_map/ppermute | solution.py:400
  134.9 4.7 %grad_logits.1 = (bf16[128,1024]{1,0:T(8,128)(2,1)}, bf16[128,1024]{1,0:T(8,128)(2,1)}, bf16[128,1024]{1,0:T(8,128)(2,1)}, bf16[128,1024]{1,0:T(8,128)(2,1)}, f32[8,128]{1,0:T(8,128)S(1)}) custom-call(s32[1]{0:T(128)} %bitcast.tok_ref, s32[4]{0:T(128)S(1)} %add_multiply_fusion.base_ref, s32[128,1]{1,0:T(8,128)S(1)} %copy.11.labels_ref, ...), custom_call_target="tpu_custom_call" | custom-call | flops 1024 | bytes 1024 | tf_op jit(solution)/shard_map/grad_logits/pallas_call | solution.py:349
  140.0 2.6 %collective-permute-start.27 = (bf16[128,1024]{1,0:T(8,128)(2,1)}, bf16[128,1024]{1,0:T(8,128)(2,1)S(1)}, u32[]{:S(2)}, u32[]{:S(2)}) collective-permute-start(bf16[128,1024]{1,0:T(8,128)(2,1)} %get-tuple-element.52), channel_id=1, source_target_pairs={{0,24},{8,16},{16,8},{24,0},{1,25},{9,17},{17,9},{25,1},{2,26},{10... | collective-permute-start | bytes 786440 | tf_op jit(solution)/shard_map/ppermute | solution.py:400
  143.7 3.3 %collective-permute-done.25 = f32[128]{0:T(128)S(1)} collective-permute-done((f32[128]{0:T(128)S(1)}, f32[128]{0:T(128)S(1)}, u32[]{:S(2)}, u32[]{:S(2)}) %collective-permute-start.25) | collective-permute-done | bytes 544 | tf_op jit(solution)/shard_map/ppermute | solution.py:400
  147.0 1.4 collective-permute-start.26
  148.4 3.0 %collective-permute-done.26 = f32[128]{0:T(128)S(1)} collective-permute-done((f32[128]{0:T(128)S(1)}, f32[128]{0:T(128)S(1)}, u32[]{:S(2)}, u32[]{:S(2)}) %collective-permute-start.26) | collective-permute-done | bytes 544 | tf_op jit(solution)/shard_map/ppermute | solution.py:400
  152.0 3.1 %collective-permute-done.28.refs_1_ = bf16[128,1024]{1,0:T(8,128)(2,1)S(1)} collective-permute-done((bf16[128,1024]{1,0:T(8,128)(2,1)}, bf16[128,1024]{1,0:T(8,128)(2,1)S(1)}, u32[]{:S(2)}, u32[]{:S(2)}) %collective-permute-start.28) | collective-permute-done | bytes 262176 | tf_op jit(solution)/shard_map/ppermute | solution.py:400
  156.3 9.2 %head_product.1 = bf16[4608,1024]{1,0:T(8,128)(2,1)} custom-call(s32[1]{0:T(128)} %bitcast.tok_ref, bf16[4608,512]{1,0:T(8,128)(2,1)} %get-tuple-element.51.a_ref, bf16[128,1024]{1,0:T(8,128)(2,1)S(1)} %collective-permute-done.27.refs_0_, bf16[128,1024]{1,0:T(8,128)(2,1)S(1)} %collective-permute-done.28.refs_1_, ...), custom_call_target="tpu_custom_call" | custom-call | flops 1024 | bytes 1024 | tf_op jit(solution)/shard_map/head_product/pallas_call | solution.py:385
  (84 shorter events, 19.8 us)
Async XLA Ops:
  0.6 31.2 %collective-permute-start.9 = (bf16[32,4,128,128]{3,2,1,0:T(8,128)(2,1)}, bf16[32,4,128,128]{3,2,1,0:T(8,128)(2,1)}, u32[]{:S(2)}, u32[]{:S(2)}) collective-permute-start(bf16[32,4,128,128]{3,2,1,0:T(8,128)(2,1)} %w_own.3), channel_id=1, source_target_pairs={{0,1},{1,0},{2,3},{3,2},{4,5},{5,4},{6,7},{7,6},{8,9},{9,8},{10,11... | collective-permute-start | bytes 12582920 | tf_op jit(solution)/shard_map/ppermute | solution.py:400
  1.2 27.0 %collective-permute-start.1 = (bf16[128,4096]{1,0:T(8,128)(2,1)}, bf16[128,4096]{1,0:T(8,128)(2,1)}, u32[]{:S(2)}, u32[]{:S(2)}) collective-permute-start(bf16[128,4096]{1,0:T(8,128)(2,1)} %x_own.1), channel_id=1, source_target_pairs={{0,1},{1,0},{2,3},{3,2},{4,5},{5,4},{6,7},{7,6},{8,9},{9,8},{10,11... | collective-permute-start | bytes 3145736 | tf_op jit(solution)/shard_map/ppermute | solution.py:400
  4.7 59.0 %all-to-all-start = ((bf16[4,64,4608]{2,1,0:T(8,128)(2,1)}), bf16[4,64,4608]{2,1,0:T(8,128)(2,1)S(1)}, u32[]{:S(2)}, u32[]{:S(2)}) async-start(bf16[4,64,4608]{2,1,0:T(8,128)(2,1)} %broadcast_in_dim.15), calls=%async_computation | async-start | bytes 4718592 | tf_op jit(solution)/shard_map/all_to_all | solution.py:422
  10.0 6.1 %collective-permute-start.2 = (f32[8,128]{1,0:T(8,128)S(1)}, f32[8,128]{1,0:T(8,128)S(1)}, u32[]{:S(2)}, u32[]{:S(2)}) collective-permute-start(f32[8,128]{1,0:T(8,128)S(1)} %teacher_stats.1.refs_0_), channel_id=1, source_target_pairs={{0,2},{1,3},{2,0},{3,1},{4,6},{5,7},{6,4},{7,5},{8,10},{9,11},{10,... | collective-permute-start | bytes 12296 | tf_op jit(solution)/shard_map/ppermute | solution.py:400
  12.3 2.6 %collective-permute-start = (s32[32,4]{1,0:T(8,128)}, s32[32,4]{1,0:T(8,128)S(1)}, u32[]{:S(2)}, u32[]{:S(2)}) collective-permute-start(s32[32,4]{1,0:T(8,128)} %copy.9.own_ref), channel_id=1, source_target_pairs={{0,1},{1,0},{2,3},{3,2},{4,5},{5,4},{6,7},{7,6},{8,9},{9,8},{10,11... | collective-permute-start | bytes 1544 | tf_op jit(solution)/shard_map/ppermute | solution.py:400
  12.3 4.5 %collective-permute-start.3 = (f32[8,128]{1,0:T(8,128)S(1)}, f32[8,128]{1,0:T(8,128)S(1)}, u32[]{:S(2)}, u32[]{:S(2)}) collective-permute-start(f32[8,128]{1,0:T(8,128)S(1)} %teacher_stats.1.refs_0_), channel_id=1, source_target_pairs={{0,4},{1,5},{2,6},{3,7},{4,0},{5,1},{6,2},{7,3},{8,12},{9,13},{10,... | collective-permute-start | bytes 12296 | tf_op jit(solution)/shard_map/ppermute | solution.py:400
  14.9 5.4 %collective-permute-start.4 = (f32[8,128]{1,0:T(8,128)S(1)}, f32[8,128]{1,0:T(8,128)S(1)}, u32[]{:S(2)}, u32[]{:S(2)}) collective-permute-start(f32[8,128]{1,0:T(8,128)S(1)} %teacher_stats.1.refs_0_), channel_id=1, source_target_pairs={{0,6},{1,7},{2,4},{3,5},{4,2},{5,3},{6,0},{7,1},{8,14},{9,15},{10,... | collective-permute-start | bytes 12296 | tf_op jit(solution)/shard_map/ppermute | solution.py:400
  16.1 4.1 %collective-permute-start.5 = (f32[8,128]{1,0:T(8,128)S(1)}, f32[8,128]{1,0:T(8,128)}, u32[]{:S(2)}, u32[]{:S(2)}) collective-permute-start(f32[8,128]{1,0:T(8,128)S(1)} %teacher_stats.1.refs_0_), channel_id=1, source_target_pairs={{0,1},{1,0},{2,3},{3,2},{4,5},{5,4},{6,7},{7,6},{8,9},{9,8},{10,11... | collective-permute-start | bytes 12296 | tf_op jit(solution)/shard_map/ppermute | solution.py:400
  16.8 11.3 %collective-permute-start.6 = (f32[8,128]{1,0:T(8,128)S(1)}, f32[8,128]{1,0:T(8,128)}, u32[]{:S(2)}, u32[]{:S(2)}) collective-permute-start(f32[8,128]{1,0:T(8,128)S(1)} %collective-permute-done.2.refs_1_), channel_id=1, source_target_pairs={{0,1},{1,0},{2,3},{3,2},{4,5},{5,4},{6,7},{7,6},{8,9},{9,8},{10,11... | collective-permute-start | bytes 12296 | tf_op jit(solution)/shard_map/ppermute | solution.py:400
  20.3 7.8 %collective-permute-start.7 = (f32[8,128]{1,0:T(8,128)S(1)}, f32[8,128]{1,0:T(8,128)}, u32[]{:S(2)}, u32[]{:S(2)}) collective-permute-start(f32[8,128]{1,0:T(8,128)S(1)} %collective-permute-done.3.refs_2_), channel_id=1, source_target_pairs={{0,1},{1,0},{2,3},{3,2},{4,5},{5,4},{6,7},{7,6},{8,9},{9,8},{10,11... | collective-permute-start | bytes 12296 | tf_op jit(solution)/shard_map/ppermute | solution.py:400
  20.3 7.8 %collective-permute-start.8 = (f32[8,128]{1,0:T(8,128)S(1)}, f32[8,128]{1,0:T(8,128)}, u32[]{:S(2)}, u32[]{:S(2)}) collective-permute-start(f32[8,128]{1,0:T(8,128)S(1)} %collective-permute-done.4.refs_3_), channel_id=1, source_target_pairs={{0,1},{1,0},{2,3},{3,2},{4,5},{5,4},{6,7},{7,6},{8,9},{9,8},{10,11... | collective-permute-start | bytes 12296 | tf_op jit(solution)/shard_map/ppermute | solution.py:400
  38.1 24.3 %collective-permute-start.10 = (bf16[32,128,128]{2,1,0:T(8,128)(2,1)}, bf16[32,128,128]{2,1,0:T(8,128)(2,1)S(1)}, u32[]{:S(2)}, u32[]{:S(2)}) collective-permute-start(bf16[32,128,128]{2,1,0:T(8,128)(2,1)} %get-tuple-element.31), channel_id=1, source_target_pairs={{0,2},{1,3},{6,4},{7,5},{8,10},{9,11},{14,12},{15,13},{16,18},{17,... | collective-permute-start | bytes 3145736 | tf_op jit(solution)/shard_map/ppermute | solution.py:426
  63.7 11.4 %collective-permute-start.11 = (bf16[256,4608]{1,0:T(8,128)(2,1)S(1)}, bf16[256,4608]{1,0:T(8,128)(2,1)S(1)}, u32[]{:S(2)}, u32[]{:S(2)}) collective-permute-start(bf16[256,4608]{1,0:T(8,128)(2,1)S(1)} %bitcast.16), channel_id=1, source_target_pairs={{0,1},{1,0},{2,3},{3,2},{4,5},{5,4},{6,7},{7,6},{8,9},{9,8},{10,11... | collective-permute-start | bytes 7077896 | tf_op jit(solution)/shard_map/ppermute | solution.py:400
  64.7 27.8 %collective-permute-start.13 = (bf16[32,128,128]{2,1,0:T(8,128)(2,1)}, bf16[32,128,128]{2,1,0:T(8,128)(2,1)}, u32[]{:S(2)}, u32[]{:S(2)}) collective-permute-start(bf16[32,128,128]{2,1,0:T(8,128)(2,1)} %get-tuple-element.43), channel_id=1, source_target_pairs={{0,2},{1,3},{6,4},{7,5},{8,10},{9,11},{14,12},{15,13},{16,18},{17,... | collective-permute-start | bytes 3145736 | tf_op jit(solution)/shard_map/ppermute | solution.py:426
  69.7 30.1 %collective-permute-start.12 = (bf16[32,128,128]{2,1,0:T(8,128)(2,1)}, bf16[32,128,128]{2,1,0:T(8,128)(2,1)}, u32[]{:S(2)}, u32[]{:S(2)}) collective-permute-start(bf16[32,128,128]{2,1,0:T(8,128)(2,1)} %add_convert_fusion.2.after_ref), channel_id=1, source_target_pairs={{2,4},{3,5},{4,2},{5,3},{10,12},{11,13},{12,10},{13,11},{18,20},{1... | collective-permute-start | bytes 3145736 | tf_op jit(solution)/shard_map/ppermute | solution.py:426
  71.4 55.3 %collective-permute-start.21 = (bf16[32,128,128]{2,1,0:T(8,128)(2,1)}, bf16[32,128,128]{2,1,0:T(8,128)(2,1)}, u32[]{:S(2)}, u32[]{:S(2)}) collective-permute-start(bf16[32,128,128]{2,1,0:T(8,128)(2,1)} %get-tuple-element.49), channel_id=1, source_target_pairs={{0,2},{1,3},{6,4},{7,5},{8,10},{9,11},{14,12},{15,13},{16,18},{17,... | collective-permute-start | bytes 3145736 | tf_op jit(solution)/shard_map/ppermute | solution.py:426
  92.5 27.4 %all-to-all-start.1 = ((f32[4,128,1024]{2,1,0:T(8,128)}), f32[4,128,1024]{2,1,0:T(8,128)S(1)}, u32[]{:S(2)}, u32[]{:S(2)}) async-start(f32[4,128,1024]{2,1,0:T(8,128)} %get-tuple-element.42), calls=%async_computation.1 | async-start | bytes 4194304 | tf_op jit(solution)/shard_map/all_to_all | solution.py:422
  102.4 25.6 %collective-permute-start.23 = (bf16[32,128,128]{2,1,0:T(8,128)(2,1)}, bf16[32,128,128]{2,1,0:T(8,128)(2,1)}, u32[]{:S(2)}, u32[]{:S(2)}) collective-permute-start(bf16[32,128,128]{2,1,0:T(8,128)(2,1)} %add_convert_fusion), channel_id=1, source_target_pairs={{2,0},{3,1},{4,6},{5,7},{10,8},{11,9},{12,14},{13,15},{18,16},{19,... | collective-permute-start | bytes 3145736 | tf_op jit(solution)/shard_map/ppermute | solution.py:426
  103.7 30.3 %collective-permute-start.22 = (bf16[32,128,128]{2,1,0:T(8,128)(2,1)}, bf16[32,128,128]{2,1,0:T(8,128)(2,1)}, u32[]{:S(2)}, u32[]{:S(2)}) collective-permute-start(bf16[32,128,128]{2,1,0:T(8,128)(2,1)} %add_convert_fusion.1), channel_id=1, source_target_pairs={{2,4},{3,5},{4,2},{5,3},{10,12},{11,13},{12,10},{13,11},{18,20},{1... | collective-permute-start | bytes 3145736 | tf_op jit(solution)/shard_map/ppermute | solution.py:426
  121.3 6.7 %collective-permute-start.14 = (f32[8,128]{1,0:T(8,128)S(1)}, f32[8,128]{1,0:T(8,128)S(1)}, u32[]{:S(2)}, u32[]{:S(2)}) collective-permute-start(f32[8,128]{1,0:T(8,128)S(1)} %student_stats.1.refs_0_), channel_id=1, source_target_pairs={{0,2},{1,3},{2,0},{3,1},{4,6},{5,7},{6,4},{7,5},{8,10},{9,11},{10,... | collective-permute-start | bytes 12296 | tf_op jit(solution)/shard_map/ppermute | solution.py:400
  123.8 9.7 %collective-permute-start.15 = (f32[8,128]{1,0:T(8,128)S(1)}, f32[8,128]{1,0:T(8,128)S(1)}, u32[]{:S(2)}, u32[]{:S(2)}) collective-permute-start(f32[8,128]{1,0:T(8,128)S(1)} %student_stats.1.refs_0_), channel_id=1, source_target_pairs={{0,4},{1,5},{2,6},{3,7},{4,0},{5,1},{6,2},{7,3},{8,12},{9,13},{10,... | collective-permute-start | bytes 12296 | tf_op jit(solution)/shard_map/ppermute | solution.py:400
  126.6 6.9 %collective-permute-start.16 = (f32[8,128]{1,0:T(8,128)S(1)}, f32[8,128]{1,0:T(8,128)S(1)}, u32[]{:S(2)}, u32[]{:S(2)}) collective-permute-start(f32[8,128]{1,0:T(8,128)S(1)} %student_stats.1.refs_0_), channel_id=1, source_target_pairs={{0,6},{1,7},{2,4},{3,5},{4,2},{5,3},{6,0},{7,1},{8,14},{9,15},{10,... | collective-permute-start | bytes 12296 | tf_op jit(solution)/shard_map/ppermute | solution.py:400
  128.0 6.0 %collective-permute-start.17 = (f32[8,128]{1,0:T(8,128)S(1)}, f32[8,128]{1,0:T(8,128)S(1)}, u32[]{:S(2)}, u32[]{:S(2)}) collective-permute-start(f32[8,128]{1,0:T(8,128)S(1)} %student_stats.1.refs_0_), channel_id=1, source_target_pairs={{0,1},{1,0},{2,3},{3,2},{4,5},{5,4},{6,7},{7,6},{8,9},{9,8},{10,11... | collective-permute-start | bytes 12296 | tf_op jit(solution)/shard_map/ppermute | solution.py:400
  128.0 6.0 %collective-permute-start.18 = (f32[8,128]{1,0:T(8,128)S(1)}, f32[8,128]{1,0:T(8,128)S(1)}, u32[]{:S(2)}, u32[]{:S(2)}) collective-permute-start(f32[8,128]{1,0:T(8,128)S(1)} %collective-permute-done.14.refs_1_), channel_id=1, source_target_pairs={{0,1},{1,0},{2,3},{3,2},{4,5},{5,4},{6,7},{7,6},{8,9},{9,8},{10,11... | collective-permute-start | bytes 12296 | tf_op jit(solution)/shard_map/ppermute | solution.py:400
  133.5 1.2 collective-permute-start.19
  133.5 1.3 collective-permute-start.20
  139.6 3.9 %collective-permute-start.24 = (f32[128]{0:T(128)S(1)}, f32[128]{0:T(128)S(1)}, u32[]{:S(2)}, u32[]{:S(2)}) collective-permute-start(f32[128]{0:T(128)S(1)} %slice_bitcast_fusion), channel_id=1, source_target_pairs={{0,1},{1,0},{2,3},{3,2},{4,5},{5,4},{6,7},{7,6},{8,9},{9,8},{10,11... | collective-permute-start | bytes 1544 | tf_op jit(solution)/shard_map/ppermute | solution.py:400
  140.0 12.0 %collective-permute-start.27 = (bf16[128,1024]{1,0:T(8,128)(2,1)}, bf16[128,1024]{1,0:T(8,128)(2,1)S(1)}, u32[]{:S(2)}, u32[]{:S(2)}) collective-permute-start(bf16[128,1024]{1,0:T(8,128)(2,1)} %get-tuple-element.52), channel_id=1, source_target_pairs={{0,24},{8,16},{16,8},{24,0},{1,25},{9,17},{17,9},{25,1},{2,26},{10... | collective-permute-start | bytes 786440 | tf_op jit(solution)/shard_map/ppermute | solution.py:400
  142.6 12.5 %collective-permute-start.28 = (bf16[128,1024]{1,0:T(8,128)(2,1)}, bf16[128,1024]{1,0:T(8,128)(2,1)S(1)}, u32[]{:S(2)}, u32[]{:S(2)}) collective-permute-start(bf16[128,1024]{1,0:T(8,128)(2,1)} %get-tuple-element.53), channel_id=1, source_target_pairs={{0,16},{8,24},{16,0},{24,8},{1,17},{9,25},{17,1},{25,9},{2,18},{10... | collective-permute-start | bytes 786440 | tf_op jit(solution)/shard_map/ppermute | solution.py:400
  143.2 12.2 %collective-permute-start.29 = (bf16[128,1024]{1,0:T(8,128)(2,1)}, bf16[128,1024]{1,0:T(8,128)(2,1)S(1)}, u32[]{:S(2)}, u32[]{:S(2)}) collective-permute-start(bf16[128,1024]{1,0:T(8,128)(2,1)} %get-tuple-element.54), channel_id=1, source_target_pairs={{0,8},{8,0},{16,24},{24,16},{1,9},{9,1},{17,25},{25,17},{2,10},{10... | collective-permute-start | bytes 786440 | tf_op jit(solution)/shard_map/ppermute | solution.py:400
  143.5 3.5 %collective-permute-start.25 = (f32[128]{0:T(128)S(1)}, f32[128]{0:T(128)S(1)}, u32[]{:S(2)}, u32[]{:S(2)}) collective-permute-start(f32[128]{0:T(128)S(1)} %fusion), channel_id=1, source_target_pairs={{0,2},{1,3},{2,0},{3,1},{4,6},{5,7},{6,4},{7,5},{8,10},{9,11},{10,... | collective-permute-start | bytes 1544 | tf_op jit(solution)/shard_map/ppermute | solution.py:400
  147.0 4.4 %collective-permute-start.26 = (f32[128]{0:T(128)S(1)}, f32[128]{0:T(128)S(1)}, u32[]{:S(2)}, u32[]{:S(2)}) collective-permute-start(f32[128]{0:T(128)S(1)} %add.48), channel_id=1, source_target_pairs={{0,4},{1,5},{2,6},{3,7},{4,0},{5,1},{6,2},{7,3},{8,12},{9,13},{10,... | collective-permute-start | bytes 1544 | tf_op jit(solution)/shard_map/ppermute | solution.py:400
  (14 other events, 92.6 us)

commit v3 on v2

--- a/solution.py
+++ b/solution.py
@@ -10,9 +10,10 @@
 F32 = jnp.float32
 BF16 = jnp.bfloat16
 LANES = 128
-BATCH = 4
+BATCH = 8
 COST = pl.CostEstimate(flops=1024, bytes_accessed=1024, transcendentals=0)
-SLOT_BASE = 1024
+SLOT_BITS = 10
+SLOT_BASE = 1 << SLOT_BITS
 SMEM_SPEC = pl.BlockSpec(memory_space=pltpu.SMEM)
 VMEM_SPEC = pl.BlockSpec(memory_space=pltpu.VMEM)
 
@@ -81,52 +82,38 @@
     return lax.shift_right_logical(x, n.bit_length() - 1) if n & (n - 1) == 0 else x // n
 
 
-def plan_kernel(spot_ref, own_ref, peer_ref, list_ref, count_ref, *, per, n_vocab, in_line):
-    core, z = spot_ref[0], spot_ref[1]
-    pieces = count_ref.shape[0]
-    entries, fan = own_ref.shape
-
-    def visit(i, counts):
-        counts = list(counts)
+def plan_kernel(own_ref, peer_ref, list_ref, count_ref):
+    lists = count_ref.shape[0]
+    entries = own_ref.shape[0]
+    for p in range(lists):
+        count_ref[p] = 0
+
+    def visit(i, carry):
         for side, ref in enumerate((own_ref, peer_ref)):
-            for f in range(fan):
-                block = ref[i, f]
-                owner = divide(block, per)
-                owner_tok = divide(owner, n_vocab)
-                owner_vocab = owner - owner_tok * n_vocab
-                owner_z = divide(owner_vocab, 2)
-                slot = owner_tok * per + block - owner * per
-                if in_line:
-                    outer = (owner_z == 0) | (owner_z == 3)
-                    near = jnp.where(owner_z == z, 3, 2)
-                    place = jnp.where(divide(owner_z, 2) == divide(z, 2), near, jnp.where(outer, 0, 1))
-                else:
-                    place = owner_z
-                place = jnp.where(owner_vocab - owner_z * 2 == core, place, pieces)
-                n = 0
-                for p in range(pieces):
-                    n = jnp.where(place == p, counts[p], n)
-                    counts[p] = counts[p] + jnp.where(place == p, 1, 0)
-                list_ref[place, n] = ((side * entries + i) * fan + f) * SLOT_BASE + slot
-        return tuple(counts)
-
-    counts = lax.fori_loop(0, entries, visit, (jnp.int32(0),) * pieces)
-    for p in range(pieces):
-        count_ref[p] = counts[p]
+            code = ref[i]
+            row = lax.shift_right_logical(code, SLOT_BITS)
+            n = count_ref[row]
+            list_ref[row, n] = (side * entries + i) * SLOT_BASE + (code & (SLOT_BASE - 1))
+            count_ref[row] = n + 1
+        return carry
+
+    lax.fori_loop(0, entries, visit, 0, unroll=8)
+    for p in range(lists):
+        n = count_ref[p]
         for k in range(BATCH - 1):
-            list_ref[p, counts[p] + k] = SLOT_BASE - 1
-
-
-def plan(spot, own_target, peer_target, pieces, per, n_vocab, in_line):
-    room = 2 * own_target.size + BATCH
-    return pl.pallas_call(
-        functools.partial(plan_kernel, per=per, n_vocab=n_vocab, in_line=in_line),
-        in_specs=[SMEM_SPEC] * 3,
+            list_ref[p, n + k] = SLOT_BASE - 1
+
+
+def plan(own_code, peer_code, lists):
+    room = 2 * own_code.size + BATCH
+    return pl.pallas_call(
+        plan_kernel,
+        in_specs=[SMEM_SPEC] * 2,
         out_specs=[SMEM_SPEC] * 2,
-        out_shape=[jax.ShapeDtypeStruct((pieces + 1, room), jnp.int32), jax.ShapeDtypeStruct((pieces,), jnp.int32)],
+        out_shape=[jax.ShapeDtypeStruct((lists, room), jnp.int32), jax.ShapeDtypeStruct((lists,), jnp.int32)],
         cost_estimate=COST,
         name="entry_lists",
-    )(spot, own_target, peer_target)
+    )(own_code, peer_code)
 
 
 def probs_kernel(x_own, x_peer, *refs):
@@ -141,14 +128,14 @@
             probs[side * blocks + j] = (raised * scale).astype(BF16)
 
 
-def sums_kernel(list_ref, count_ref, probs, w_own, w_peer, *refs, first, fan):
+def sums_kernel(spot_ref, list_ref, count_ref, probs, w_own, w_peer, *refs, first, fan, pieces):
     outs, mass_ref, acc = refs[:-2], refs[-2], refs[-1]
     step = pl.program_id(0)
     slots, rows, _ = outs[0].shape
     side = w_own.shape[0] * fan
     mass = jnp.zeros((rows, LANES), F32)
     for k, out in enumerate(outs):
-        piece = first + k + step
+        piece = spot_ref[0] * pieces + first + k + step
         acc[...] = jnp.zeros_like(acc)
 
         def add(i, carry):
@@ -156,7 +143,7 @@
             for u in range(BATCH):
                 item = list_ref[piece, i * BATCH + u]
                 slot = item & (SLOT_BASE - 1)
-                entry = lax.shift_right_logical(item, SLOT_BASE.bit_length() - 1)
+                entry = lax.shift_right_logical(item, SLOT_BITS)
                 weight = jnp.where(entry < side, 0, 1)
                 parts.append((entry, slot, weight))
             for entry, slot, peer in parts:
@@ -200,22 +187,22 @@
     )(x_own, x_peer, *stats)
 
 
-def chip_sums(lists, counts, probs, w_own, w_peer, first, n_out, steps, slots):
+def chip_sums(spot, lists, counts, probs, w_own, w_peer, first, n_out, steps, slots):
     rows = probs.shape[1]
     fan = w_own.shape[1]
     whole = lambda shape: pl.BlockSpec(shape, lambda s: (0,) * len(shape))
     out = pltpu.HBM((steps * slots, rows, LANES), BF16)
     return pl.pallas_call(
-        functools.partial(sums_kernel, first=first, fan=fan),
+        functools.partial(sums_kernel, first=first, fan=fan, pieces=counts.shape[0] // 2),
         grid=(steps,),
-        in_specs=[SMEM_SPEC] * 2 + [VMEM_SPEC] * 3,
+        in_specs=[SMEM_SPEC] * 3 + [VMEM_SPEC] * 3,
         out_specs=[pl.BlockSpec((slots, rows, LANES), lambda s: (s, 0, 0))] * n_out + [whole((8, rows))],
         out_shape=[out] * n_out + [jax.ShapeDtypeStruct((8, rows), F32)],
         scratch_shapes=[pltpu.VMEM((slots + 1, rows, LANES), F32)],
         compiler_params=params(32),
         cost_estimate=COST,
         name="chip_sums",
-    )(lists, counts, probs, w_own, w_peer)
+    )(spot, lists, counts, probs, w_own, w_peer)
 
 
 def logits_kernel(spot_ref, after_ref, near_ref, far_ref, head_ref, *refs):
@@ -259,7 +246,7 @@
         compiler_params=params(40),
         cost_estimate=COST,
         name="student_logits",
-    )(spot, after, near, far, head)
+    )(spot, after, near, far, pltpu.with_memory_space_constraint(head, pltpu.HBM))
 
 
 def student_kernel(base_ref, labels_ref, mass_ref, logits_ref, stat_ref):
@@ -295,23 +282,39 @@
     )(base, label_column, mass, logits)
 
 
-def grad_kernel(tok_ref, base_ref, labels_ref, *refs, n_stats, n_sums):
-    stats, sums = refs[:n_stats], refs[n_stats : n_stats + n_sums]
-    logits_ref, *grads, loss_ref, columns, inner = refs[n_stats + n_sums :]
+def totals_kernel(*refs):
+    stats, (columns, loss_ref) = refs[:-2], refs[-2:]
+    parts = split_rows(stats)
+    mass = tree(jnp.add, [r[0] for r in parts])
+    top, total = total_at(parts, 1, 2)
+    log_total = top + jnp.log(total)
+    label_logit = tree(jnp.add, [r[3] for r in parts])
+    columns[...] = columns_from_rows([mass + 1.0, log_total])
+    loss_ref[...] = mass * log_total + log_total - label_logit
+
+
+def token_totals(stats):
+    rows = stats[0].shape[1]
+    return pl.pallas_call(
+        totals_kernel,
+        in_specs=[VMEM_SPEC] * len(stats),
+        out_specs=[VMEM_SPEC] * 2,
+        out_shape=[jax.ShapeDtypeStruct((rows, LANES), F32), jax.ShapeDtypeStruct((1, rows), F32)],
+        compiler_params=params(16),
+        cost_estimate=COST,
+        name="token_totals",
+    )(*stats)
+
+
+def grad_kernel(tok_ref, base_ref, labels_ref, columns, *refs, n_sums):
+    sums = refs[:n_sums]
+    logits_ref, *grads, inner_ref, inner = refs[n_sums:]
     step = pl.program_id(0)
     _, rows, cols = logits_ref.shape
 
     @pl.when(step == 0)
     def _():
-        parts = split_rows(stats)
-        mass = tree(jnp.add, [r[0] for r in parts])
-        top, total = total_at(parts, 1, 2)
-        log_total = top + jnp.log(total)
-        label_logit = tree(jnp.add, [r[3] for r in parts])
-        columns[...] = columns_from_rows([mass + 1.0, log_total])
         inner[...] = jnp.zeros_like(inner)
-        loss_ref[...] = jnp.zeros_like(loss_ref)
-        loss_ref[0:1, :] = mass * log_total + log_total - label_logit
 
     lane = lax.broadcasted_iota(jnp.int32, (rows, LANES), 1)
     lift, log_total = columns[:, 0:1], columns[:, 1:2]
@@ -334,35 +337,34 @@
 
     @pl.when(step == pl.num_programs(0) - 1)
     def _():
-        loss_ref[1:2, :] = rows_from_columns([jnp.sum(inner[...], axis=1, keepdims=True)])[0:1, :]
+        inner_ref[...] = rows_from_columns([jnp.sum(inner[...], axis=1, keepdims=True)])[0:1, :]
 
 
 def token_group(step, tok_ref, n_tok):
     return tok_ref[0] ^ (n_tok - 1 - step)
 
 
-def grad_logits(tok, base, label_column, stats, sums, logits):
+def grad_logits(tok, base, label_column, columns, sums, logits):
     n_tok, rows, cols = logits.shape
     per = cols // LANES
     whole = lambda shape: pl.BlockSpec(shape, lambda t, tok_ref: (0,) * len(shape))
     group = lambda t, tok_ref: token_group(t, tok_ref, n_tok)
     return pl.pallas_call(
-        functools.partial(grad_kernel, n_stats=len(stats), n_sums=len(sums)),
+        functools.partial(grad_kernel, n_sums=len(sums)),
         grid_spec=pltpu.PrefetchScalarGridSpec(
             num_scalar_prefetch=1,
             grid=(n_tok,),
-            in_specs=[SMEM_SPEC, whole(label_column.shape)]
-            + [whole(s.shape) for s in stats]
+            in_specs=[SMEM_SPEC, whole(label_column.shape), whole(columns.shape)]
             + [pl.BlockSpec((s.shape[0], per, rows, LANES), lambda t, r: (0, group(t, r), 0, 0)) for s in sums]
             + [pl.BlockSpec((1, rows, cols), lambda t, r: (group(t, r), 0, 0))],
-            out_specs=[whole((rows, cols))] * n_tok + [whole((8, rows))],
-            scratch_shapes=[pltpu.VMEM((rows, LANES), F32), pltpu.VMEM((rows, LANES), F32)],
+            out_specs=[whole((rows, cols))] * n_tok + [whole((1, rows))],
+            scratch_shapes=[pltpu.VMEM((rows, LANES), F32)],
         ),
-        out_shape=[pltpu.HBM((rows, cols), BF16)] * n_tok + [jax.ShapeDtypeStruct((8, rows), F32)],
+        out_shape=[pltpu.HBM((rows, cols), BF16)] * n_tok + [jax.ShapeDtypeStruct((1, rows), F32)],
         compiler_params=params(24),
         cost_estimate=COST,
         name="grad_logits",
-    )(tok, base, label_column, *stats, *sums, logits)
+    )(tok, base, label_column, columns, *sums, logits)
 
 
 def product_kernel(tok_ref, a_ref, *refs):
@@ -440,31 +442,43 @@
     slots = n_tok * per
     in_line = n_z == 4
 
+    owner = map_target // per
+    owner_vocab = owner % n_vocab
+    owner_z = owner_vocab // 2
+    if in_line:
+        z = vocab // 2
+        outer = (owner_z == 0) | (owner_z == n_z - 1)
+        near_place = jnp.where(owner_z == z, 3, 2)
+        place = jnp.where((owner_z // 2) == (z // 2), near_place, jnp.where(outer, 0, 1))
+    else:
+        place = owner_z
+    slot = (owner // n_vocab) * per + map_target % per
+    code = (((owner_vocab % 2) * n_z + place) * SLOT_BASE + slot).astype(jnp.int32).reshape(-1)
+
     peer_logits = swap(teacher_logits, "vocab", 1)
-    peer_target = swap(map_target, "vocab", 1)
+    peer_code = swap(code, "vocab", 1)
     peer_weight = swap(map_weight, "vocab", 1)
     teacher = teacher_stats(teacher_logits)
     totals = gather_cores(teacher)
     half = lax.dynamic_slice_in_dim(hidden, spot[0] * (rows // 2), rows // 2)
     half, teacher = lax.optimization_barrier((half, teacher))
     near = exchange_tok(jnp.broadcast_to(half, (n_tok,) + half.shape)).reshape(n_tok * (rows // 2), -1)
-    lists, counts = plan(spot, map_target, peer_target, n_z, per, n_vocab, in_line)
+    lists, counts = plan(code, peer_code, 2 * n_z)
     probs = teacher_probs(teacher_logits, peer_logits, totals)
 
     if in_line:
         inward, across, outward = [(0, 1), (3, 2)], [(1, 2), (2, 1)], [(1, 0), (2, 3)]
-        far_outer, far_inner, mass_a = chip_sums(lists, counts, probs, map_weight, peer_weight, 0, 2, 1, slots)
+        far_outer, mass_a = chip_sums(spot, lists, counts, probs, map_weight, peer_weight, 0, 1, 1, slots)
         first = send(far_outer, inward)
+        near, mass_a = lax.optimization_barrier((near, mass_a))
+        probs, far_outer = lax.optimization_barrier((probs, far_outer))
+        far_inner, beside, own, mass_b = chip_sums(
+            spot, lists, counts, probs, map_weight, peer_weight, 1, 3, 1, slots
+        )
         second = send(far_inner, inward)
-        probs, mass_a = lax.optimization_barrier((probs, mass_a))
-        beside, own, mass_b = chip_sums(lists, counts, probs, map_weight, peer_weight, 2, 2, 1, slots)
-        first, mass = lax.optimization_barrier((first, mass_a + mass_b))
-        merged = plus(far_outer, first)
-        crossed_outer = send(merged, across)
-        waited, near, after = lax.optimization_barrier((beside, near, merged))
-        third = send(waited, inward)
+        mass = mass_a + mass_b
     else:
-        sums, mass = chip_sums(lists, counts, probs, map_weight, peer_weight, 0, 1, n_z, slots)
+        sums, mass = chip_sums(spot, lists, counts, probs, map_weight, peer_weight, 0, 1, n_z, slots)
         lines = [[2 * z + c for z in range(n_z)] for c in range(2)]
         sums = lax.all_to_all(
             sums.reshape(n_z, slots, rows, block),
@@ -475,33 +489,40 @@
             tiled=True,
         )
         sums = [sums]
-        after = mass
 
     far = swap(near, "vocab", 1)
-    scores, turned = student_logits(spot, after, near, far, new_head, n_tok)
+    scores, turned = student_logits(spot, mass, near, far, new_head, n_tok)
     scores = exchange_tok(scores)
     label_column = lax.dynamic_slice_in_dim(labels, tok * rows, rows).reshape(rows, 1)
     base = (jnp.arange(n_tok, dtype=jnp.int32) * n_vocab + vocab) * new_cols
     if in_line:
-        second, turned = lax.optimization_barrier((second, turned))
+        first, turned = lax.optimization_barrier((first, turned))
+        merged = plus(far_outer, first)
+        crossed_outer = send(merged, across)
+        scores, merged = lax.optimization_barrier((scores, merged))
+        student = student_stats(base, label_column, mass, scores)
+        second, waited, student = lax.optimization_barrier((second, beside, student))
+        third = send(waited, inward)
         merged_inner = plus(far_inner, second)
         crossed_inner = send(merged_inner, across)
         crossed_outer, merged_inner = lax.optimization_barrier((crossed_outer, merged_inner))
         merged_near = plus(beside, crossed_outer)
         arrived = send(merged_near, outward)
-        scores, merged_near = lax.optimization_barrier((scores, merged_near))
+        student, merged_near = lax.optimization_barrier((student, merged_near))
         sums = [x[None] for x in (own, third, crossed_inner, arrived)]
-    stats = gather_cores(student_stats(base, label_column, mass, scores))
+    else:
+        student = student_stats(base, label_column, mass, scores)
+    stats = gather_cores(student)
 
     group = tok.astype(jnp.int32).reshape(1)
-    *grads, loss_rows = grad_logits(group, base, label_column, stats, sums, scores)
+    columns, base_loss = token_totals(stats)
+    *grads, inner = grad_logits(group, base, label_column, columns, sums, scores)
     grads = [swap(x, "tok", n_tok - 1 - r) for r, x in enumerate(grads[:-1])] + [grads[-1]]
-    inner = loss_rows[1]
     mask = 1
     while mask < n_vocab:
         inner = inner + swap(inner, "vocab", mask)
         mask *= 2
-    return (loss_rows[0] - inner, head_product(group, turned, grads))
+    return ((base_loss - inner).reshape(rows), head_product(group, turned, grads))
 
 
 def solution(mesh):

time: 167 us -> 166 us (level)
  Pallas kernels: 48.5 us -> 41.3 us
  waiting for transfers between devices: 54.8 us -> 59.9 us
  local copies, waits for them, and re-layouts: 8.02 us -> 11.1 us
    ppermute x6, waiting for transfers between devices: 21.6 us -> 0.02 us  [send(): lax.ppermute(x, 'vocab', [(2 * a + c, 2 * b + c) for a, b in hops for c i...]
    ppermute x24, waiting for transfers between devices: 19.6 us -> 37.2 us  [swap(): lax.ppermute(x, axis, [(i, i ^ mask) for i in range(lax.axis_size(axis))])]
    all_to_all x2, waiting for transfers between devices: 13.6 us -> 22.7 us  [exchange_tok(): return lax.all_to_all(x, 'tok', split_axis=0, concat_axis=0, tiled=True)]
    pallas_call x4 -> x5, Pallas kernels: 25.4 us -> 18.8 us  [the longest x2 12.4 us: chip_sums(): pl.pallas_call(functools.partial(sums_kernel, first=first, fan=fan, piece...]
    unnamed x29 -> x34, local copies, waits for them, and re-layouts: 5.5 us -> 8.44 us
  transfers between devices with their start and end apart: 32 -> 32, of which waited for: 12 -> 13; matrix products, arithmetic and copies ran while one was open for 7% -> 6% of each run, Pallas kernels for 21% -> 18%
where the time goes in v3:
time: 166 us; the launch traced here: 165 us
  waiting for transfers between devices  59.9 us (36%)
  starting transfers between devices  44.5 us (27%)
  Pallas kernels  41.3 us (25%)
  local copies, waits for them, and re-layouts  11.1 us (7%)
  other arithmetic  6.9 us (4%)
    ppermute x24, waiting for transfers between devices, swap(): lax.ppermute(x, axis, [(i, i ^ mask) for i in range(lax.axis_size(axis))])  37.2 us
    all_to_all x2, waiting for transfers between devices, exchange_tok(): return lax.all_to_all(x, 'tok', split_axis=0, concat_axis=0, tiled=True)  22.7 us
    ppermute x24, starting transfers between devices, swap(): lax.ppermute(x, axis, [(i, i ^ mask) for i in range(lax.axis_size(axis))])  20.3 us
    ppermute x6, starting transfers between devices, send(): lax.ppermute(x, 'vocab', [(2 * a + c, 2 * b + c) for a, b in hops for c i...  15.7 us
    pallas_call x2, Pallas kernels, chip_sums(): pl.pallas_call(functools.partial(sums_kernel, first=first, fan=fan, piece...  12.4 us
    pallas_call x1, Pallas kernels, student_logits(): pl.pallas_call(logits_kernel, grid=(cols // tile,), in_specs=[SMEM_SPEC,...  10.4 us
    pallas_call x1, Pallas kernels, head_product(): pl.pallas_call(product_kernel, grid=(m // tile,), in_specs=[SMEM_SPEC, pl...  9.17 us
    all_to_all x2, starting transfers between devices, exchange_tok(): return lax.all_to_all(x, 'tok', split_axis=0, concat_axis=0, tiled=True)  8.55 us
  transfers between devices with their start and end apart: 32, of which 13 were waited for; matrix products, arithmetic and copies ran while one was open for 6% of the time, Pallas kernels for 18%

profile of v3, /device:TPU:0, one launch (start us, length us, event | category | flops | bytes accessed | tf_op | source)
XLA Modules:
  0.0 164.6 jit_solution(7028287928183296620)
XLA Ops:
  3.1 1.6 broadcast_in_dim.21
  4.7 4.9 %all-to-all-start = ((bf16[4,64,4608]{2,1,0:T(8,128)(2,1)}), bf16[4,64,4608]{2,1,0:T(8,128)(2,1)}, u32[]{:S(2)}, u32[]{:S(2)}) async-start(bf16[4,64,4608]{2,1,0:T(8,128)(2,1)} %broadcast_in_dim.21), calls=%async_computation | async-start | bytes 4718592 | tf_op jit(solution)/shard_map/all_to_all | solution.py:424
  9.7 2.7 %collective-permute-start.2 = (f32[8,128]{1,0:T(8,128)S(1)}, f32[8,128]{1,0:T(8,128)S(1)}, u32[]{:S(2)}, u32[]{:S(2)}) collective-permute-start(f32[8,128]{1,0:T(8,128)S(1)} %teacher_stats.1.refs_0_), channel_id=1, source_target_pairs={{0,2},{1,3},{2,0},{3,1},{4,6},{5,7},{6,4},{7,5},{8,10},{9,11},{10,... | collective-permute-start | bytes 12296 | tf_op jit(solution)/shard_map/ppermute | solution.py:402
  12.8 2.7 %collective-permute-start.3 = (f32[8,128]{1,0:T(8,128)S(1)}, f32[8,128]{1,0:T(8,128)S(1)}, u32[]{:S(2)}, u32[]{:S(2)}) collective-permute-start(f32[8,128]{1,0:T(8,128)S(1)} %teacher_stats.1.refs_0_), channel_id=1, source_target_pairs={{0,4},{1,5},{2,6},{3,7},{4,0},{5,1},{6,2},{7,3},{8,12},{9,13},{10,... | collective-permute-start | bytes 12296 | tf_op jit(solution)/shard_map/ppermute | solution.py:402
  17.4 3.5 %collective-permute-done.4.refs_3_ = f32[8,128]{1,0:T(8,128)S(1)} collective-permute-done((f32[8,128]{1,0:T(8,128)S(1)}, f32[8,128]{1,0:T(8,128)S(1)}, u32[]{:S(2)}, u32[]{:S(2)}) %collective-permute-start.4) | collective-permute-done | bytes 4128 | tf_op jit(solution)/shard_map/ppermute | solution.py:402
  21.5 3.0 %entry_lists.1 = (s32[8,264]{1,0:T(8,128)}, s32[8]{0:T(128)}) custom-call(s32[128]{0:T(128)} %copy-done.15, s32[128]{0:T(128)} %copy-done.16), custom_call_target="tpu_custom_call" | custom-call | flops 1024 | bytes 1024 | tf_op jit(solution)/shard_map/entry_lists/pallas_call | solution.py:109
  25.6 1.7 %copy-done.5 = bf16[128,4096]{1,0:T(8,128)(2,1)S(1)} copy-done((bf16[128,4096]{1,0:T(8,128)(2,1)S(1)}, bf16[128,4096]{1,0:T(8,128)(2,1)}, u32[]{:S(2)}) %copy-start.5) | copy-done | bytes 1048600
  29.6 4.8 %chip_sums.2 = (bf16[32,128,128]{2,1,0:T(8,128)(2,1)}, f32[8,128]{1,0:T(8,128)S(1)}) custom-call(s32[2]{0:T(128)S(1)} %pad_add_fusion.spot_ref, s32[8,264]{1,0:T(8,128)S(1)} %copy-done.10, s32[8]{0:T(128)S(1)} %copy-done.11, bf16[64,128,128]{2,1,0:T(8,128)(2,1)S(1)} %teacher_probs.1.probs, bf16[32,4,128,128]{3,2,1,0:T(8,128)(2,1)S(1)} %copy-done.1, ...), custom_call_target="tpu_custom_call" | custom-call | flops 1024 | bytes 1024 | tf_op jit(solution)/shard_map/chip_sums/pallas_call | solution.py:195
  34.3 4.4 %all-to-all-done = bf16[4,64,4608]{2,1,0:T(8,128)(2,1)} async-done(((bf16[4,64,4608]{2,1,0:T(8,128)(2,1)}), bf16[4,64,4608]{2,1,0:T(8,128)(2,1)}, u32[]{:S(2)}, u32[]{:S(2)}) %all-to-all-start) | async-done | bytes 2359328 | tf_op jit(solution)/shard_map/all_to_all | solution.py:424
  38.8 4.8 %collective-permute-start.12 = (bf16[32,128,128]{2,1,0:T(8,128)(2,1)}, bf16[32,128,128]{2,1,0:T(8,128)(2,1)}, u32[]{:S(2)}, u32[]{:S(2)}) collective-permute-start(bf16[32,128,128]{2,1,0:T(8,128)(2,1)} %get-tuple-element.44), channel_id=1, source_target_pairs={{0,2},{1,3},{6,4},{7,5},{8,10},{9,11},{14,12},{15,13},{16,18},{17,... | collective-permute-start | bytes 3145736 | tf_op jit(solution)/shard_map/ppermute | solution.py:428
  43.5 2.2 %copy-done.2 = bf16[32,4,128,128]{3,2,1,0:T(8,128)(2,1)S(1)} copy-done((bf16[32,4,128,128]{3,2,1,0:T(8,128)(2,1)S(1)}, bf16[32,4,128,128]{3,2,1,0:T(8,128)(2,1)}, u32[]{:S(2)}) %copy-start.2) | copy-done | bytes 4194328
  45.7 7.6 %chip_sums.3 = (bf16[32,128,128]{2,1,0:T(8,128)(2,1)}, bf16[32,128,128]{2,1,0:T(8,128)(2,1)}, bf16[32,128,128]{2,1,0:T(8,128)(2,1)}, f32[8,128]{1,0:T(8,128)S(1)}) custom-call(s32[2]{0:T(128)S(1)} %pad_add_fusion.spot_ref, s32[8,264]{1,0:T(8,128)S(1)} %copy-done.10, s32[8]{0:T(128)S(1)} %copy-done.11, bf16[64,128,128]{2,1,0:T(8,128)(2,1)S(1)} %teacher_probs.1.probs, ...), custom_call_target="tpu_custom_call" | custom-call | flops 1024 | bytes 1024 | tf_op jit(solution)/shard_map/chip_sums/pallas_call | solution.py:195
  53.4 10.4 %student_logits.1 = (f32[4,128,1024]{2,1,0:T(8,128)}, bf16[4608,512]{1,0:T(8,128)(2,1)}) custom-call(s32[2]{0:T(128)S(1)} %pad_add_fusion.spot_ref, f32[8,128]{1,0:T(8,128)S(1)} %add.77.after_ref.mass_ref, bf16[256,4608]{1,0:T(8,128)(2,1)} %bitcast.3.near_ref, bf16[256,4608]{1,0:T(8,128)(2,1)S(1)} %collective-permute-done.11.far_ref, bf16[4608,1024]{1,0:T(8,128)(2,1)} %head_ref.1), custom_call_target="tpu_custom_call" | custom-call | flops 1024 | bytes 1024 | tf_op jit(solution)/shard_map/student_logits/pallas_call | solution.py:237
  63.7 3.6 %all-to-all-start.1 = ((f32[4,128,1024]{2,1,0:T(8,128)}), f32[4,128,1024]{2,1,0:T(8,128)S(1)}, u32[]{:S(2)}, u32[]{:S(2)}) async-start(f32[4,128,1024]{2,1,0:T(8,128)} %get-tuple-element.43), calls=%async_computation.1 | async-start | bytes 4194304 | tf_op jit(solution)/shard_map/all_to_all | solution.py:424
  67.3 2.3 %collective-permute-start.10 = (bf16[32,128,128]{2,1,0:T(8,128)(2,1)}, bf16[32,128,128]{2,1,0:T(8,128)(2,1)}, u32[]{:S(2)}, u32[]{:S(2)}) collective-permute-start(bf16[32,128,128]{2,1,0:T(8,128)(2,1)} %get-tuple-element.36), channel_id=1, source_target_pairs={{0,2},{1,3},{6,4},{7,5},{8,10},{9,11},{14,12},{15,13},{16,18},{17,... | collective-permute-start | bytes 3145736 | tf_op jit(solution)/shard_map/ppermute | solution.py:428
  69.6 3.0 %add_convert_fusion.2 = bf16[32,128,128]{2,1,0:T(8,128)(2,1)} fusion(bf16[32,128,128]{2,1,0:T(8,128)(2,1)} %collective-permute-done.12, bf16[32,128,128]{2,1,0:T(8,128)(2,1)} %get-tuple-element.44), kind=kLoop, calls=%fused_computation.2 | loop fusion | flops 2097152 | bytes 3145728 | tf_op jit(solution)/shard_map/convert_element_type | solution.py:420
  72.6 1.6 collective-permute-start.13
  75.1 18.2 %all-to-all-done.1.logits_ref.refs_4_ = f32[4,128,1024]{2,1,0:T(8,128)S(1)} async-done(((f32[4,128,1024]{2,1,0:T(8,128)}), f32[4,128,1024]{2,1,0:T(8,128)S(1)}, u32[]{:S(2)}, u32[]{:S(2)}) %all-to-all-start.1) | async-done | bytes 2097184 | tf_op jit(solution)/shard_map/all_to_all | solution.py:424
  94.7 1.7 %add_convert_fusion.1 = bf16[32,128,128]{2,1,0:T(8,128)(2,1)S(1)} fusion(bf16[32,128,128]{2,1,0:T(8,128)(2,1)} %collective-permute-done.10, bf16[32,128,128]{2,1,0:T(8,128)(2,1)S(1)} %copy-done.13), kind=kLoop, calls=%fused_computation.1 | loop fusion | flops 2097152 | bytes 3145728 | tf_op jit(solution)/shard_map/convert_element_type | solution.py:420
  97.3 1.6 add_convert_fusion
  100.2 4.9 %collective-permute-start.21 = (bf16[32,128,128]{2,1,0:T(8,128)(2,1)S(1)}, bf16[32,128,128]{2,1,0:T(8,128)(2,1)S(1)}, u32[]{:S(2)}, u32[]{:S(2)}) collective-permute-start(bf16[32,128,128]{2,1,0:T(8,128)(2,1)S(1)} %copy-done.12), channel_id=1, source_target_pairs={{0,2},{1,3},{6,4},{7,5},{8,10},{9,11},{14,12},{15,13},{16,18},{17,... | collective-permute-start | bytes 3145736 | tf_op jit(solution)/shard_map/ppermute | solution.py:428
  105.2 3.2 %collective-permute-start.15 = (f32[8,128]{1,0:T(8,128)S(1)}, f32[8,128]{1,0:T(8,128)S(1)}, u32[]{:S(2)}, u32[]{:S(2)}) collective-permute-start(f32[8,128]{1,0:T(8,128)S(1)} %student_stats.1.refs_0_), channel_id=1, source_target_pairs={{0,4},{1,5},{2,6},{3,7},{4,0},{5,1},{6,2},{7,3},{8,12},{9,13},{10,... | collective-permute-start | bytes 12296 | tf_op jit(solution)/shard_map/ppermute | solution.py:402
  108.4 19.2 %collective-permute-done.14.refs_1_ = f32[8,128]{1,0:T(8,128)S(1)} collective-permute-done((f32[8,128]{1,0:T(8,128)S(1)}, f32[8,128]{1,0:T(8,128)S(1)}, u32[]{:S(2)}, u32[]{:S(2)}) %collective-permute-start.14) | collective-permute-done | bytes 4128 | tf_op jit(solution)/shard_map/ppermute | solution.py:402
  127.7 2.4 %collective-permute-start.16 = (f32[8,128]{1,0:T(8,128)S(1)}, f32[8,128]{1,0:T(8,128)S(1)}, u32[]{:S(2)}, u32[]{:S(2)}) collective-permute-start(f32[8,128]{1,0:T(8,128)S(1)} %student_stats.1.refs_0_), channel_id=1, source_target_pairs={{0,6},{1,7},{2,4},{3,5},{4,2},{5,3},{6,0},{7,1},{8,14},{9,15},{10,... | collective-permute-start | bytes 12296 | tf_op jit(solution)/shard_map/ppermute | solution.py:402
  130.1 3.0 %collective-permute-done.16.refs_3_ = f32[8,128]{1,0:T(8,128)S(1)} collective-permute-done((f32[8,128]{1,0:T(8,128)S(1)}, f32[8,128]{1,0:T(8,128)S(1)}, u32[]{:S(2)}, u32[]{:S(2)}) %collective-permute-start.16) | collective-permute-done | bytes 4128 | tf_op jit(solution)/shard_map/ppermute | solution.py:402
  135.6 3.3 %grad_logits.1 = (bf16[128,1024]{1,0:T(8,128)(2,1)}, bf16[128,1024]{1,0:T(8,128)(2,1)}, bf16[128,1024]{1,0:T(8,128)(2,1)}, bf16[128,1024]{1,0:T(8,128)(2,1)}, f32[1,128]{1,0:T(1,128)S(1)}) custom-call(s32[1]{0:T(128)} %bitcast.4.tok_ref, s32[4]{0:T(128)S(1)} %add_multiply_fusion.base_ref, s32[128,1]{1,0:T(8,128)S(1)} %copy.12.labels_ref, ...), custom_call_target="tpu_custom_call" | custom-call | flops 1024 | bytes 1024 | tf_op jit(solution)/shard_map/grad_logits/pallas_call | solution.py:352
  138.9 2.9 %collective-permute-start.27 = (bf16[128,1024]{1,0:T(8,128)(2,1)}, bf16[128,1024]{1,0:T(8,128)(2,1)S(1)}, u32[]{:S(2)}, u32[]{:S(2)}) collective-permute-start(bf16[128,1024]{1,0:T(8,128)(2,1)} %get-tuple-element.58), channel_id=1, source_target_pairs={{0,24},{8,16},{16,8},{24,0},{1,25},{9,17},{17,9},{25,1},{2,26},{10... | collective-permute-start | bytes 786440 | tf_op jit(solution)/shard_map/ppermute | solution.py:402
  144.2 2.9 %collective-permute-done.25 = f32[1,128]{1,0:T(1,128)S(1)} collective-permute-done((f32[1,128]{1,0:T(1,128)S(1)}, f32[1,128]{1,0:T(1,128)S(1)}, u32[]{:S(2)}, u32[]{:S(2)}) %collective-permute-start.25) | collective-permute-done | bytes 544 | tf_op jit(solution)/shard_map/ppermute | solution.py:402
  147.0 1.6 collective-permute-start.26
  148.7 2.8 %collective-permute-done.26 = f32[1,128]{1,0:T(1,128)S(1)} collective-permute-done((f32[1,128]{1,0:T(1,128)S(1)}, f32[1,128]{1,0:T(1,128)S(1)}, u32[]{:S(2)}, u32[]{:S(2)}) %collective-permute-start.26) | collective-permute-done | bytes 544 | tf_op jit(solution)/shard_map/ppermute | solution.py:402
  152.0 2.2 %collective-permute-done.28.refs_1_ = bf16[128,1024]{1,0:T(8,128)(2,1)S(1)} collective-permute-done((bf16[128,1024]{1,0:T(8,128)(2,1)}, bf16[128,1024]{1,0:T(8,128)(2,1)S(1)}, u32[]{:S(2)}, u32[]{:S(2)}) %collective-permute-start.28) | collective-permute-done | bytes 262176 | tf_op jit(solution)/shard_map/ppermute | solution.py:402
  155.5 9.2 %head_product.1 = bf16[4608,1024]{1,0:T(8,128)(2,1)} custom-call(s32[1]{0:T(128)} %bitcast.4.tok_ref, bf16[4608,512]{1,0:T(8,128)(2,1)} %get-tuple-element.57.a_ref, bf16[128,1024]{1,0:T(8,128)(2,1)S(1)} %collective-permute-done.27.refs_0_, bf16[128,1024]{1,0:T(8,128)(2,1)S(1)} %collective-permute-done.28.refs_1_, ...), custom_call_target="tpu_custom_call" | custom-call | flops 1024 | bytes 1024 | tf_op jit(solution)/shard_map/head_product/pallas_call | solution.py:387
  (92 shorter events, 19.8 us)
Async XLA Ops:
  0.6 28.9 %collective-permute-start.9 = (bf16[32,4,128,128]{3,2,1,0:T(8,128)(2,1)}, bf16[32,4,128,128]{3,2,1,0:T(8,128)(2,1)}, u32[]{:S(2)}, u32[]{:S(2)}) collective-permute-start(bf16[32,4,128,128]{3,2,1,0:T(8,128)(2,1)} %w_own.3), channel_id=1, source_target_pairs={{0,1},{1,0},{2,3},{3,2},{4,5},{5,4},{6,7},{7,6},{8,9},{9,8},{10,11... | collective-permute-start | bytes 12582920 | tf_op jit(solution)/shard_map/ppermute | solution.py:402
  4.7 34.1 %all-to-all-start = ((bf16[4,64,4608]{2,1,0:T(8,128)(2,1)}), bf16[4,64,4608]{2,1,0:T(8,128)(2,1)}, u32[]{:S(2)}, u32[]{:S(2)}) async-start(bf16[4,64,4608]{2,1,0:T(8,128)(2,1)} %broadcast_in_dim.21), calls=%async_computation | async-start | bytes 4718592 | tf_op jit(solution)/shard_map/all_to_all | solution.py:424
  9.6 14.9 %collective-permute-start.1 = (bf16[128,4096]{1,0:T(8,128)(2,1)S(1)}, bf16[128,4096]{1,0:T(8,128)(2,1)S(1)}, u32[]{:S(2)}, u32[]{:S(2)}) collective-permute-start(bf16[128,4096]{1,0:T(8,128)(2,1)S(1)} %copy-done.4), channel_id=1, source_target_pairs={{0,1},{1,0},{2,3},{3,2},{4,5},{5,4},{6,7},{7,6},{8,9},{9,8},{10,11... | collective-permute-start | bytes 3145736 | tf_op jit(solution)/shard_map/ppermute | solution.py:402
  9.7 7.1 %collective-permute-start.2 = (f32[8,128]{1,0:T(8,128)S(1)}, f32[8,128]{1,0:T(8,128)S(1)}, u32[]{:S(2)}, u32[]{:S(2)}) collective-permute-start(f32[8,128]{1,0:T(8,128)S(1)} %teacher_stats.1.refs_0_), channel_id=1, source_target_pairs={{0,2},{1,3},{2,0},{3,1},{4,6},{5,7},{6,4},{7,5},{8,10},{9,11},{10,... | collective-permute-start | bytes 12296 | tf_op jit(solution)/shard_map/ppermute | solution.py:402
  12.7 2.7 %collective-permute-start = (s32[128]{0:T(128)S(1)}, s32[128]{0:T(128)S(1)}, u32[]{:S(2)}, u32[]{:S(2)}) collective-permute-start(s32[128]{0:T(128)S(1)} %reshape.19.own_ref), channel_id=1, source_target_pairs={{0,1},{1,0},{2,3},{3,2},{4,5},{5,4},{6,7},{7,6},{8,9},{9,8},{10,11... | collective-permute-start | bytes 1544 | tf_op jit(solution)/shard_map/ppermute | solution.py:402
  12.8 4.6 %collective-permute-start.3 = (f32[8,128]{1,0:T(8,128)S(1)}, f32[8,128]{1,0:T(8,128)S(1)}, u32[]{:S(2)}, u32[]{:S(2)}) collective-permute-start(f32[8,128]{1,0:T(8,128)S(1)} %teacher_stats.1.refs_0_), channel_id=1, source_target_pairs={{0,4},{1,5},{2,6},{3,7},{4,0},{5,1},{6,2},{7,3},{8,12},{9,13},{10,... | collective-permute-start | bytes 12296 | tf_op jit(solution)/shard_map/ppermute | solution.py:402
  15.5 5.4 %collective-permute-start.4 = (f32[8,128]{1,0:T(8,128)S(1)}, f32[8,128]{1,0:T(8,128)S(1)}, u32[]{:S(2)}, u32[]{:S(2)}) collective-permute-start(f32[8,128]{1,0:T(8,128)S(1)} %teacher_stats.1.refs_0_), channel_id=1, source_target_pairs={{0,6},{1,7},{2,4},{3,5},{4,2},{5,3},{6,0},{7,1},{8,14},{9,15},{10,... | collective-permute-start | bytes 12296 | tf_op jit(solution)/shard_map/ppermute | solution.py:402
  16.8 4.1 %collective-permute-start.5 = (f32[8,128]{1,0:T(8,128)S(1)}, f32[8,128]{1,0:T(8,128)S(1)}, u32[]{:S(2)}, u32[]{:S(2)}) collective-permute-start(f32[8,128]{1,0:T(8,128)S(1)} %teacher_stats.1.refs_0_), channel_id=1, source_target_pairs={{0,1},{1,0},{2,3},{3,2},{4,5},{5,4},{6,7},{7,6},{8,9},{9,8},{10,11... | collective-permute-start | bytes 12296 | tf_op jit(solution)/shard_map/ppermute | solution.py:402
  17.4 7.1 %collective-permute-start.6 = (f32[8,128]{1,0:T(8,128)S(1)}, f32[8,128]{1,0:T(8,128)S(1)}, u32[]{:S(2)}, u32[]{:S(2)}) collective-permute-start(f32[8,128]{1,0:T(8,128)S(1)} %collective-permute-done.2.refs_1_), channel_id=1, source_target_pairs={{0,1},{1,0},{2,3},{3,2},{4,5},{5,4},{6,7},{7,6},{8,9},{9,8},{10,11... | collective-permute-start | bytes 12296 | tf_op jit(solution)/shard_map/ppermute | solution.py:402
  20.9 3.7 %collective-permute-start.7 = (f32[8,128]{1,0:T(8,128)S(1)}, f32[8,128]{1,0:T(8,128)S(1)}, u32[]{:S(2)}, u32[]{:S(2)}) collective-permute-start(f32[8,128]{1,0:T(8,128)S(1)} %collective-permute-done.3.refs_2_), channel_id=1, source_target_pairs={{0,1},{1,0},{2,3},{3,2},{4,5},{5,4},{6,7},{7,6},{8,9},{9,8},{10,11... | collective-permute-start | bytes 12296 | tf_op jit(solution)/shard_map/ppermute | solution.py:402
  20.9 3.7 %collective-permute-start.8 = (f32[8,128]{1,0:T(8,128)S(1)}, f32[8,128]{1,0:T(8,128)S(1)}, u32[]{:S(2)}, u32[]{:S(2)}) collective-permute-start(f32[8,128]{1,0:T(8,128)S(1)} %collective-permute-done.4.refs_3_), channel_id=1, source_target_pairs={{0,1},{1,0},{2,3},{3,2},{4,5},{5,4},{6,7},{7,6},{8,9},{9,8},{10,11... | collective-permute-start | bytes 12296 | tf_op jit(solution)/shard_map/ppermute | solution.py:402
  38.8 14.6 %collective-permute-start.11 = (bf16[256,4608]{1,0:T(8,128)(2,1)}, bf16[256,4608]{1,0:T(8,128)(2,1)S(1)}, u32[]{:S(2)}, u32[]{:S(2)}) collective-permute-start(bf16[256,4608]{1,0:T(8,128)(2,1)} %bitcast.3.near_ref), channel_id=1, source_target_pairs={{0,1},{1,0},{2,3},{3,2},{4,5},{5,4},{6,7},{7,6},{8,9},{9,8},{10,11... | collective-permute-start | bytes 7077896 | tf_op jit(solution)/shard_map/ppermute | solution.py:402
  38.8 30.9 %collective-permute-start.12 = (bf16[32,128,128]{2,1,0:T(8,128)(2,1)}, bf16[32,128,128]{2,1,0:T(8,128)(2,1)}, u32[]{:S(2)}, u32[]{:S(2)}) collective-permute-start(bf16[32,128,128]{2,1,0:T(8,128)(2,1)} %get-tuple-element.44), channel_id=1, source_target_pairs={{0,2},{1,3},{6,4},{7,5},{8,10},{9,11},{14,12},{15,13},{16,18},{17,... | collective-permute-start | bytes 3145736 | tf_op jit(solution)/shard_map/ppermute | solution.py:428
  63.7 29.6 %all-to-all-start.1 = ((f32[4,128,1024]{2,1,0:T(8,128)}), f32[4,128,1024]{2,1,0:T(8,128)S(1)}, u32[]{:S(2)}, u32[]{:S(2)}) async-start(f32[4,128,1024]{2,1,0:T(8,128)} %get-tuple-element.43), calls=%async_computation.1 | async-start | bytes 4194304 | tf_op jit(solution)/shard_map/all_to_all | solution.py:424
  67.3 27.4 %collective-permute-start.10 = (bf16[32,128,128]{2,1,0:T(8,128)(2,1)}, bf16[32,128,128]{2,1,0:T(8,128)(2,1)}, u32[]{:S(2)}, u32[]{:S(2)}) collective-permute-start(bf16[32,128,128]{2,1,0:T(8,128)(2,1)} %get-tuple-element.36), channel_id=1, source_target_pairs={{0,2},{1,3},{6,4},{7,5},{8,10},{9,11},{14,12},{15,13},{16,18},{17,... | collective-permute-start | bytes 3145736 | tf_op jit(solution)/shard_map/ppermute | solution.py:428
  72.6 24.7 %collective-permute-start.13 = (bf16[32,128,128]{2,1,0:T(8,128)(2,1)}, bf16[32,128,128]{2,1,0:T(8,128)(2,1)}, u32[]{:S(2)}, u32[]{:S(2)}) collective-permute-start(bf16[32,128,128]{2,1,0:T(8,128)(2,1)} %add_convert_fusion.2), channel_id=1, source_target_pairs={{2,4},{3,5},{4,2},{5,3},{10,12},{11,13},{12,10},{13,11},{18,20},{1... | collective-permute-start | bytes 3145736 | tf_op jit(solution)/shard_map/ppermute | solution.py:428
  96.4 39.1 %collective-permute-start.22 = (bf16[32,128,128]{2,1,0:T(8,128)(2,1)S(1)}, bf16[32,128,128]{2,1,0:T(8,128)(2,1)S(1)}, u32[]{:S(2)}, u32[]{:S(2)}) collective-permute-start(bf16[32,128,128]{2,1,0:T(8,128)(2,1)S(1)} %add_convert_fusion.1), channel_id=1, source_target_pairs={{2,4},{3,5},{4,2},{5,3},{10,12},{11,13},{12,10},{13,11},{18,20},{1... | collective-permute-start | bytes 3145736 | tf_op jit(solution)/shard_map/ppermute | solution.py:428
  98.9 36.6 %collective-permute-start.23 = (bf16[32,128,128]{2,1,0:T(8,128)(2,1)S(1)}, bf16[32,128,128]{2,1,0:T(8,128)(2,1)S(1)}, u32[]{:S(2)}, u32[]{:S(2)}) collective-permute-start(bf16[32,128,128]{2,1,0:T(8,128)(2,1)S(1)} %add_convert_fusion), channel_id=1, source_target_pairs={{2,0},{3,1},{4,6},{5,7},{10,8},{11,9},{12,14},{13,15},{18,16},{19,... | collective-permute-start | bytes 3145736 | tf_op jit(solution)/shard_map/ppermute | solution.py:428
  100.2 35.3 %collective-permute-start.21 = (bf16[32,128,128]{2,1,0:T(8,128)(2,1)S(1)}, bf16[32,128,128]{2,1,0:T(8,128)(2,1)S(1)}, u32[]{:S(2)}, u32[]{:S(2)}) collective-permute-start(bf16[32,128,128]{2,1,0:T(8,128)(2,1)S(1)} %copy-done.12), channel_id=1, source_target_pairs={{0,2},{1,3},{6,4},{7,5},{8,10},{9,11},{14,12},{15,13},{16,18},{17,... | collective-permute-start | bytes 3145736 | tf_op jit(solution)/shard_map/ppermute | solution.py:428
  105.1 22.5 %collective-permute-start.14 = (f32[8,128]{1,0:T(8,128)S(1)}, f32[8,128]{1,0:T(8,128)S(1)}, u32[]{:S(2)}, u32[]{:S(2)}) collective-permute-start(f32[8,128]{1,0:T(8,128)S(1)} %student_stats.1.refs_0_), channel_id=1, source_target_pairs={{0,2},{1,3},{2,0},{3,1},{4,6},{5,7},{6,4},{7,5},{8,10},{9,11},{10,... | collective-permute-start | bytes 12296 | tf_op jit(solution)/shard_map/ppermute | solution.py:402
  105.2 24.9 %collective-permute-start.15 = (f32[8,128]{1,0:T(8,128)S(1)}, f32[8,128]{1,0:T(8,128)S(1)}, u32[]{:S(2)}, u32[]{:S(2)}) collective-permute-start(f32[8,128]{1,0:T(8,128)S(1)} %student_stats.1.refs_0_), channel_id=1, source_target_pairs={{0,4},{1,5},{2,6},{3,7},{4,0},{5,1},{6,2},{7,3},{8,12},{9,13},{10,... | collective-permute-start | bytes 12296 | tf_op jit(solution)/shard_map/ppermute | solution.py:402
  127.7 5.4 %collective-permute-start.16 = (f32[8,128]{1,0:T(8,128)S(1)}, f32[8,128]{1,0:T(8,128)S(1)}, u32[]{:S(2)}, u32[]{:S(2)}) collective-permute-start(f32[8,128]{1,0:T(8,128)S(1)} %student_stats.1.refs_0_), channel_id=1, source_target_pairs={{0,6},{1,7},{2,4},{3,5},{4,2},{5,3},{6,0},{7,1},{8,14},{9,15},{10,... | collective-permute-start | bytes 12296 | tf_op jit(solution)/shard_map/ppermute | solution.py:402
  130.1 3.0 %collective-permute-start.17 = (f32[8,128]{1,0:T(8,128)S(1)}, f32[8,128]{1,0:T(8,128)S(1)}, u32[]{:S(2)}, u32[]{:S(2)}) collective-permute-start(f32[8,128]{1,0:T(8,128)S(1)} %student_stats.1.refs_0_), channel_id=1, source_target_pairs={{0,1},{1,0},{2,3},{3,2},{4,5},{5,4},{6,7},{7,6},{8,9},{9,8},{10,11... | collective-permute-start | bytes 12296 | tf_op jit(solution)/shard_map/ppermute | solution.py:402
  133.1 1.2 collective-permute-start.18
  133.1 1.3 collective-permute-start.19
  134.2 1.2 collective-permute-start.20
  138.9 13.1 %collective-permute-start.27 = (bf16[128,1024]{1,0:T(8,128)(2,1)}, bf16[128,1024]{1,0:T(8,128)(2,1)S(1)}, u32[]{:S(2)}, u32[]{:S(2)}) collective-permute-start(bf16[128,1024]{1,0:T(8,128)(2,1)} %get-tuple-element.58), channel_id=1, source_target_pairs={{0,24},{8,16},{16,8},{24,0},{1,25},{9,17},{17,9},{25,1},{2,26},{10... | collective-permute-start | bytes 786440 | tf_op jit(solution)/shard_map/ppermute | solution.py:402
  141.7 12.5 %collective-permute-start.28 = (bf16[128,1024]{1,0:T(8,128)(2,1)}, bf16[128,1024]{1,0:T(8,128)(2,1)S(1)}, u32[]{:S(2)}, u32[]{:S(2)}) collective-permute-start(bf16[128,1024]{1,0:T(8,128)(2,1)} %get-tuple-element.59), channel_id=1, source_target_pairs={{0,16},{8,24},{16,0},{24,8},{1,17},{9,25},{17,1},{25,9},{2,18},{10... | collective-permute-start | bytes 786440 | tf_op jit(solution)/shard_map/ppermute | solution.py:402
  142.3 12.2 %collective-permute-start.29 = (bf16[128,1024]{1,0:T(8,128)(2,1)}, bf16[128,1024]{1,0:T(8,128)(2,1)S(1)}, u32[]{:S(2)}, u32[]{:S(2)}) collective-permute-start(bf16[128,1024]{1,0:T(8,128)(2,1)} %get-tuple-element.60), channel_id=1, source_target_pairs={{0,8},{8,0},{16,24},{24,16},{1,9},{9,1},{17,25},{25,17},{2,10},{10... | collective-permute-start | bytes 786440 | tf_op jit(solution)/shard_map/ppermute | solution.py:402
  142.4 1.1 collective-permute-start.24
  143.5 3.5 %collective-permute-start.25 = (f32[1,128]{1,0:T(1,128)S(1)}, f32[1,128]{1,0:T(1,128)S(1)}, u32[]{:S(2)}, u32[]{:S(2)}) collective-permute-start(f32[1,128]{1,0:T(1,128)S(1)} %add.81), channel_id=1, source_target_pairs={{0,2},{1,3},{2,0},{3,1},{4,6},{5,7},{6,4},{7,5},{8,10},{9,11},{10,... | collective-permute-start | bytes 1544 | tf_op jit(solution)/shard_map/ppermute | solution.py:402
  147.0 4.4 %collective-permute-start.26 = (f32[1,128]{1,0:T(1,128)S(1)}, f32[1,128]{1,0:T(1,128)S(1)}, u32[]{:S(2)}, u32[]{:S(2)}) collective-permute-start(f32[1,128]{1,0:T(1,128)S(1)} %add.82), channel_id=1, source_target_pairs={{0,4},{1,5},{2,6},{3,7},{4,0},{5,1},{6,2},{7,3},{8,12},{9,13},{10,... | collective-permute-start | bytes 1544 | tf_op jit(solution)/shard_map/ppermute | solution.py:402
  (17 other events, 88.3 us)

commit v4 on v3

--- a/solution.py
+++ b/solution.py
@@ -111,6 +111,7 @@
         in_specs=[SMEM_SPEC] * 2,
         out_specs=[SMEM_SPEC] * 2,
         out_shape=[jax.ShapeDtypeStruct((lists, room), jnp.int32), jax.ShapeDtypeStruct((lists,), jnp.int32)],
+        compiler_params=params(1),
         cost_estimate=COST,
         name="entry_lists",
     )(own_code, peer_code)
@@ -249,37 +250,60 @@
     )(spot, after, near, far, pltpu.with_memory_space_constraint(head, pltpu.HBM))
 
 
-def student_kernel(base_ref, labels_ref, mass_ref, logits_ref, stat_ref):
+def student_kernel(spot_ref, labels_ref, mass_ref, logits_ref, *outs):
     n_tok, rows, cols = logits_ref.shape
     lane = lax.broadcasted_iota(jnp.int32, (rows, LANES), 1)
-    label = labels_ref[...]
-    top = jnp.full((rows, LANES), -jnp.inf, F32)
-    hit = jnp.zeros((rows, LANES), F32)
-    for t in range(n_tok):
+    for r, out in enumerate(outs):
+        t = spot_ref[0] ^ r
+        label = labels_ref[t] - spot_ref[1]
+        top = jnp.full((rows, LANES), -jnp.inf, F32)
+        hit = jnp.zeros((rows, LANES), F32)
         for b in range(0, cols, LANES):
             block = logits_ref[t, :, b : b + LANES]
             top = jnp.maximum(top, block)
-            hit = hit + jnp.where(lane == label - (base_ref[t] + b), block, 0.0)
-    top = jnp.max(top, axis=1, keepdims=True)
-    total = jnp.zeros((rows, LANES), F32)
-    for t in range(n_tok):
+            hit = hit + jnp.where(lane == label - b, block, 0.0)
+        top = jnp.max(top, axis=1, keepdims=True)
+        total = jnp.zeros((rows, LANES), F32)
         for b in range(0, cols, LANES):
             total = total + jnp.exp(logits_ref[t, :, b : b + LANES] - top)
-    total = jnp.sum(total, axis=1, keepdims=True)
-    hit = jnp.sum(hit, axis=1, keepdims=True)
-    stat_ref[...] = mass_ref[...] + rows_from_columns([jnp.zeros_like(hit), top, total, hit])
-
-
-def student_stats(base, label_column, mass, logits):
+        total = jnp.sum(total, axis=1, keepdims=True)
+        hit = jnp.sum(hit, axis=1, keepdims=True)
+        out[...] = rows_from_columns([jnp.zeros_like(hit), top, total, hit])
+    outs[0][0:1, :] = mass_ref[0:1, :]
+
+
+def student_stats(spot, label_columns, mass, logits):
+    n_tok, rows, _ = logits.shape
     return pl.pallas_call(
         student_kernel,
         in_specs=[SMEM_SPEC] + [VMEM_SPEC] * 3,
+        out_specs=[VMEM_SPEC] * n_tok,
+        out_shape=[jax.ShapeDtypeStruct((8, rows), F32)] * n_tok,
+        compiler_params=params(16),
+        cost_estimate=COST,
+        name="student_stats",
+    )(spot, label_columns, mass, logits)
+
+
+def merge_kernel(*refs):
+    stats, out = refs[:-1], refs[-1]
+    parts = split_rows(stats)
+    mass = tree(jnp.add, [r[0] for r in parts])
+    top, total = total_at(parts, 1, 2)
+    hit = tree(jnp.add, [r[3] for r in parts])
+    out[...] = jnp.concatenate([mass, top, total, hit, jnp.zeros((4, top.shape[1]), F32)], axis=0)
+
+
+def merge_stats(stats):
+    return pl.pallas_call(
+        merge_kernel,
+        in_specs=[VMEM_SPEC] * len(stats),
         out_specs=VMEM_SPEC,
-        out_shape=jax.ShapeDtypeStruct(mass.shape, F32),
-        compiler_params=params(16),
-        cost_estimate=COST,
-        name="student_stats",
-    )(base, label_column, mass, logits)
+        out_shape=jax.ShapeDtypeStruct(stats[0].shape, F32),
+        compiler_params=params(1),
+        cost_estimate=COST,
+        name="merge_stats",
+    )(*stats)
 
 
 def totals_kernel(*refs):
@@ -416,6 +440,12 @@
     return chips + [swap(chip, "vocab", 1) for chip in chips]
 
 
+def half_rows(hidden, spot, n_tok):
+    half = hidden.shape[0] // 2
+    own = lax.dynamic_slice_in_dim(hidden, spot[0] * half, half)
+    return jnp.broadcast_to(own, (n_tok,) + own.shape)
+
+
 def plus(a, b):
     return (a.astype(F32) + b.astype(F32)).astype(BF16)
 
@@ -460,9 +490,6 @@
     peer_weight = swap(map_weight, "vocab", 1)
     teacher = teacher_stats(teacher_logits)
     totals = gather_cores(teacher)
-    half = lax.dynamic_slice_in_dim(hidden, spot[0] * (rows // 2), rows // 2)
-    half, teacher = lax.optimization_barrier((half, teacher))
-    near = exchange_tok(jnp.broadcast_to(half, (n_tok,) + half.shape)).reshape(n_tok * (rows // 2), -1)
     lists, counts = plan(code, peer_code, 2 * n_z)
     probs = teacher_probs(teacher_logits, peer_logits, totals)
 
@@ -470,13 +497,18 @@
         inward, across, outward = [(0, 1), (3, 2)], [(1, 2), (2, 1)], [(1, 0), (2, 3)]
         far_outer, mass_a = chip_sums(spot, lists, counts, probs, map_weight, peer_weight, 0, 1, 1, slots)
         first = send(far_outer, inward)
-        near, mass_a = lax.optimization_barrier((near, mass_a))
-        probs, far_outer = lax.optimization_barrier((probs, far_outer))
+        rows_in, mass_a = lax.optimization_barrier((hidden, mass_a))
+        copies, probs = lax.optimization_barrier((half_rows(rows_in, spot, n_tok), probs))
+        near = exchange_tok(copies)
         far_inner, beside, own, mass_b = chip_sums(
             spot, lists, counts, probs, map_weight, peer_weight, 1, 3, 1, slots
         )
         second = send(far_inner, inward)
-        mass = mass_a + mass_b
+        first, mass = lax.optimization_barrier((first, mass_a + mass_b))
+        merged = plus(far_outer, first)
+        crossed_outer = send(merged, across)
+        near, waited, merged = lax.optimization_barrier((near, beside, merged))
+        third = send(waited, inward)
     else:
         sums, mass = chip_sums(spot, lists, counts, probs, map_weight, peer_weight, 0, 1, n_z, slots)
         lines = [[2 * z + c for z in range(n_z)] for c in range(2)]
@@ -489,30 +521,30 @@
             tiled=True,
         )
         sums = [sums]
-
+        near = exchange_tok(half_rows(hidden, spot, n_tok))
+
+    near = near.reshape(n_tok * (rows // 2), -1)
     far = swap(near, "vocab", 1)
     scores, turned = student_logits(spot, mass, near, far, new_head, n_tok)
+    base = (jnp.arange(n_tok, dtype=jnp.int32) * n_vocab + vocab) * new_cols
+    own_base = (tok * n_vocab + vocab) * new_cols
+    label_columns = labels.reshape(n_tok, rows, 1)
+    label_column = lax.dynamic_index_in_dim(label_columns, tok, keepdims=False)
+    place = jnp.stack([tok, own_base]).astype(jnp.int32)
+    student = student_stats(place, label_columns, mass, scores)
+    student = merge_stats([student[0]] + [swap(student[r], "tok", r) for r in range(1, n_tok)])
+    student = merge_stats([student, swap(student, "vocab", 1)])
     scores = exchange_tok(scores)
-    label_column = lax.dynamic_slice_in_dim(labels, tok * rows, rows).reshape(rows, 1)
-    base = (jnp.arange(n_tok, dtype=jnp.int32) * n_vocab + vocab) * new_cols
     if in_line:
-        first, turned = lax.optimization_barrier((first, turned))
-        merged = plus(far_outer, first)
-        crossed_outer = send(merged, across)
-        scores, merged = lax.optimization_barrier((scores, merged))
-        student = student_stats(base, label_column, mass, scores)
-        second, waited, student = lax.optimization_barrier((second, beside, student))
-        third = send(waited, inward)
+        second, turned = lax.optimization_barrier((second, turned))
         merged_inner = plus(far_inner, second)
         crossed_inner = send(merged_inner, across)
         crossed_outer, merged_inner = lax.optimization_barrier((crossed_outer, merged_inner))
         merged_near = plus(beside, crossed_outer)
         arrived = send(merged_near, outward)
-        student, merged_near = lax.optimization_barrier((student, merged_near))
+        student, scores, merged_near = lax.optimization_barrier((student, scores, merged_near))
         sums = [x[None] for x in (own, third, crossed_inner, arrived)]
-    else:
-        student = student_stats(base, label_column, mass, scores)
-    stats = gather_cores(student)
+    stats = gather_chips(student)
 
     group = tok.astype(jnp.int32).reshape(1)
     columns, base_loss = token_totals(stats)

time: 166 us -> 157 us (0.946)
  waiting for transfers between devices: 59.9 us -> 40.9 us
  starting transfers between devices: 44.5 us -> 48.9 us
  Pallas kernels: 41.3 us -> 43.8 us
  local copies, waits for them, and re-layouts: 11.1 us -> 13.3 us
    all_to_all x2, waiting for transfers between devices: 22.7 us -> 3 us  [exchange_tok(): return lax.all_to_all(x, 'tok', split_axis=0, concat_axis=0, tiled=True)]
    ppermute x6, waiting for transfers between devices: 0.02 us -> 15.2 us  [send(): lax.ppermute(x, 'vocab', [(2 * a + c, 2 * b + c) for a, b in hops for c i...]
    ppermute x24, waiting for transfers between devices: 37.2 us -> 22.7 us  [swap(): lax.ppermute(x, axis, [(i, i ^ mask) for i in range(lax.axis_size(axis))])]
    ppermute x24, starting transfers between devices: 20.3 us -> 28.5 us  [swap(): lax.ppermute(x, axis, [(i, i ^ mask) for i in range(lax.axis_size(axis))])]
    ppermute x6, starting transfers between devices: 15.7 us -> 12 us  [send(): lax.ppermute(x, 'vocab', [(2 * a + c, 2 * b + c) for a, b in hops for c i...]
    unnamed x34 -> x26, local copies, waits for them, and re-layouts: 8.44 us -> 11.2 us
  transfers between devices with their start and end apart: 32 -> 32, of which waited for: 13 -> 14; matrix products, arithmetic and copies ran while one was open for 6% -> 6% of each run, Pallas kernels for 18% -> 16%
where the time goes in v4:
time: 157 us; the launch traced here: 156 us
  starting transfers between devices  48.9 us (31%)
  Pallas kernels  43.8 us (28%)
  waiting for transfers between devices  40.9 us (26%)
  local copies, waits for them, and re-layouts  13.3 us (8%)
  other arithmetic  8.31 us (5%)
    ppermute x24, starting transfers between devices, swap(): lax.ppermute(x, axis, [(i, i ^ mask) for i in range(lax.axis_size(axis))])  28.5 us
    ppermute x24, waiting for transfers between devices, swap(): lax.ppermute(x, axis, [(i, i ^ mask) for i in range(lax.axis_size(axis))])  22.7 us
    ppermute x6, waiting for transfers between devices, send(): lax.ppermute(x, 'vocab', [(2 * a + c, 2 * b + c) for a, b in hops for c i...  15.2 us
    pallas_call x2, Pallas kernels, chip_sums(): pl.pallas_call(functools.partial(sums_kernel, first=first, fan=fan, piece...  13 us
    ppermute x6, starting transfers between devices, send(): lax.ppermute(x, 'vocab', [(2 * a + c, 2 * b + c) for a, b in hops for c i...  12 us
    unnamed x26, local copies, waits for them, and re-layouts  11.2 us
    pallas_call x1, Pallas kernels, student_logits(): pl.pallas_call(logits_kernel, grid=(cols // tile,), in_specs=[SMEM_SPEC,...  10.4 us
    pallas_call x1, Pallas kernels, head_product(): pl.pallas_call(product_kernel, grid=(m // tile,), in_specs=[SMEM_SPEC, pl...  9.16 us
  transfers between devices with their start and end apart: 32, of which 14 were waited for; matrix products, arithmetic and copies ran while one was open for 6% of the time, Pallas kernels for 16%

profile of v4, /device:TPU:0, one launch (start us, length us, event | category | flops | bytes accessed | tf_op | source)
XLA Modules:
  0.0 156.2 jit_solution(10272938362454930858)
XLA Ops:
  3.1 3.0 %collective-permute-start.2 = (f32[8,128]{1,0:T(8,128)S(1)}, f32[8,128]{1,0:T(8,128)S(1)}, u32[]{:S(2)}, u32[]{:S(2)}) collective-permute-start(f32[8,128]{1,0:T(8,128)S(1)} %teacher_stats.1.refs_0_), channel_id=1, source_target_pairs={{0,2},{1,3},{2,0},{3,1},{4,6},{5,7},{6,4},{7,5},{8,10},{9,11},{10,... | collective-permute-start | bytes 12296 | tf_op jit(solution)/shard_map/ppermute | solution.py:426
  7.1 2.7 %collective-permute-start.3 = (f32[8,128]{1,0:T(8,128)S(1)}, f32[8,128]{1,0:T(8,128)S(1)}, u32[]{:S(2)}, u32[]{:S(2)}) collective-permute-start(f32[8,128]{1,0:T(8,128)S(1)} %teacher_stats.1.refs_0_), channel_id=1, source_target_pairs={{0,4},{1,5},{2,6},{3,7},{4,0},{5,1},{6,2},{7,3},{8,12},{9,13},{10,... | collective-permute-start | bytes 12296 | tf_op jit(solution)/shard_map/ppermute | solution.py:426
  9.7 3.8 %collective-permute-start.4 = (f32[8,128]{1,0:T(8,128)S(1)}, f32[8,128]{1,0:T(8,128)S(1)}, u32[]{:S(2)}, u32[]{:S(2)}) collective-permute-start(f32[8,128]{1,0:T(8,128)S(1)} %teacher_stats.1.refs_0_), channel_id=1, source_target_pairs={{0,6},{1,7},{2,4},{3,5},{4,2},{5,3},{6,0},{7,1},{8,14},{9,15},{10,... | collective-permute-start | bytes 12296 | tf_op jit(solution)/shard_map/ppermute | solution.py:426
  15.7 3.0 %entry_lists.1 = (s32[8,264]{1,0:T(8,128)S(1)}, s32[8]{0:T(128)S(1)}) custom-call(s32[128]{0:T(128)S(1)} %reshape.18.own_ref, s32[128]{0:T(128)S(1)} %collective-permute-done.peer_ref), custom_call_target="tpu_custom_call" | custom-call | flops 1024 | bytes 1024 | tf_op jit(solution)/shard_map/entry_lists/pallas_call | solution.py:109
  19.8 1.8 %copy-done.5 = bf16[128,4096]{1,0:T(8,128)(2,1)S(1)} copy-done((bf16[128,4096]{1,0:T(8,128)(2,1)S(1)}, bf16[128,4096]{1,0:T(8,128)(2,1)}, u32[]{:S(2)}) %copy-start.5) | copy-done | bytes 1048600
  23.8 5.0 %chip_sums.2 = (bf16[32,128,128]{2,1,0:T(8,128)(2,1)}, f32[8,128]{1,0:T(8,128)S(1)}) custom-call(s32[2]{0:T(128)S(1)} %pad_add_fusion.1.spot_ref, s32[8,264]{1,0:T(8,128)S(1)} %get-tuple-element.36.list_ref, s32[8]{0:T(128)S(1)} %get-tuple-element.37.count_ref, bf16[64,128,128]{2,1,0:T(8,128)(2,1)S(1)} %teacher_probs.1.probs, ...), custom_call_target="tpu_custom_call" | custom-call | flops 1024 | bytes 1024 | tf_op jit(solution)/shard_map/chip_sums/pallas_call | solution.py:196
  30.4 4.7 %all-to-all-start = ((bf16[4,64,4608]{2,1,0:T(8,128)(2,1)}), bf16[4,64,4608]{2,1,0:T(8,128)(2,1)}, u32[]{:S(2)}, u32[]{:S(2)}) async-start(bf16[4,64,4608]{2,1,0:T(8,128)(2,1)} %broadcast_in_dim.21), calls=%async_computation | async-start | bytes 4718592 | tf_op jit(solution)/shard_map/all_to_all | solution.py:454
  36.5 2.2 %copy-done.2 = bf16[32,4,128,128]{3,2,1,0:T(8,128)(2,1)S(1)} copy-done((bf16[32,4,128,128]{3,2,1,0:T(8,128)(2,1)S(1)}, bf16[32,4,128,128]{3,2,1,0:T(8,128)(2,1)}, u32[]{:S(2)}) %copy-start.2) | copy-done | bytes 4194328
  38.7 8.0 %chip_sums.3 = (bf16[32,128,128]{2,1,0:T(8,128)(2,1)}, bf16[32,128,128]{2,1,0:T(8,128)(2,1)}, bf16[32,128,128]{2,1,0:T(8,128)(2,1)}, f32[8,128]{1,0:T(8,128)S(1)}) custom-call(s32[2]{0:T(128)S(1)} %pad_add_fusion.1.spot_ref, s32[8,264]{1,0:T(8,128)S(1)} %get-tuple-element.36.list_ref, s32[8]{0:T(128)S(1)} %get-tuple-element.37.count_ref, ...), custom_call_target="tpu_custom_call" | custom-call | flops 1024 | bytes 1024 | tf_op jit(solution)/shard_map/chip_sums/pallas_call | solution.py:196
  46.7 12.6 %collective-permute-done.10 = bf16[32,128,128]{2,1,0:T(8,128)(2,1)S(1)} collective-permute-done((bf16[32,128,128]{2,1,0:T(8,128)(2,1)}, bf16[32,128,128]{2,1,0:T(8,128)(2,1)S(1)}, u32[]{:S(2)}, u32[]{:S(2)}) %collective-permute-start.10) | collective-permute-done | bytes 1048608 | tf_op jit(solution)/shard_map/ppermute | solution.py:458
  60.6 3.0 %all-to-all-done = bf16[4,64,4608]{2,1,0:T(8,128)(2,1)} async-done(((bf16[4,64,4608]{2,1,0:T(8,128)(2,1)}), bf16[4,64,4608]{2,1,0:T(8,128)(2,1)}, u32[]{:S(2)}, u32[]{:S(2)}) %all-to-all-start) | async-done | bytes 2359328 | tf_op jit(solution)/shard_map/all_to_all | solution.py:454
  63.6 2.3 %collective-permute-start.17 = (bf16[32,128,128]{2,1,0:T(8,128)(2,1)}, bf16[32,128,128]{2,1,0:T(8,128)(2,1)}, u32[]{:S(2)}, u32[]{:S(2)}) collective-permute-start(bf16[32,128,128]{2,1,0:T(8,128)(2,1)} %get-tuple-element.54), channel_id=1, source_target_pairs={{0,2},{1,3},{6,4},{7,5},{8,10},{9,11},{14,12},{15,13},{16,18},{17,... | collective-permute-start | bytes 3145736 | tf_op jit(solution)/shard_map/ppermute | solution.py:458
  65.9 1.7 %collective-permute-start.16 = (bf16[32,128,128]{2,1,0:T(8,128)(2,1)}, bf16[32,128,128]{2,1,0:T(8,128)(2,1)}, u32[]{:S(2)}, u32[]{:S(2)}) collective-permute-start(bf16[32,128,128]{2,1,0:T(8,128)(2,1)} %add_convert_fusion.2), channel_id=1, source_target_pairs={{2,4},{3,5},{4,2},{5,3},{10,12},{11,13},{12,10},{13,11},{18,20},{1... | collective-permute-start | bytes 3145736 | tf_op jit(solution)/shard_map/ppermute | solution.py:458
  68.4 10.4 %student_logits.1 = (f32[4,128,1024]{2,1,0:T(8,128)}, bf16[4608,512]{1,0:T(8,128)(2,1)}) custom-call(s32[2]{0:T(128)S(1)} %pad_add_fusion.1.spot_ref, f32[8,128]{1,0:T(8,128)S(1)} %add.79.after_ref.mass_ref, bf16[256,4608]{1,0:T(8,128)(2,1)} %bitcast.5.near_ref, bf16[256,4608]{1,0:T(8,128)(2,1)S(1)} %collective-permute-done.11.far_ref, ...), custom_call_target="tpu_custom_call" | custom-call | flops 1024 | bytes 1024 | tf_op jit(solution)/shard_map/student_logits/pallas_call | solution.py:238
  78.7 3.7 %all-to-all-start.1 = ((f32[4,128,1024]{2,1,0:T(8,128)}), f32[4,128,1024]{2,1,0:T(8,128)S(1)}, u32[]{:S(2)}, u32[]{:S(2)}) async-start(f32[4,128,1024]{2,1,0:T(8,128)} %get-tuple-element.49.logits_ref), calls=%async_computation.1 | async-start | bytes 4194304 | tf_op jit(solution)/shard_map/all_to_all | solution.py:454
  82.5 3.7 %collective-permute-start.21 = (bf16[32,128,128]{2,1,0:T(8,128)(2,1)}, bf16[32,128,128]{2,1,0:T(8,128)(2,1)}, u32[]{:S(2)}, u32[]{:S(2)}) collective-permute-start(bf16[32,128,128]{2,1,0:T(8,128)(2,1)} %get-tuple-element.62), channel_id=1, source_target_pairs={{0,2},{1,3},{6,4},{7,5},{8,10},{9,11},{14,12},{15,13},{16,18},{17,... | collective-permute-start | bytes 3145736 | tf_op jit(solution)/shard_map/ppermute | solution.py:458
  86.2 2.6 %collective-permute-done.17 = bf16[32,128,128]{2,1,0:T(8,128)(2,1)} collective-permute-done((bf16[32,128,128]{2,1,0:T(8,128)(2,1)}, bf16[32,128,128]{2,1,0:T(8,128)(2,1)}, u32[]{:S(2)}, u32[]{:S(2)}) %collective-permute-start.17) | collective-permute-done | bytes 1048608 | tf_op jit(solution)/shard_map/ppermute | solution.py:458
  88.8 3.0 %add_convert_fusion.1 = bf16[32,128,128]{2,1,0:T(8,128)(2,1)} fusion(bf16[32,128,128]{2,1,0:T(8,128)(2,1)} %collective-permute-done.17, bf16[32,128,128]{2,1,0:T(8,128)(2,1)} %get-tuple-element.54), kind=kLoop, calls=%fused_computation.1 | loop fusion | flops 2097152 | bytes 3145728 | tf_op jit(solution)/shard_map/convert_element_type | solution.py:450
  91.8 2.6 %add_convert_fusion = bf16[32,128,128]{2,1,0:T(8,128)(2,1)} fusion(bf16[32,128,128]{2,1,0:T(8,128)(2,1)} %collective-permute-done.16, bf16[32,128,128]{2,1,0:T(8,128)(2,1)S(1)} %copy-done.10), kind=kLoop, calls=%fused_computation | loop fusion | flops 2097152 | bytes 3145728 | tf_op jit(solution)/shard_map/convert_element_type | solution.py:450
  99.1 2.1 %student_stats.1 = (f32[8,128]{1,0:T(8,128)S(1)}, f32[8,128]{1,0:T(8,128)S(1)}, f32[8,128]{1,0:T(8,128)S(1)}, f32[8,128]{1,0:T(8,128)S(1)}) custom-call(s32[2]{0:T(128)S(1)} %pad_add_fusion.spot_ref, s32[4,128,1]{2,1,0:T(8,128)S(1)} %copy.11.labels_ref, f32[8,128]{1,0:T(8,128)S(1)} %add.79.after_ref.mass_ref, f32[4,128,1024]{2,1,0:T(8,128)S(1)} %copy-done.3), custom_call_target="tpu_custom_call" | custom-call | flops 1024 | bytes 1024 | tf_op jit(solution)/shard_map/student_stats/pallas_call | solution.py:277
  101.2 2.3 %collective-permute-start.12 = (f32[8,128]{1,0:T(8,128)S(1)}, f32[8,128]{1,0:T(8,128)S(1)}, u32[]{:S(2)}, u32[]{:S(2)}) collective-permute-start(f32[8,128]{1,0:T(8,128)S(1)} %get-tuple-element.51), channel_id=1, source_target_pairs={{0,8},{8,0},{16,24},{24,16},{1,9},{9,1},{17,25},{25,17},{2,10},{10... | collective-permute-start | bytes 12296 | tf_op jit(solution)/shard_map/ppermute | solution.py:426
  105.0 2.8 %collective-permute-done.12.refs_1_ = f32[8,128]{1,0:T(8,128)S(1)} collective-permute-done((f32[8,128]{1,0:T(8,128)S(1)}, f32[8,128]{1,0:T(8,128)S(1)}, u32[]{:S(2)}, u32[]{:S(2)}) %collective-permute-start.12) | collective-permute-done | bytes 4128 | tf_op jit(solution)/shard_map/ppermute | solution.py:426
  109.3 3.1 %collective-permute-done.14.refs_3_ = f32[8,128]{1,0:T(8,128)S(1)} collective-permute-done((f32[8,128]{1,0:T(8,128)S(1)}, f32[8,128]{1,0:T(8,128)S(1)}, u32[]{:S(2)}, u32[]{:S(2)}) %collective-permute-start.14) | collective-permute-done | bytes 4128 | tf_op jit(solution)/shard_map/ppermute | solution.py:426
  113.6 3.8 %collective-permute-start.18 = (f32[8,128]{1,0:T(8,128)S(1)}, f32[8,128]{1,0:T(8,128)S(1)}, u32[]{:S(2)}, u32[]{:S(2)}) collective-permute-start(f32[8,128]{1,0:T(8,128)S(1)} %merge_stats.3.refs_0_), channel_id=1, source_target_pairs={{0,2},{1,3},{2,0},{3,1},{4,6},{5,7},{6,4},{7,5},{8,10},{9,11},{10,... | collective-permute-start | bytes 12296 | tf_op jit(solution)/shard_map/ppermute | solution.py:426
  117.4 4.1 %collective-permute-done.18.refs_1_ = f32[8,128]{1,0:T(8,128)S(1)} collective-permute-done((f32[8,128]{1,0:T(8,128)S(1)}, f32[8,128]{1,0:T(8,128)S(1)}, u32[]{:S(2)}, u32[]{:S(2)}) %collective-permute-start.18) | collective-permute-done | bytes 4128 | tf_op jit(solution)/shard_map/ppermute | solution.py:426
  121.5 3.1 %collective-permute-start.20 = (f32[8,128]{1,0:T(8,128)S(1)}, f32[8,128]{1,0:T(8,128)S(1)}, u32[]{:S(2)}, u32[]{:S(2)}) collective-permute-start(f32[8,128]{1,0:T(8,128)S(1)} %merge_stats.3.refs_0_), channel_id=1, source_target_pairs={{0,6},{1,7},{2,4},{3,5},{4,2},{5,3},{6,0},{7,1},{8,14},{9,15},{10,... | collective-permute-start | bytes 12296 | tf_op jit(solution)/shard_map/ppermute | solution.py:426
  128.3 4.6 %grad_logits.1 = (bf16[128,1024]{1,0:T(8,128)(2,1)}, bf16[128,1024]{1,0:T(8,128)(2,1)}, bf16[128,1024]{1,0:T(8,128)(2,1)}, bf16[128,1024]{1,0:T(8,128)(2,1)}, f32[1,128]{1,0:T(1,128)S(1)}) custom-call(s32[1]{0:T(128)} %bitcast.tok_ref, s32[4]{0:T(128)S(1)} %add_multiply_fusion.base_ref, s32[128,1]{1,0:T(8,128)S(1)} %copy.12.labels_ref, ...), custom_call_target="tpu_custom_call" | custom-call | flops 1024 | bytes 1024 | tf_op jit(solution)/shard_map/grad_logits/pallas_call | solution.py:376
  132.9 2.8 %collective-permute-start.27 = (bf16[128,1024]{1,0:T(8,128)(2,1)}, bf16[128,1024]{1,0:T(8,128)(2,1)S(1)}, u32[]{:S(2)}, u32[]{:S(2)}) collective-permute-start(bf16[128,1024]{1,0:T(8,128)(2,1)} %get-tuple-element.66), channel_id=1, source_target_pairs={{0,24},{8,16},{16,8},{24,0},{1,25},{9,17},{17,9},{25,1},{2,26},{10... | collective-permute-start | bytes 786440 | tf_op jit(solution)/shard_map/ppermute | solution.py:426
  137.5 3.5 %collective-permute-done.25 = f32[1,128]{1,0:T(1,128)S(1)} collective-permute-done((f32[1,128]{1,0:T(1,128)S(1)}, f32[1,128]{1,0:T(1,128)S(1)}, u32[]{:S(2)}, u32[]{:S(2)}) %collective-permute-start.25) | collective-permute-done | bytes 544 | tf_op jit(solution)/shard_map/ppermute | solution.py:426
  141.1 1.7 %collective-permute-start.26 = (f32[1,128]{1,0:T(1,128)S(1)}, f32[1,128]{1,0:T(1,128)S(1)}, u32[]{:S(2)}, u32[]{:S(2)}) collective-permute-start(f32[1,128]{1,0:T(1,128)S(1)} %add.87), channel_id=1, source_target_pairs={{0,4},{1,5},{2,6},{3,7},{4,0},{5,1},{6,2},{7,3},{8,12},{9,13},{10,... | collective-permute-start | bytes 1544 | tf_op jit(solution)/shard_map/ppermute | solution.py:426
  142.7 2.8 %collective-permute-done.26 = f32[1,128]{1,0:T(1,128)S(1)} collective-permute-done((f32[1,128]{1,0:T(1,128)S(1)}, f32[1,128]{1,0:T(1,128)S(1)}, u32[]{:S(2)}, u32[]{:S(2)}) %collective-permute-start.26) | collective-permute-done | bytes 544 | tf_op jit(solution)/shard_map/ppermute | solution.py:426
  147.0 9.2 %head_product.1 = bf16[4608,1024]{1,0:T(8,128)(2,1)} custom-call(s32[1]{0:T(128)} %bitcast.tok_ref, bf16[4608,512]{1,0:T(8,128)(2,1)} %get-tuple-element.65.a_ref, bf16[128,1024]{1,0:T(8,128)(2,1)S(1)} %collective-permute-done.27.refs_0_, bf16[128,1024]{1,0:T(8,128)(2,1)S(1)} %collective-permute-done.28.refs_1_, ...), custom_call_target="tpu_custom_call" | custom-call | flops 1024 | bytes 1024 | tf_op jit(solution)/shard_map/head_product/pallas_call | solution.py:411
  (88 shorter events, 29.8 us)
Async XLA Ops:
  0.6 23.1 %collective-permute-start.9 = (bf16[32,4,128,128]{3,2,1,0:T(8,128)(2,1)}, bf16[32,4,128,128]{3,2,1,0:T(8,128)(2,1)}, u32[]{:S(2)}, u32[]{:S(2)}) collective-permute-start(bf16[32,4,128,128]{3,2,1,0:T(8,128)(2,1)} %w_own.3), channel_id=1, source_target_pairs={{0,1},{1,0},{2,3},{3,2},{4,5},{5,4},{6,7},{7,6},{8,9},{9,8},{10,11... | collective-permute-start | bytes 12582920 | tf_op jit(solution)/shard_map/ppermute | solution.py:426
  1.2 17.6 %collective-permute-start.1 = (bf16[128,4096]{1,0:T(8,128)(2,1)}, bf16[128,4096]{1,0:T(8,128)(2,1)S(1)}, u32[]{:S(2)}, u32[]{:S(2)}) collective-permute-start(bf16[128,4096]{1,0:T(8,128)(2,1)} %x_own.1), channel_id=1, source_target_pairs={{0,1},{1,0},{2,3},{3,2},{4,5},{5,4},{6,7},{7,6},{8,9},{9,8},{10,11... | collective-permute-start | bytes 3145736 | tf_op jit(solution)/shard_map/ppermute | solution.py:426
  3.1 10.5 %collective-permute-start.2 = (f32[8,128]{1,0:T(8,128)S(1)}, f32[8,128]{1,0:T(8,128)S(1)}, u32[]{:S(2)}, u32[]{:S(2)}) collective-permute-start(f32[8,128]{1,0:T(8,128)S(1)} %teacher_stats.1.refs_0_), channel_id=1, source_target_pairs={{0,2},{1,3},{2,0},{3,1},{4,6},{5,7},{6,4},{7,5},{8,10},{9,11},{10,... | collective-permute-start | bytes 12296 | tf_op jit(solution)/shard_map/ppermute | solution.py:426
  7.0 2.7 %collective-permute-start = (s32[128]{0:T(128)S(1)}, s32[128]{0:T(128)S(1)}, u32[]{:S(2)}, u32[]{:S(2)}) collective-permute-start(s32[128]{0:T(128)S(1)} %reshape.18.own_ref), channel_id=1, source_target_pairs={{0,1},{1,0},{2,3},{3,2},{4,5},{5,4},{6,7},{7,6},{8,9},{9,8},{10,11... | collective-permute-start | bytes 1544 | tf_op jit(solution)/shard_map/ppermute | solution.py:426
  7.1 6.5 %collective-permute-start.3 = (f32[8,128]{1,0:T(8,128)S(1)}, f32[8,128]{1,0:T(8,128)S(1)}, u32[]{:S(2)}, u32[]{:S(2)}) collective-permute-start(f32[8,128]{1,0:T(8,128)S(1)} %teacher_stats.1.refs_0_), channel_id=1, source_target_pairs={{0,4},{1,5},{2,6},{3,7},{4,0},{5,1},{6,2},{7,3},{8,12},{9,13},{10,... | collective-permute-start | bytes 12296 | tf_op jit(solution)/shard_map/ppermute | solution.py:426
  9.7 5.4 %collective-permute-start.4 = (f32[8,128]{1,0:T(8,128)S(1)}, f32[8,128]{1,0:T(8,128)S(1)}, u32[]{:S(2)}, u32[]{:S(2)}) collective-permute-start(f32[8,128]{1,0:T(8,128)S(1)} %teacher_stats.1.refs_0_), channel_id=1, source_target_pairs={{0,6},{1,7},{2,4},{3,5},{4,2},{5,3},{6,0},{7,1},{8,14},{9,15},{10,... | collective-permute-start | bytes 12296 | tf_op jit(solution)/shard_map/ppermute | solution.py:426
  13.5 1.6 %collective-permute-start.5 = (f32[8,128]{1,0:T(8,128)S(1)}, f32[8,128]{1,0:T(8,128)S(1)}, u32[]{:S(2)}, u32[]{:S(2)}) collective-permute-start(f32[8,128]{1,0:T(8,128)S(1)} %teacher_stats.1.refs_0_), channel_id=1, source_target_pairs={{0,1},{1,0},{2,3},{3,2},{4,5},{5,4},{6,7},{7,6},{8,9},{9,8},{10,11... | collective-permute-start | bytes 12296 | tf_op jit(solution)/shard_map/ppermute | solution.py:426
  13.6 5.2 %collective-permute-start.6 = (f32[8,128]{1,0:T(8,128)S(1)}, f32[8,128]{1,0:T(8,128)S(1)}, u32[]{:S(2)}, u32[]{:S(2)}) collective-permute-start(f32[8,128]{1,0:T(8,128)S(1)} %collective-permute-done.2.refs_1_), channel_id=1, source_target_pairs={{0,1},{1,0},{2,3},{3,2},{4,5},{5,4},{6,7},{7,6},{8,9},{9,8},{10,11... | collective-permute-start | bytes 12296 | tf_op jit(solution)/shard_map/ppermute | solution.py:426
  15.2 3.6 %collective-permute-start.7 = (f32[8,128]{1,0:T(8,128)S(1)}, f32[8,128]{1,0:T(8,128)S(1)}, u32[]{:S(2)}, u32[]{:S(2)}) collective-permute-start(f32[8,128]{1,0:T(8,128)S(1)} %collective-permute-done.3.refs_2_), channel_id=1, source_target_pairs={{0,1},{1,0},{2,3},{3,2},{4,5},{5,4},{6,7},{7,6},{8,9},{9,8},{10,11... | collective-permute-start | bytes 12296 | tf_op jit(solution)/shard_map/ppermute | solution.py:426
  15.2 3.6 %collective-permute-start.8 = (f32[8,128]{1,0:T(8,128)S(1)}, f32[8,128]{1,0:T(8,128)S(1)}, u32[]{:S(2)}, u32[]{:S(2)}) collective-permute-start(f32[8,128]{1,0:T(8,128)S(1)} %collective-permute-done.4.refs_3_), channel_id=1, source_target_pairs={{0,1},{1,0},{2,3},{3,2},{4,5},{5,4},{6,7},{7,6},{8,9},{9,8},{10,11... | collective-permute-start | bytes 12296 | tf_op jit(solution)/shard_map/ppermute | solution.py:426
  30.4 33.2 %all-to-all-start = ((bf16[4,64,4608]{2,1,0:T(8,128)(2,1)}), bf16[4,64,4608]{2,1,0:T(8,128)(2,1)}, u32[]{:S(2)}, u32[]{:S(2)}) async-start(bf16[4,64,4608]{2,1,0:T(8,128)(2,1)} %broadcast_in_dim.21), calls=%async_computation | async-start | bytes 4718592 | tf_op jit(solution)/shard_map/all_to_all | solution.py:454
  35.1 24.2 %collective-permute-start.10 = (bf16[32,128,128]{2,1,0:T(8,128)(2,1)}, bf16[32,128,128]{2,1,0:T(8,128)(2,1)S(1)}, u32[]{:S(2)}, u32[]{:S(2)}) collective-permute-start(bf16[32,128,128]{2,1,0:T(8,128)(2,1)} %get-tuple-element.38), channel_id=1, source_target_pairs={{0,2},{1,3},{6,4},{7,5},{8,10},{9,11},{14,12},{15,13},{16,18},{17,... | collective-permute-start | bytes 3145736 | tf_op jit(solution)/shard_map/ppermute | solution.py:458
  63.6 4.7 %collective-permute-start.11 = (bf16[256,4608]{1,0:T(8,128)(2,1)}, bf16[256,4608]{1,0:T(8,128)(2,1)S(1)}, u32[]{:S(2)}, u32[]{:S(2)}) collective-permute-start(bf16[256,4608]{1,0:T(8,128)(2,1)} %bitcast.5.near_ref), channel_id=1, source_target_pairs={{0,1},{1,0},{2,3},{3,2},{4,5},{5,4},{6,7},{7,6},{8,9},{9,8},{10,11... | collective-permute-start | bytes 7077896 | tf_op jit(solution)/shard_map/ppermute | solution.py:426
  63.6 25.1 %collective-permute-start.17 = (bf16[32,128,128]{2,1,0:T(8,128)(2,1)}, bf16[32,128,128]{2,1,0:T(8,128)(2,1)}, u32[]{:S(2)}, u32[]{:S(2)}) collective-permute-start(bf16[32,128,128]{2,1,0:T(8,128)(2,1)} %get-tuple-element.54), channel_id=1, source_target_pairs={{0,2},{1,3},{6,4},{7,5},{8,10},{9,11},{14,12},{15,13},{16,18},{17,... | collective-permute-start | bytes 3145736 | tf_op jit(solution)/shard_map/ppermute | solution.py:458
  65.9 25.9 %collective-permute-start.16 = (bf16[32,128,128]{2,1,0:T(8,128)(2,1)}, bf16[32,128,128]{2,1,0:T(8,128)(2,1)}, u32[]{:S(2)}, u32[]{:S(2)}) collective-permute-start(bf16[32,128,128]{2,1,0:T(8,128)(2,1)} %add_convert_fusion.2), channel_id=1, source_target_pairs={{2,4},{3,5},{4,2},{5,3},{10,12},{11,13},{12,10},{13,11},{18,20},{1... | collective-permute-start | bytes 3145736 | tf_op jit(solution)/shard_map/ppermute | solution.py:458
  78.7 34.9 %all-to-all-start.1 = ((f32[4,128,1024]{2,1,0:T(8,128)}), f32[4,128,1024]{2,1,0:T(8,128)S(1)}, u32[]{:S(2)}, u32[]{:S(2)}) async-start(f32[4,128,1024]{2,1,0:T(8,128)} %get-tuple-element.49.logits_ref), calls=%async_computation.1 | async-start | bytes 4194304 | tf_op jit(solution)/shard_map/all_to_all | solution.py:454
  82.5 44.6 %collective-permute-start.21 = (bf16[32,128,128]{2,1,0:T(8,128)(2,1)}, bf16[32,128,128]{2,1,0:T(8,128)(2,1)}, u32[]{:S(2)}, u32[]{:S(2)}) collective-permute-start(bf16[32,128,128]{2,1,0:T(8,128)(2,1)} %get-tuple-element.62), channel_id=1, source_target_pairs={{0,2},{1,3},{6,4},{7,5},{8,10},{9,11},{14,12},{15,13},{16,18},{17,... | collective-permute-start | bytes 3145736 | tf_op jit(solution)/shard_map/ppermute | solution.py:458
  94.4 32.7 %collective-permute-start.23 = (bf16[32,128,128]{2,1,0:T(8,128)(2,1)}, bf16[32,128,128]{2,1,0:T(8,128)(2,1)}, u32[]{:S(2)}, u32[]{:S(2)}) collective-permute-start(bf16[32,128,128]{2,1,0:T(8,128)(2,1)} %add_convert_fusion), channel_id=1, source_target_pairs={{2,0},{3,1},{4,6},{5,7},{10,8},{11,9},{12,14},{13,15},{18,16},{19,... | collective-permute-start | bytes 3145736 | tf_op jit(solution)/shard_map/ppermute | solution.py:458
  95.7 31.4 %collective-permute-start.22 = (bf16[32,128,128]{2,1,0:T(8,128)(2,1)}, bf16[32,128,128]{2,1,0:T(8,128)(2,1)}, u32[]{:S(2)}, u32[]{:S(2)}) collective-permute-start(bf16[32,128,128]{2,1,0:T(8,128)(2,1)} %add_convert_fusion.1), channel_id=1, source_target_pairs={{2,4},{3,5},{4,2},{5,3},{10,12},{11,13},{12,10},{13,11},{18,20},{1... | collective-permute-start | bytes 3145736 | tf_op jit(solution)/shard_map/ppermute | solution.py:458
  101.2 6.6 %collective-permute-start.12 = (f32[8,128]{1,0:T(8,128)S(1)}, f32[8,128]{1,0:T(8,128)S(1)}, u32[]{:S(2)}, u32[]{:S(2)}) collective-permute-start(f32[8,128]{1,0:T(8,128)S(1)} %get-tuple-element.51), channel_id=1, source_target_pairs={{0,8},{8,0},{16,24},{24,16},{1,9},{9,1},{17,25},{25,17},{2,10},{10... | collective-permute-start | bytes 12296 | tf_op jit(solution)/shard_map/ppermute | solution.py:426
  103.5 5.8 %collective-permute-start.13 = (f32[8,128]{1,0:T(8,128)S(1)}, f32[8,128]{1,0:T(8,128)S(1)}, u32[]{:S(2)}, u32[]{:S(2)}) collective-permute-start(f32[8,128]{1,0:T(8,128)S(1)} %get-tuple-element.52), channel_id=1, source_target_pairs={{0,16},{8,24},{16,0},{24,8},{1,17},{9,25},{17,1},{25,9},{2,18},{10... | collective-permute-start | bytes 12296 | tf_op jit(solution)/shard_map/ppermute | solution.py:426
  107.9 4.5 %collective-permute-start.14 = (f32[8,128]{1,0:T(8,128)S(1)}, f32[8,128]{1,0:T(8,128)S(1)}, u32[]{:S(2)}, u32[]{:S(2)}) collective-permute-start(f32[8,128]{1,0:T(8,128)S(1)} %get-tuple-element.53), channel_id=1, source_target_pairs={{0,24},{8,16},{16,8},{24,0},{1,25},{9,17},{17,9},{25,1},{2,26},{10... | collective-permute-start | bytes 12296 | tf_op jit(solution)/shard_map/ppermute | solution.py:426
  112.4 1.2 collective-permute-start.15
  113.6 7.9 %collective-permute-start.18 = (f32[8,128]{1,0:T(8,128)S(1)}, f32[8,128]{1,0:T(8,128)S(1)}, u32[]{:S(2)}, u32[]{:S(2)}) collective-permute-start(f32[8,128]{1,0:T(8,128)S(1)} %merge_stats.3.refs_0_), channel_id=1, source_target_pairs={{0,2},{1,3},{2,0},{3,1},{4,6},{5,7},{6,4},{7,5},{8,10},{9,11},{10,... | collective-permute-start | bytes 12296 | tf_op jit(solution)/shard_map/ppermute | solution.py:426
  117.4 8.8 %collective-permute-start.19 = (f32[8,128]{1,0:T(8,128)S(1)}, f32[8,128]{1,0:T(8,128)S(1)}, u32[]{:S(2)}, u32[]{:S(2)}) collective-permute-start(f32[8,128]{1,0:T(8,128)S(1)} %merge_stats.3.refs_0_), channel_id=1, source_target_pairs={{0,4},{1,5},{2,6},{3,7},{4,0},{5,1},{6,2},{7,3},{8,12},{9,13},{10,... | collective-permute-start | bytes 12296 | tf_op jit(solution)/shard_map/ppermute | solution.py:426
  121.5 5.4 %collective-permute-start.20 = (f32[8,128]{1,0:T(8,128)S(1)}, f32[8,128]{1,0:T(8,128)S(1)}, u32[]{:S(2)}, u32[]{:S(2)}) collective-permute-start(f32[8,128]{1,0:T(8,128)S(1)} %merge_stats.3.refs_0_), channel_id=1, source_target_pairs={{0,6},{1,7},{2,4},{3,5},{4,2},{5,3},{6,0},{7,1},{8,14},{9,15},{10,... | collective-permute-start | bytes 12296 | tf_op jit(solution)/shard_map/ppermute | solution.py:426
  132.9 13.1 %collective-permute-start.27 = (bf16[128,1024]{1,0:T(8,128)(2,1)}, bf16[128,1024]{1,0:T(8,128)(2,1)S(1)}, u32[]{:S(2)}, u32[]{:S(2)}) collective-permute-start(bf16[128,1024]{1,0:T(8,128)(2,1)} %get-tuple-element.66), channel_id=1, source_target_pairs={{0,24},{8,16},{16,8},{24,0},{1,25},{9,17},{17,9},{25,1},{2,26},{10... | collective-permute-start | bytes 786440 | tf_op jit(solution)/shard_map/ppermute | solution.py:426
  135.7 10.3 %collective-permute-start.28 = (bf16[128,1024]{1,0:T(8,128)(2,1)}, bf16[128,1024]{1,0:T(8,128)(2,1)S(1)}, u32[]{:S(2)}, u32[]{:S(2)}) collective-permute-start(bf16[128,1024]{1,0:T(8,128)(2,1)} %get-tuple-element.67), channel_id=1, source_target_pairs={{0,16},{8,24},{16,0},{24,8},{1,17},{9,25},{17,1},{25,9},{2,18},{10... | collective-permute-start | bytes 786440 | tf_op jit(solution)/shard_map/ppermute | solution.py:426
  136.2 9.8 %collective-permute-start.29 = (bf16[128,1024]{1,0:T(8,128)(2,1)}, bf16[128,1024]{1,0:T(8,128)(2,1)S(1)}, u32[]{:S(2)}, u32[]{:S(2)}) collective-permute-start(bf16[128,1024]{1,0:T(8,128)(2,1)} %get-tuple-element.68), channel_id=1, source_target_pairs={{0,8},{8,0},{16,24},{24,16},{1,9},{9,1},{17,25},{25,17},{2,10},{10... | collective-permute-start | bytes 786440 | tf_op jit(solution)/shard_map/ppermute | solution.py:426
  136.4 1.1 collective-permute-start.24
  137.5 3.5 %collective-permute-start.25 = (f32[1,128]{1,0:T(1,128)S(1)}, f32[1,128]{1,0:T(1,128)S(1)}, u32[]{:S(2)}, u32[]{:S(2)}) collective-permute-start(f32[1,128]{1,0:T(1,128)S(1)} %add.86), channel_id=1, source_target_pairs={{0,2},{1,3},{2,0},{3,1},{4,6},{5,7},{6,4},{7,5},{8,10},{9,11},{10,... | collective-permute-start | bytes 1544 | tf_op jit(solution)/shard_map/ppermute | solution.py:426
  141.1 4.4 %collective-permute-start.26 = (f32[1,128]{1,0:T(1,128)S(1)}, f32[1,128]{1,0:T(1,128)S(1)}, u32[]{:S(2)}, u32[]{:S(2)}) collective-permute-start(f32[1,128]{1,0:T(1,128)S(1)} %add.87), channel_id=1, source_target_pairs={{0,4},{1,5},{2,6},{3,7},{4,0},{5,1},{6,2},{7,3},{8,12},{9,13},{10,... | collective-permute-start | bytes 1544 | tf_op jit(solution)/shard_map/ppermute | solution.py:426
  (13 other events, 79.9 us)
